TPU v7x, 256 devices: a whole 4x4x8 slice. The times are simulated.
256 devices in a mesh: seq: 32 (over x_lo, z, core), head: 8 (over y, x_hi).
Axes of the slice: x: 4 (x_hi: 2, x_lo: 2; x = x_hi * 2 + x_lo), y: 4, z: 8, core: 2. Of those that a mesh axis runs over, the one named last changes fastest.
Arguments:
- tokens: bfloat16 [8192, 2048], P('seq', 'head'), may hold values from -12 to 12
- weight_in: bfloat16 [2048, 4096], P(None, 'head'), may hold values from -0.125 to 0.125
- weight_out: bfloat16 [2048, 4096], P(None, 'head'), may hold values from -0.09375 to 0.09375
- state_keys: bfloat16 [2, 8192, 128], P(None, 'seq'), may hold values from -6 to 6
- state_queries: bfloat16 [2, 8192, 128], P(None, 'seq'), may hold values from -0.01171875 to 0.01171875
- log_decay: bfloat16 [2, 8192, 32], P(None, 'seq', 'head'), may hold values from -0.6 to 0
- skip_gain: float32 [32], P('head'), may hold values from 0.5 to 1.5
- cotangent: bfloat16 [8192, 2048], P('seq', 'head'), may hold values from -1.5 to 1.5
Outputs:
- mixed: bfloat16 [8192, 2048], P('seq', 'head')
- gradient_tokens: bfloat16 [8192, 2048], P('seq', 'head')
- gradient_in: float32 [2048, 4096], P('seq', 'head')
- gradient_out: float32 [2048, 4096], P('seq', 'head')
All inputs are finite; a program needn't handle non-finite values.
Results may differ from a plain program's by a relative error of at most 0.03.
Values may be sent and summed in bfloat16 or wider, within the bound.
No kernel may reach another device: no remote copies, remote signals or barrier semaphores. Data moves between devices by JAX's collectives and lax.ppermute only.
A program may use at most 128 MiB of HBM per device.

v0:
```python
import jax
import jax.numpy as jnp
from jax import lax
from jax.sharding import PartitionSpec as P

BLOCK = 256


def prefix_2(x, axis, combine, identity, reverse):
    count, place = (lax.axis_size(axis), lax.axis_index(axis))
    everything = jax.tree.map(lambda part: lax.all_gather(part, axis), x)
    start = jax.tree.map(
        lambda part, zero: jnp.broadcast_to(jnp.asarray(zero, part.dtype), part.shape), x, identity
    )

    def turn(k, before):
        at = count - 1 - k if reverse else k
        reached = at > place if reverse else at < place
        new = combine(before, jax.tree.map(lambda part: part[at], everything))
        return jax.tree.map(lambda a, b: jnp.where(reached, a, b), new, before)

    return lax.fori_loop(0, count, turn, start)


def swapped(block, axis, bit):
    count = lax.axis_size(axis)
    route = []
    for low in range(count):
        high = low | 1 << bit
        if high != low and high < count:
            route += [(low, high), (high, low)]
    return lax.ppermute(block, axis, route)


def combine_states(earlier, latter):
    return (earlier[0] + latter[0], jnp.exp(latter[0])[..., None, None] * earlier[1] + latter[1])


def prepare(values, state_keys, state_queries, log_decay, exclusive, flipped):
    if flipped:
        values = jnp.flip(values, 0)
        state_keys = jnp.flip(state_keys, 0)
        state_queries = jnp.flip(state_queries, 0)
        log_decay = jnp.flip(log_decay, 0)
    row_count, channels = values.shape
    head_count = log_decay.shape[1]
    head_size = channels // head_count
    block_count = row_count // BLOCK
    state_dim = state_keys.shape[1]
    step_logs = log_decay.astype(jnp.float32).reshape(block_count, BLOCK, head_count)
    inclusive = jnp.cumsum(step_logs, axis=1)
    position = inclusive - step_logs if exclusive else inclusive
    totals = inclusive[:, -1, :]
    blocked = values.reshape(block_count, BLOCK, head_count, head_size)
    key_rows = state_keys.reshape(block_count, BLOCK, state_dim)
    query_rows = state_queries.reshape(block_count, BLOCK, state_dim)
    scores = jnp.einsum("cin,cjn->cij", query_rows, key_rows, preferred_element_type=jnp.float32)
    causal = lax.broadcasted_iota(jnp.int32, (BLOCK, BLOCK), 0) >= lax.broadcasted_iota(
        jnp.int32, (BLOCK, BLOCK), 1
    )
    heads_first = jnp.transpose(position, (0, 2, 1))
    log_gaps = heads_first[:, :, :, None] - heads_first[:, :, None, :]
    decays = jnp.where(causal, jnp.exp(jnp.where(causal, log_gaps, 0.0)), 0.0)
    weights = (scores[:, None] * decays).astype(jnp.bfloat16)
    inside = jnp.einsum("chij,cjhp->cihp", weights, blocked, preferred_element_type=jnp.float32)
    remaining = jnp.transpose(jnp.exp(totals[:, None, :] - position), (0, 2, 1))
    key_weights = (remaining[:, :, :, None] * key_rows[:, None, :, :].astype(jnp.float32)).astype(
        jnp.bfloat16
    )
    block_states = jnp.einsum(
        "chjn,cjhp->chnp", key_weights, blocked, preferred_element_type=jnp.float32
    )
    summary = (
        jnp.zeros((head_count,), jnp.float32),
        jnp.zeros((head_count, state_dim, head_size), jnp.float32),
    )
    summary = combine_states(summary, (totals[0], block_states[0]))
    return ((inside, position, totals, query_rows, block_states), summary)


def complete(pieces_in, carried, flipped, row_count, channels):
    inside, position, totals, query_rows, block_states = pieces_in
    from_before = jnp.einsum(
        "in,hnp->ihp", query_rows[0].astype(jnp.float32), carried, precision=lax.Precision.HIGHEST
    )
    pieces = [inside[0] + jnp.exp(position[0])[:, :, None] * from_before]
    concluding_answer = jnp.stack(pieces).reshape(row_count, channels)
    if flipped:
        concluding_answer = jnp.flip(concluding_answer, 0)
    return concluding_answer


def carry_alone(summary, flipped):
    identity = (jnp.zeros_like(summary[0]), jnp.zeros_like(summary[1]))
    prefix = prefix_2(summary, "seq", combine_states, identity, flipped)
    return prefix[1]


def finish(scanned, values, skip_gain):
    row_count, channels = values.shape
    head_count = skip_gain.shape[0]
    shaped = scanned.reshape(row_count, head_count, channels // head_count)
    direct = skip_gain[None, :, None] * values.reshape(shaped.shape).astype(jnp.float32)
    return (shaped + direct).reshape(row_count, channels).astype(jnp.bfloat16)


def mirror_inputs(value_rows, key_rows, query_rows, decay_rows):
    for level in range(lax.axis_size("seq").bit_length() - 1):
        value_rows, key_rows, query_rows, decay_rows = swapped(
            (value_rows, key_rows, query_rows, decay_rows), "seq", level
        )
    return (
        jnp.flip(value_rows, 0),
        jnp.flip(key_rows, 0),
        jnp.flip(query_rows, 0),
        jnp.flip(decay_rows, 0),
    )


def mirror_back(value_rows):
    for level in range(lax.axis_size("seq").bit_length() - 1):
        value_rows = swapped(value_rows, "seq", level)
    return jnp.flip(value_rows, 0)


def contract_rows(left_side, right_side):
    return lax.dot_general(
        left_side, right_side, (((0,), (0,)), ((), ())), preferred_element_type=jnp.float32
    )


def contract_cols(left_side, right_side):
    return lax.dot_general(
        left_side, right_side, (((1,), (1,)), ((), ())), preferred_element_type=jnp.float32
    )


def shards(
    tokens, weight_in, weight_out, state_keys, state_queries, log_decay, skip_gain, cotangent
):
    gathered = lax.all_gather(tokens, "head", axis=1, tiled=True)
    weight_in_flip = jnp.flip(weight_in, 0)
    weight_out_flip = jnp.flip(weight_out, 0)
    forward_input = jnp.dot(gathered, weight_in, preferred_element_type=jnp.float32).astype(
        jnp.bfloat16
    )
    reverse_input = jnp.dot(gathered, weight_in_flip, preferred_element_type=jnp.float32).astype(
        jnp.bfloat16
    )
    full_cotangent = lax.all_gather(cotangent, "head", axis=1, tiled=True)
    forward_delta = jnp.dot(full_cotangent, weight_out, preferred_element_type=jnp.float32).astype(
        jnp.bfloat16
    )
    reverse_delta = jnp.dot(
        full_cotangent, weight_out_flip, preferred_element_type=jnp.float32
    ).astype(jnp.bfloat16)
    mirror_vals, mirror_keys, mirror_queries, mirror_decay = mirror_inputs(
        reverse_input, state_keys[1], state_queries[1], log_decay[1]
    )
    mirror_delta = mirror_back(reverse_delta)
    tasks = [
        (forward_input, state_keys[0], state_queries[0], log_decay[0], False, False),
        (mirror_vals, mirror_keys, mirror_queries, mirror_decay, False, False),
        (forward_delta, state_queries[0], state_keys[0], log_decay[0], True, True),
        (mirror_delta, mirror_queries, mirror_keys, mirror_decay, True, True),
    ]
    prepared = [prepare(*task) for task in tasks]
    summaries = [entry[1] for entry in prepared]
    directions = [task[5] for task in tasks]
    carries = [carry_alone(summaries[index], directions[index]) for index in range(4)]
    results = []
    for index in range(4):
        values = tasks[index][0]
        scanned = complete(
            prepared[index][0], carries[index], directions[index], values.shape[0], values.shape[1]
        )
        results.append(finish(scanned, values, skip_gain))
    forward_output, second_output, forward_back, fourth_output = results
    reverse_output = mirror_back(second_output)
    reverse_back = mirror_back(fourth_output)
    partial_out = contract_cols(forward_output, weight_out) + contract_cols(
        reverse_output, weight_out_flip
    )
    mixed = lax.psum_scatter(
        partial_out.astype(jnp.bfloat16), "head", scatter_dimension=1, tiled=True
    )
    partial_tokens = contract_cols(forward_back, weight_in) + contract_cols(
        reverse_back, weight_in_flip
    )
    gradient_tokens = lax.psum_scatter(
        partial_tokens.astype(jnp.bfloat16), "head", scatter_dimension=1, tiled=True
    )
    tokens_flip = jnp.flip(gathered, 1)
    cotangent_flip = jnp.flip(full_cotangent, 1)
    direct = contract_rows(gathered, forward_back)
    gradient_in = lax.psum_scatter(
        (direct + contract_rows(tokens_flip, reverse_back)).astype(jnp.bfloat16),
        "seq",
        scatter_dimension=0,
        tiled=True,
    ).astype(jnp.float32)
    direct = contract_rows(full_cotangent, forward_output)
    gradient_out = lax.psum_scatter(
        (direct + contract_rows(cotangent_flip, reverse_output)).astype(jnp.bfloat16),
        "seq",
        scatter_dimension=0,
        tiled=True,
    ).astype(jnp.float32)
    return (mixed, gradient_tokens, gradient_in, gradient_out)


def solution(mesh):
    return jax.shard_map(
        shards,
        mesh=mesh,
        in_specs=(
            P("seq", "head"),
            P(None, "head"),
            P(None, "head"),
            P(None, "seq", None),
            P(None, "seq", None),
            P(None, "seq", "head"),
            P("head"),
            P("seq", "head"),
        ),
        out_specs=(P("seq", "head"), P("seq", "head"), P("seq", "head"), P("seq", "head")),
        check_vma=False,
    )
```

profile of v0, /device:TPU:8, one launch (start us, length us, event | category | flops | bytes accessed | tf_op | source)
XLA Modules:
  0.0 1106.5 jit_solution(5700603591561339416)
XLA Ops:
  14.1 48.4 %all-gather.17.cloned.1.call-done = bf16[256,2048]{1,0:T(8,128)(2,1)} async-done(((bf16[256,256]{1,0:T(8,128)(2,1)}), bf16[256,2048]{1,0:T(8,128)(2,1)}) %all-gather.17.cloned.1.call-update) | async-done | bytes 1048592 | tf_op jit(solution)/shard_map/all_gather | solution.py:150
  65.8 20.4 %rev.67 = bf16[2048,512]{1,0:T(8,128)(2,1)} reverse(bf16[2048,512]{1,0:T(8,128)(2,1)S(1)} %copy-done.1), dimensions={0} | reverse | bytes 4194304 | tf_op jit(solution)/shard_map/jit(_flip)/rev | solution.py:143
  139.2 13.3 %collective-permute-done.7 = bf16[256,128]{1,0:T(8,128)(2,1)S(1)} collective-permute-done((bf16[256,128]{1,0:T(8,128)(2,1)}, bf16[256,128]{1,0:T(8,128)(2,1)S(1)}, u32[]{:S(2)}, u32[]{:S(2)}) %collective-permute-start.7) | collective-permute-done | bytes 65568 | tf_op jit(solution)/shard_map/ppermute | solution.py:32
  171.8 20.4 %rev.61 = bf16[2048,512]{1,0:T(8,128)(2,1)} reverse(bf16[2048,512]{1,0:T(8,128)(2,1)S(1)} %copy-done), dimensions={0} | reverse | bytes 4194304 | tf_op jit(solution)/shard_map/jit(_flip)/rev | solution.py:142
  197.0 8.0 collective-permute-done.1
  208.7 11.7 %collective-permute-done.2 = bf16[256,512]{1,0:T(8,128)(2,1)S(1)} collective-permute-done((bf16[256,512]{1,0:T(8,128)(2,1)S(1)}, bf16[256,512]{1,0:T(8,128)(2,1)S(1)}, u32[]{:S(2)}, u32[]{:S(2)}) %collective-permute-start.2) | collective-permute-done | bytes 262176 | tf_op jit(solution)/shard_map/ppermute | solution.py:32
  224.2 17.7 %collective-permute-done.12 = bf16[256,128]{1,0:T(8,128)(2,1)S(1)} collective-permute-done((bf16[256,128]{1,0:T(8,128)(2,1)S(1)}, bf16[256,128]{1,0:T(8,128)(2,1)S(1)}, u32[]{:S(2)}, u32[]{:S(2)}) %collective-permute-start.12) | collective-permute-done | bytes 65568 | tf_op jit(solution)/shard_map/ppermute | solution.py:32
  251.1 8.6 collective-permute-done.14
  273.7 34.8 %all-gather.4 = f32[32,1,4]{2,1,0:T(1,128)} all-gather(f32[1,1,4]{2,1,0:T(1,128)} %get-tuple-element.663), channel_id=6, replica_groups=mesh['seq'=32,'head'=8] {'seq'}, dimensions={0}, use_global_device_ids=true | all-gather | bytes 528 | tf_op jit(solution)/shard_map/all_gather | solution.py:11
  317.3 31.7 %all-gather.6 = f32[32,1,4]{2,1,0:T(1,128)} all-gather(f32[1,1,4]{2,1,0:T(1,128)} %get-tuple-element.661), channel_id=8, replica_groups=mesh['seq'=32,'head'=8] {'seq'}, dimensions={0}, use_global_device_ids=true | all-gather | bytes 528 | tf_op jit(solution)/shard_map/all_gather | solution.py:11
  349.1 34.7 %all-gather.2 = f32[32,1,4]{2,1,0:T(1,128)} all-gather(f32[1,1,4]{2,1,0:T(1,128)} %get-tuple-element.670), channel_id=4, replica_groups=mesh['seq'=32,'head'=8] {'seq'}, dimensions={0}, use_global_device_ids=true | all-gather | bytes 528 | tf_op jit(solution)/shard_map/all_gather | solution.py:11
  398.1 56.7 %while.62 = (s32[]{:T(128)}, f32[4,128,128]{2,1,0:T(8,128)S(1)}, s32[]{:T(128)}, f32[32,4]{1,0:T(8,128)}, f32[32,4,128,128]{3,2,1,0:T(8,128)}, /*index=5*/s32[]{:T(128)}, s32[]{:T(128)}, s32[]{:T(128)}, s32[]{:T(128)}) while((s32[]{:T(128)}, f32[4,128,128]{2,1,0:T(8,128)S(1)}, s32[]{:T(128)}, f32[32,4]{1,0:T(8,128)}, ...), condition=%wide.region_12.13_spmd.clone, body=%wide.region_11.12_spmd.clone.sunk | while | flops 262152 | bytes 786647 | solution.py:22
  460.8 56.6 %while.63 = (s32[]{:T(128)}, f32[4,128,128]{2,1,0:T(8,128)S(1)}, s32[]{:T(128)}, f32[32,4]{1,0:T(8,128)}, f32[32,4,128,128]{3,2,1,0:T(8,128)}, /*index=5*/s32[]{:T(128)}, s32[]{:T(128)}, s32[]{:T(128)}, s32[]{:T(128)}) while((s32[]{:T(128)}, f32[4,128,128]{2,1,0:T(8,128)S(1)}, s32[]{:T(128)}, f32[32,4]{1,0:T(8,128)}, ...), condition=%wide.region_16.17_spmd.clone, body=%wide.region_15.16_spmd.clone.sunk | while | flops 262152 | bytes 786647 | solution.py:22
  529.5 56.2 %while.61 = (s32[]{:T(128)}, f32[4,128,128]{2,1,0:T(8,128)S(1)}, s32[]{:T(128)}, f32[32,4]{1,0:T(8,128)}, f32[32,4,128,128]{3,2,1,0:T(8,128)}, /*index=5*/s32[]{:T(128)}, s32[]{:T(128)}) while((s32[]{:T(128)}, f32[4,128,128]{2,1,0:T(8,128)S(1)}, s32[]{:T(128)}, f32[32,4]{1,0:T(8,128)}, f32[32,4,128,128]{3,2,1,0:T(8,128)}, ...), condition=%wide.region_7.8_spmd.clone, body=%wide.region_6.7_spmd.clone.sunk | while | flops 262148 | bytes 786585 | solution.py:22
  594.9 13.9 %collective-permute-done.32 = bf16[256,512]{1,0:T(8,128)(2,1)} collective-permute-done((bf16[256,512]{1,0:T(8,128)(2,1)S(1)}, bf16[256,512]{1,0:T(8,128)(2,1)}, u32[]{:S(2)}, u32[]{:S(2)}) %collective-permute-start.32) | collective-permute-done | bytes 262176 | tf_op jit(solution)/shard_map/ppermute | solution.py:32
  610.7 38.0 %all-gather = f32[32,1,4]{2,1,0:T(1,128)} all-gather(f32[1,1,4]{2,1,0:T(1,128)S(1)} %copy-done.36), channel_id=2, replica_groups=mesh['seq'=32,'head'=8] {'seq'}, dimensions={0}, use_global_device_ids=true | all-gather | bytes 528 | tf_op jit(solution)/shard_map/all_gather | solution.py:11
  648.7 16.3 %rev.76 = bf16[256,2048]{1,0:T(8,128)(2,1)} reverse(bf16[256,2048]{1,0:T(8,128)(2,1)} %all-gather.15.cloned.1.call-done), dimensions={1} | reverse | bytes 2097152 | tf_op jit(solution)/shard_map/jit(_flip)/rev | solution.py:193
  665.0 11.4 %rev.77 = bf16[256,2048]{1,0:T(8,128)(2,1)} reverse(bf16[256,2048]{1,0:T(8,128)(2,1)S(1)} %copy-done.6), dimensions={1} | reverse | bytes 2097152 | tf_op jit(solution)/shard_map/jit(_flip)/rev | solution.py:194
  682.6 10.4 collective-permute-done.22
  707.2 56.4 %while.60 = (s32[]{:T(128)}, f32[4,128,128]{2,1,0:T(8,128)S(1)}, s32[]{:T(128)}, f32[32,4]{1,0:T(8,128)}, f32[32,4,128,128]{3,2,1,0:T(8,128)}, /*index=5*/s32[]{:T(128)}, s32[]{:T(128)}) while((s32[]{:T(128)}, f32[4,128,128]{2,1,0:T(8,128)S(1)}, s32[]{:T(128)}, f32[32,4]{1,0:T(8,128)}, f32[32,4,128,128]{3,2,1,0:T(8,128)}, ...), condition=%wide.region_3.4_spmd.clone, body=%wide.region_2.3_spmd.clone.sunk | while | flops 262148 | bytes 786585 | solution.py:22
  791.3 33.6 %reduce-scatter.13.cloned.1.call-done = bf16[64,512]{1,0:T(8,128)(2,1)} async-done(((bf16[2048,512]{1,0:T(8,128)(2,1)}), bf16[64,512]{1,0:T(8,128)(2,1)}) %reduce-scatter.13.cloned.1.call-update) | async-done | bytes 65552
  826.6 115.2 %reduce-scatter.15.cloned.1.call-done = bf16[64,512]{1,0:T(8,128)(2,1)} async-done(((bf16[2048,512]{1,0:T(8,128)(2,1)}), bf16[64,512]{1,0:T(8,128)(2,1)}) %reduce-scatter.15.cloned.1.call-update) | async-done | bytes 65552
  943.5 75.0 %reduce-scatter.11.cloned.1.call-done = bf16[256,256]{1,0:T(8,128)(2,1)} async-done(((bf16[256,2048]{1,0:T(8,128)(2,1)}), bf16[256,256]{1,0:T(8,128)(2,1)}) %reduce-scatter.11.cloned.1.call-update) | async-done | bytes 131088 | tf_op jit(solution)/shard_map/reduce_scatter | solution.py:190
  1018.5 80.8 %reduce-scatter.9.cloned.1.call-done = bf16[256,256]{1,0:T(8,128)(2,1)} async-done(((bf16[256,2048]{1,0:T(8,128)(2,1)}), bf16[256,256]{1,0:T(8,128)(2,1)}) %reduce-scatter.9.cloned.1.call-update) | async-done | bytes 131088 | tf_op jit(solution)/shard_map/reduce_scatter | solution.py:184
  (545 shorter events, 444.2 us)
Async XLA Ops:
  7.2 55.3 %all-gather.17.cloned.1.call-start = ((), (), s32[]{:S(2)}) async-start(), calls=%async_computation.6 | async-start | bytes 1179648 | tf_op jit(solution)/shard_map/all_gather | solution.py:150
  7.9 184.3 %all-gather.15.cloned.1.call-start = ((), (), s32[]{:S(2)}) async-start(), calls=%async_computation.4 | async-start | bytes 1179648 | tf_op jit(solution)/shard_map/all_gather | solution.py:141
  8.7 389.4 %all-gather.23.cloned.1.call-start = ((), (), s32[]{:S(2)}) async-start(), calls=%async_computation.10 | async-start | bytes 8650752 | tf_op jit(solution)/shard_map/all_gather | solution.py:11
  65.8 395.1 %all-gather.25.cloned.1.call-start = ((), (), s32[]{:S(2)}) async-start(), calls=%async_computation.11 | async-start | bytes 8650752 | tf_op jit(solution)/shard_map/all_gather | solution.py:11
  98.5 31.5 %collective-permute-start.27 = (bf16[256,512]{1,0:T(8,128)(2,1)S(1)}, bf16[256,512]{1,0:T(8,128)(2,1)S(1)}, u32[]{:S(2)}, u32[]{:S(2)}) collective-permute-start(bf16[256,512]{1,0:T(8,128)(2,1)S(1)} %collective-permute-done.26), channel_id=1, source_target_pairs={{0,32},{32,0},{8,40},{40,8},{16,48},{48,16},{24,56},{56,24},{64,96... | collective-permute-start | bytes 786440 | tf_op jit(solution)/shard_map/ppermute | solution.py:32
  130.0 27.2 %collective-permute-start.28 = (bf16[256,512]{1,0:T(8,128)(2,1)S(1)}, bf16[256,512]{1,0:T(8,128)(2,1)S(1)}, u32[]{:S(2)}, u32[]{:S(2)}) collective-permute-start(bf16[256,512]{1,0:T(8,128)(2,1)S(1)} %collective-permute-done.27), channel_id=1, source_target_pairs={{0,64},{64,0},{8,72},{72,8},{16,80},{80,16},{24,88},{88,24},{32,96... | collective-permute-start | bytes 786440 | tf_op jit(solution)/shard_map/ppermute | solution.py:32
  136.0 16.5 %collective-permute-start.7 = (bf16[256,128]{1,0:T(8,128)(2,1)}, bf16[256,128]{1,0:T(8,128)(2,1)S(1)}, u32[]{:S(2)}, u32[]{:S(2)}) collective-permute-start(bf16[256,128]{1,0:T(8,128)(2,1)} %collective-permute-done.6), channel_id=1, source_target_pairs={{0,32},{32,0},{8,40},{40,8},{16,48},{48,16},{24,56},{56,24},{64,96... | collective-permute-start | bytes 196616 | tf_op jit(solution)/shard_map/ppermute | solution.py:32
  171.8 357.7 %all-gather.21.cloned.1.call-start = ((), (), s32[]{:S(2)}) async-start(), calls=%async_computation.9 | async-start | bytes 8650752 | tf_op jit(solution)/shard_map/all_gather | solution.py:11
  205.0 15.4 %collective-permute-start.2 = (bf16[256,512]{1,0:T(8,128)(2,1)S(1)}, bf16[256,512]{1,0:T(8,128)(2,1)S(1)}, u32[]{:S(2)}, u32[]{:S(2)}) collective-permute-start(bf16[256,512]{1,0:T(8,128)(2,1)S(1)} %collective-permute-done.1), channel_id=1, source_target_pairs={{0,32},{32,0},{8,40},{40,8},{16,48},{48,16},{24,56},{56,24},{64,96... | collective-permute-start | bytes 786440 | tf_op jit(solution)/shard_map/ppermute | solution.py:32
  208.3 15.3 %collective-permute-start.11 = (bf16[256,128]{1,0:T(8,128)(2,1)S(1)}, bf16[256,128]{1,0:T(8,128)(2,1)S(1)}, u32[]{:S(2)}, u32[]{:S(2)}) collective-permute-start(bf16[256,128]{1,0:T(8,128)(2,1)S(1)} %collective-permute-done.10), channel_id=1, source_target_pairs={{0,16},{16,0},{8,24},{24,8},{32,48},{48,32},{40,56},{56,40},{64,80... | collective-permute-start | bytes 196616 | tf_op jit(solution)/shard_map/ppermute | solution.py:32
  220.3 23.5 %collective-permute-start.3 = (bf16[256,512]{1,0:T(8,128)(2,1)S(1)}, bf16[256,512]{1,0:T(8,128)(2,1)}, u32[]{:S(2)}, u32[]{:S(2)}) collective-permute-start(bf16[256,512]{1,0:T(8,128)(2,1)S(1)} %collective-permute-done.2), channel_id=1, source_target_pairs={{0,64},{64,0},{8,72},{72,8},{16,80},{80,16},{24,88},{88,24},{32,96... | collective-permute-start | bytes 786440 | tf_op jit(solution)/shard_map/ppermute | solution.py:32
  223.6 18.4 %collective-permute-start.12 = (bf16[256,128]{1,0:T(8,128)(2,1)S(1)}, bf16[256,128]{1,0:T(8,128)(2,1)S(1)}, u32[]{:S(2)}, u32[]{:S(2)}) collective-permute-start(bf16[256,128]{1,0:T(8,128)(2,1)S(1)} %collective-permute-done.11), channel_id=1, source_target_pairs={{0,32},{32,0},{8,40},{40,8},{16,48},{48,16},{24,56},{56,24},{64,96... | collective-permute-start | bytes 196616 | tf_op jit(solution)/shard_map/ppermute | solution.py:32
  243.8 16.0 %collective-permute-start.4 = (bf16[256,512]{1,0:T(8,128)(2,1)}, bf16[256,512]{1,0:T(8,128)(2,1)S(1)}, u32[]{:S(2)}, u32[]{:S(2)}) collective-permute-start(bf16[256,512]{1,0:T(8,128)(2,1)} %collective-permute-done.3), channel_id=1, source_target_pairs={{0,128},{128,0},{8,136},{136,8},{16,144},{144,16},{24,152},{152,24... | collective-permute-start | bytes 786440 | tf_op jit(solution)/shard_map/ppermute | solution.py:32
  261.3 445.8 %all-gather.19.cloned.1.call-start = ((), (), s32[]{:S(2)}) async-start(), calls=%async_computation.8 | async-start | bytes 8650752 | tf_op jit(solution)/shard_map/all_gather | solution.py:11
  391.4 433.5 %reduce-scatter.13.cloned.1.call-start = ((), (), s32[]{:S(2)}) async-start(), calls=%async_computation.12 | async-start | bytes 2162688
  529.2 56.6 %collective-permute-start.30 = (bf16[256,512]{1,0:T(8,128)(2,1)}, bf16[256,512]{1,0:T(8,128)(2,1)}, u32[]{:S(2)}, u32[]{:S(2)}) collective-permute-start(bf16[256,512]{1,0:T(8,128)(2,1)} %get-tuple-element.675), channel_id=1, source_target_pairs={{0,8},{8,0},{16,24},{24,16},{32,40},{40,32},{48,56},{56,48},{64,72... | collective-permute-start | bytes 786440 | tf_op jit(solution)/shard_map/ppermute | solution.py:32
  594.7 14.2 %collective-permute-start.32 = (bf16[256,512]{1,0:T(8,128)(2,1)S(1)}, bf16[256,512]{1,0:T(8,128)(2,1)}, u32[]{:S(2)}, u32[]{:S(2)}) collective-permute-start(bf16[256,512]{1,0:T(8,128)(2,1)S(1)} %collective-permute-done.31), channel_id=1, source_target_pairs={{0,32},{32,0},{8,40},{40,8},{16,48},{48,16},{24,56},{56,24},{64,96... | collective-permute-start | bytes 786440 | tf_op jit(solution)/shard_map/ppermute | solution.py:32
  594.7 84.2 %collective-permute-start.21 = (bf16[256,512]{0,1:T(8,128)(2,1)}, bf16[256,512]{0,1:T(8,128)(2,1)}, u32[]{:S(2)}, u32[]{:S(2)}) collective-permute-start(bf16[256,512]{0,1:T(8,128)(2,1)} %collective-permute-done.20), channel_id=1, source_target_pairs={{0,16},{16,0},{8,24},{24,8},{32,48},{48,32},{40,56},{56,40},{64,80... | collective-permute-start | bytes 786440 | tf_op jit(solution)/shard_map/ppermute | solution.py:32
  608.9 70.0 %collective-permute-start.33 = (bf16[256,512]{1,0:T(8,128)(2,1)}, bf16[256,512]{1,0:T(8,128)(2,1)}, u32[]{:S(2)}, u32[]{:S(2)}) collective-permute-start(bf16[256,512]{1,0:T(8,128)(2,1)} %collective-permute-done.32), channel_id=1, source_target_pairs={{0,64},{64,0},{8,72},{72,8},{16,80},{80,16},{24,88},{88,24},{32,96... | collective-permute-start | bytes 786440 | tf_op jit(solution)/shard_map/ppermute | solution.py:32
  678.9 15.2 %collective-permute-start.34 = (bf16[256,512]{1,0:T(8,128)(2,1)}, bf16[256,512]{1,0:T(8,128)(2,1)}, u32[]{:S(2)}, u32[]{:S(2)}) collective-permute-start(bf16[256,512]{1,0:T(8,128)(2,1)} %collective-permute-done.33), channel_id=1, source_target_pairs={{0,128},{128,0},{8,136},{136,8},{16,144},{144,16},{24,152},{152,24... | collective-permute-start | bytes 786440 | tf_op jit(solution)/shard_map/ppermute | solution.py:32
  693.0 72.2 %collective-permute-start.23 = (bf16[256,512]{0,1:T(8,128)(2,1)}, bf16[256,512]{0,1:T(8,128)(2,1)}, u32[]{:S(2)}, u32[]{:S(2)}) collective-permute-start(bf16[256,512]{0,1:T(8,128)(2,1)} %collective-permute-done.22), channel_id=1, source_target_pairs={{0,64},{64,0},{8,72},{72,8},{16,80},{80,16},{24,88},{88,24},{32,96... | collective-permute-start | bytes 786440 | tf_op jit(solution)/shard_map/ppermute | solution.py:32
  707.1 234.7 %reduce-scatter.15.cloned.1.call-start = ((), (), s32[]{:S(2)}) async-start(), calls=%async_computation.13 | async-start | bytes 2162688
  783.5 235.0 %reduce-scatter.11.cloned.1.call-start = ((), (), s32[]{:S(2)}) async-start(), calls=%async_computation.7 | async-start | bytes 1179648 | tf_op jit(solution)/shard_map/reduce_scatter | solution.py:190
  787.8 311.4 %reduce-scatter.9.cloned.1.call-start = ((), (), s32[]{:S(2)}) async-start(), calls=%async_computation.5 | async-start | bytes 1179648 | tf_op jit(solution)/shard_map/reduce_scatter | solution.py:184
  (58 other events, 1289.4 us)
Sparse Core Ops, SparseCore 0:
  10.5 51.9 all-gather.16
  65.0 48.6 all-gather.14
  115.5 85.1 all-gather.22
  202.4 87.2 all-gather.24
  291.4 70.7 all-gather.20
  391.5 67.7 all-gather.18
  707.2 117.6 reduce-scatter.12
  827.5 114.1 reduce-scatter.14
  946.2 72.2 reduce-scatter.10
  1023.3 75.9 reduce-scatter.8
where the time goes:
time: 1130 us; the launch traced here: 1110 us
  waiting for transfers between devices  493 us (44%)
  local copies, waits for them, and re-layouts  214 us (19%)
  other arithmetic  152 us (13%)
  blocking collectives  139 us (12%)
  matrix products  50.3 us (4%)
  starting transfers between devices  40.6 us (4%)
  between operations  15.3 us (1%)
    unnamed x12, waiting for transfers between devices  150 us
    all_gather x4, blocking collectives, prefix_2(): everything = jax.tree.map(lambda part: lax.all_gather(part, axis), x)  139 us
    ppermute x35, waiting for transfers between devices, swapped(): return lax.ppermute(block, axis, route)  138 us
    select_n x128, other arithmetic, turn(): return jax.tree.map(lambda a, b: jnp.where(reached, a, b), new, before)  135 us
    exp x128, local copies, waits for them, and re-layouts, combine_states(): jnp.exp(latter[0])[..., None, None] * earlier[1] + latter[1]  88.2 us
    reduce_scatter x1, waiting for transfers between devices, shards(): lax.psum_scatter(partial_out.astype(jnp.bfloat16), 'head', scatter_dimens...  80.8 us
    reduce_scatter x1, waiting for transfers between devices, shards(): lax.psum_scatter(partial_tokens.astype(jnp.bfloat16), 'head', scatter_dim...  75 us
    all_gather x1, waiting for transfers between devices, shards(): full_cotangent = lax.all_gather(cotangent, 'head', axis=1, tiled=True)  48.4 us
  transfers between devices with their start and end apart: 45, of which 25 were waited for; matrix products, arithmetic and copies ran while one was open for 37% of the time, Pallas kernels for 0%

commit v1 on v0

v1 whole, which is shorter than its diff:
```python
import jax
import jax.numpy as jnp
from jax import lax
from jax.experimental import pallas as pl
from jax.experimental.pallas import tpu as pltpu
from jax.sharding import PartitionSpec as P

F32 = jnp.float32
BF16 = jnp.bfloat16
VMEM_BYTES = 48 * 1024 * 1024
HEADS = 4
N = 128
T = 256
UPWARD = (True, False, False, True)
DECAY_OF = (0, 1, 0, 1)


def mm(a, b):
    return jnp.dot(a, b, preferred_element_type=F32)


def mm_nt(a, b):
    return lax.dot_general(a, b, (((1,), (1,)), ((), ())), preferred_element_type=F32)


def call(kernel, outs, *args, scalars=0):
    return pl.pallas_call(
        kernel,
        out_shape=outs,
        in_specs=[pl.BlockSpec(memory_space=pltpu.SMEM)] * scalars
        + [pl.BlockSpec(memory_space=pltpu.VMEM)] * (len(args) - scalars),
        out_specs=[pl.BlockSpec(memory_space=pltpu.VMEM)] * len(outs),
        compiler_params=pltpu.CompilerParams(vmem_limit_bytes=VMEM_BYTES),
    )(*args)


def shaped(*dims, dtype=BF16):
    return jax.ShapeDtypeStruct(dims, dtype)


def iotas(rows, columns):
    return (
        lax.broadcasted_iota(jnp.int32, (rows, columns), 0),
        lax.broadcasted_iota(jnp.int32, (rows, columns), 1),
    )


def exchange(size):
    row, column = iotas(size, size)
    return (row + column == size - 1).astype(F32).astype(BF16)


def totals_kernel(decay, totals):
    for d in range(2):
        ones = jnp.ones((T, N), BF16)
        sums = lax.dot_general(
            decay[d], ones, (((0,), (0,)), ((), ())), preferred_element_type=F32
        )
        totals[d * HEADS : (d + 1) * HEADS, :] = sums


def weights_kernel(keys, queries, decay, w_in, w_out, inner, readers, writers, in_rev, out_rev):
    row, column = iotas(T, T)
    lower = row >= column
    upper = row <= column
    identity = (row == column).astype(F32).astype(BF16)[:N, :N]
    for d in range(2):
        k, q = keys[d], queries[d]
        k_t, q_t = mm_nt(identity, k), mm_nt(identity, q)
        k32, q32 = k.astype(F32), q.astype(F32)
        past = lower if d == 0 else upper
        reach = past.astype(F32).astype(BF16)
        down = mm(reach, decay[d])
        along = lax.dot_general(
            decay[d], reach, (((0,), (1,)), ((), ())), preferred_element_type=F32
        )
        scores, scores_t = mm_nt(q, k), mm_nt(k, q)
        future = upper if d == 0 else lower
        for h in range(HEADS):
            c = down[:, h : h + 1]
            r = along[h : h + 1, :]
            last = T - 1 if d == 0 else 0
            total_c = c[last : last + 1, :]
            total_r = r[:, last : last + 1]
            gaps = c - r
            inner[d, h] = jnp.where(
                past, scores * jnp.exp(jnp.where(past, gaps, 0.0)), 0.0
            ).astype(BF16)
            inner[2 + d, h] = jnp.where(
                future, scores_t * jnp.exp(jnp.where(future, -gaps, 0.0)), 0.0
            ).astype(BF16)
            readers[d, h] = (jnp.exp(c) * q32).astype(BF16)
            readers[2 + d, h] = (jnp.exp(total_c - c) * k32).astype(BF16)
            writers[d, h] = (jnp.exp(total_r - r) * k_t).astype(BF16)
            writers[2 + d, h] = (jnp.exp(r) * q_t).astype(BF16)
    flip = exchange(T)
    for j in range(8):
        rows = slice(T * j, T * (j + 1))
        mirrored = slice(T * (7 - j), T * (8 - j))
        in_rev[mirrored, :] = mm(flip, w_in[rows, :]).astype(BF16)
        out_rev[mirrored, :] = mm(flip, w_out[rows, :]).astype(BF16)


def inside_kernel(
    core, skip, gathered, w_in, in_rev, w_out, out_rev, inner, writers, local, own, send
):
    c = core[0]
    tokens = jnp.concatenate([gathered[j, :T, :] for j in range(8)], axis=1)
    cotangent = jnp.concatenate([gathered[j, T:, :] for j in range(8)], axis=1)
    sides = ((tokens, w_in), (tokens, in_rev), (cotangent, w_out), (cotangent, out_rev))
    for k in range(4):
        left, right = sides[k]
        values = mm(left, right[...]).astype(BF16)
        for h in range(HEADS):
            lanes = slice(N * h, N * (h + 1))
            v = values[:, lanes]
            local[k, :, lanes] = mm(inner[k, h], v) + skip[h] * v.astype(F32)
            state = mm(writers[k, h], v).astype(BF16)
            at = 2 * k + h % 2

            @pl.when(c == h // 2)
            def _():
                own[at] = state

            @pl.when(c != h // 2)
            def _():
                send[at] = state


def pair_of(c, own, recv, totals, other_totals, at):
    k, which = at // 2, at % 2
    first = DECAY_OF[k] * HEADS + which
    second = first + 2
    here = c == 0
    mine = jnp.where(here, totals[first : first + 1, :], totals[second : second + 1, :])
    theirs = jnp.where(
        here, other_totals[first : first + 1, :], other_totals[second : second + 1, :]
    )
    a, b = own[at].astype(F32), recv[at].astype(F32)
    low = (jnp.where(here, a, b), jnp.where(here, mine, theirs))
    high = (jnp.where(here, b, a), jnp.where(here, theirs, mine))
    return low, high


def chip_kernel(core, own, recv, totals, other_totals, out):
    c = core[0]
    line = lax.broadcasted_iota(jnp.int32, (16, N), 0)
    for at in range(8):
        low, high = pair_of(c, own, recv, totals, other_totals, at)
        if UPWARD[at // 2]:
            state = jnp.exp(high[1]) * low[0] + high[0]
        else:
            state = jnp.exp(low[1]) * high[0] + low[0]
        total = low[1] + high[1]
        one = total.astype(BF16).astype(F32)
        two = (total - one).astype(BF16).astype(F32)
        three = total - one - two
        note = jnp.where(line == 0, one, jnp.where(line == 1, two, jnp.where(line == 2, three, 0.0)))
        for half in range(2):
            out[2 * at + half, :64, :] = state[64 * half : 64 * (half + 1), :].astype(BF16)
            out[2 * at + half, 64:, :] = note.astype(BF16)


def carry_kernel(upward, states, out):
    up = upward[0] == 1

    def turn(step, carried):
        place = jnp.where(up, step, 15 - step)
        out[place] = carried.astype(BF16)
        note = states[place, 64:, :].astype(F32)
        decay = jnp.exp(note[0:1, :] + note[1:2, :] + note[2:3, :])
        return decay * carried + states[place, :64, :].astype(F32)

    lax.fori_loop(0, 16, turn, jnp.zeros((64, N), F32))


def spread_kernel(core, chip, own, recv, totals, other_totals, mine, send):
    c = core[0]
    here = c == 0
    for at in range(8):
        low, high = pair_of(c, own, recv, totals, other_totals, at)
        before = jnp.concatenate([chip[2 * at], chip[2 * at + 1]], axis=0).astype(F32)
        if UPWARD[at // 2]:
            at_low, at_high = before, jnp.exp(low[1]) * before + low[0]
        else:
            at_low, at_high = jnp.exp(high[1]) * before + high[0], before
        mine[at] = jnp.where(here, at_low, at_high).astype(BF16)
        send[at] = jnp.where(here, at_high, at_low).astype(BF16)


def turned_kernel(gathered, tokens_t, cotangent_t):
    row, column = iotas(T, T)
    identity = (row == column).astype(F32).astype(BF16)
    flip = exchange(T)
    for j in range(8):
        rows = slice(T * j, T * (j + 1))
        for out, part in ((tokens_t, slice(0, T)), (cotangent_t, slice(T, 2 * T))):
            out[rows, :T] = mm_nt(identity, gathered[j, part, :]).astype(BF16)
            out[rows, T:] = mm_nt(flip, gathered[7 - j, part, :]).astype(BF16)


def outputs_kernel(core, local, readers, mine, theirs, tokens_t, cotangent_t, results, keep, send):
    c = core[0]
    here = c == 0
    for k in range(4):
        for h in range(HEADS):
            lanes = slice(N * h, N * (h + 1))
            at = 2 * k + h % 2
            a, b = mine[at].astype(F32), theirs[at].astype(F32)
            carried = jnp.where(here == (h // 2 == 0), a, b).astype(BF16)
            results[T * k : T * (k + 1), lanes] = (
                local[k, :, lanes] + mm(readers[k, h], carried)
            ).astype(BF16)
    for g, (left, right) in enumerate(((tokens_t, 2), (cotangent_t, 0))):
        stacked = results[T * right : T * (right + 2), :]
        for j in range(8):
            part = mm(left[T * j : T * (j + 1), :], stacked)
            for pair in range(2):
                even = part[128 * pair : 128 * pair + 64, :]
                odd = part[128 * pair + 64 : 128 * pair + 128, :]
                at = 2 * j + pair
                keep[at // 8, at % 8, g] = jnp.where(here, even, odd).astype(BF16)
                send[at // 8, at % 8, g] = jnp.where(here, odd, even).astype(BF16)


def partials_kernel(results, w_in, in_rev, w_out, out_rev, out):
    for j in range(8):
        rows = slice(T * j, T * (j + 1))
        out[j, :T, :] = (
            mm_nt(results[:T, :], w_out[rows, :]) + mm_nt(results[T : 2 * T, :], out_rev[rows, :])
        ).astype(BF16)
        out[j, T:, :] = (
            mm_nt(results[2 * T : 3 * T, :], w_in[rows, :])
            + mm_nt(results[3 * T :, :], in_rev[rows, :])
        ).astype(BF16)


def partner(block, bit):
    count = lax.axis_size("seq")
    return lax.ppermute(block, "seq", [(i, i ^ bit) for i in range(count)])


def shards(tokens, weight_in, weight_out, state_keys, state_queries, log_decay, skip_gain, cotangent):
    place = lax.axis_index("seq")
    core = (place % 2).reshape(1)
    chip = place // 2
    x_lo = place // 16
    task = chip // 4
    upward = jnp.logical_or(task == 0, task == 3).astype(jnp.int32).reshape(1)
    chips = [[2 * i + c for i in range(16)] for c in range(2)]
    lines = [[16 * x + 2 * z + c for z in range(8)] for x in range(2) for c in range(2)]

    both = jnp.concatenate([tokens, cotangent], axis=0)
    gathered = lax.all_to_all(jnp.broadcast_to(both, (8, 2 * T, 256)), "head", 0, 0)

    (totals,) = call(totals_kernel, [shaped(8, N, dtype=F32)], log_decay)
    other_totals = partner(totals, 1)
    inner, readers, writers, in_rev, out_rev = call(
        weights_kernel,
        [
            shaped(4, HEADS, T, T),
            shaped(4, HEADS, T, N),
            shaped(4, HEADS, N, T),
            shaped(2048, 512),
            shaped(2048, 512),
        ],
        state_keys,
        state_queries,
        log_decay,
        weight_in,
        weight_out,
    )
    local, own, send = call(
        inside_kernel,
        [shaped(4, T, 512, dtype=F32), shaped(8, N, N), shaped(8, N, N)],
        core,
        skip_gain,
        gathered,
        weight_in,
        in_rev,
        weight_out,
        out_rev,
        inner,
        writers,
        scalars=2,
    )
    recv = partner(send, 1)
    (chip_states,) = call(
        chip_kernel, [shaped(16, 80, N)], core, own, recv, totals, other_totals, scalars=1
    )
    spread_states = lax.all_to_all(chip_states, "seq", 0, 0, axis_index_groups=chips)
    (carried,) = call(carry_kernel, [shaped(16, 64, N)], upward, spread_states, scalars=1)
    chip_carried = lax.all_to_all(carried, "seq", 0, 0, axis_index_groups=chips)
    mine, send = call(
        spread_kernel,
        [shaped(8, N, N), shaped(8, N, N)],
        core,
        chip_carried,
        own,
        recv,
        totals,
        other_totals,
        scalars=1,
    )
    theirs = partner(send, 1)
    tokens_t, cotangent_t = call(turned_kernel, [shaped(2048, 512)] * 2, gathered)
    results, keep, send = call(
        outputs_kernel,
        [shaped(4 * T, 512), shaped(2, 8, 2, 64, 512), shaped(2, 8, 2, 64, 512)],
        core,
        local,
        readers,
        mine,
        theirs,
        tokens_t,
        cotangent_t,
        scalars=1,
    )
    recv = partner(send, 1)
    (partials,) = call(
        partials_kernel, [shaped(8, 2 * T, 256)], results, weight_in, in_rev, weight_out, out_rev
    )
    chip_sum = keep.astype(F32) + recv.astype(F32)
    away = lax.dynamic_index_in_dim(chip_sum, 1 - x_lo, 0, keepdims=False).astype(BF16)
    stay = lax.dynamic_index_in_dim(chip_sum, x_lo, 0, keepdims=False)
    arrived = partner(away, 16)
    shares = lax.all_to_all(partials, "head", 0, 0)
    sums = jnp.sum(shares.astype(F32), axis=0).astype(BF16)
    line_sum = (stay + arrived.astype(F32)).astype(BF16)
    pieces = lax.all_to_all(line_sum, "seq", 0, 0, axis_index_groups=lines)
    gradients = jnp.sum(pieces.astype(F32), axis=0)
    return sums[:T], sums[T:], gradients[0], gradients[1]


def solution(mesh):
    return jax.shard_map(
        shards,
        mesh=mesh,
        in_specs=(
            P("seq", "head"),
            P(None, "head"),
            P(None, "head"),
            P(None, "seq", None),
            P(None, "seq", None),
            P(None, "seq", "head"),
            P("head"),
            P("seq", "head"),
        ),
        out_specs=(P("seq", "head"), P("seq", "head"), P("seq", "head"), P("seq", "head")),
        check_vma=False,
    )
```

time: 1130 us -> 204 us (0.18); the launches traced: 1110 us -> 201 us
  waiting for transfers between devices: 493 us -> 96.5 us
  local copies, waits for them, and re-layouts: 214 us -> 18.7 us
  other arithmetic: 152 us -> 8.43 us
  blocking collectives: 139 us -> 14.5 us
  matrix products: 50.3 us -> 0 us
  Pallas kernels: 0 us -> 33.4 us
  between operations: 15.3 us -> 0.85 us
  starting transfers between devices: 40.6 us -> 28.8 us
    reduce_scatter x2 -> x0, waiting for transfers between devices: 156 us -> none  [the longest x1 80.8 us: shards(): lax.psum_scatter(partial_out.astype(jnp.bfloat16), 'head', scatter_dimens...]
    unnamed x12 -> x0, waiting for transfers between devices: 150 us -> none
    all_gather x4 -> x0, blocking collectives: 139 us -> none  [prefix_2(): everything = jax.tree.map(lambda part: lax.all_gather(part, axis), x)]
    select_n x128 -> x0, other arithmetic: 135 us -> none  [turn(): return jax.tree.map(lambda a, b: jnp.where(reached, a, b), new, before)]
    ppermute x35 -> x5, waiting for transfers between devices: 138 us -> 42 us  [partner(): return lax.ppermute(block, 'seq', [(i, i ^ bit) for i in range(count)])]
    exp x132 -> x0, local copies, waits for them, and re-layouts: 92.1 us -> none  [the longest x128 88.2 us: combine_states(): jnp.exp(latter[0])[..., None, None] * earlier[1] + latter[1]]
    rev x18 -> x0, local copies, waits for them, and re-layouts: 88.2 us -> none  [the longest x1 20.4 us: shards(): weight_in_flip = jnp.flip(weight_in, 0)]
    all_to_all x0 -> x4, waiting for transfers between devices: none -> 54.6 us  [the longest x1 25.4 us: shards(): pieces = lax.all_to_all(line_sum, 'seq', 0, 0, axis_index_groups=lines)]
  transfers between devices with their start and end apart: 45 -> 9, of which waited for: 25 -> 5; matrix products, arithmetic and copies ran while one was open for 37% -> 4% of each run, Pallas kernels for 0% -> 7%
where the time goes in v1:
time: 204 us; the launch traced here: 201 us
  waiting for transfers between devices  96.5 us (47%)
  Pallas kernels  33.4 us (16%)
  starting transfers between devices  28.8 us (14%)
  local copies, waits for them, and re-layouts  18.7 us (9%)
  blocking collectives  14.5 us (7%)
  other arithmetic  8.43 us (4%)
    ppermute x5, waiting for transfers between devices, partner(): return lax.ppermute(block, 'seq', [(i, i ^ bit) for i in range(count)])  42 us
    pallas_call x9, Pallas kernels, call(): pl.pallas_call(kernel, out_shape=outs, in_specs=[pl.BlockSpec(memory_spac...  33.4 us
    all_to_all x1, waiting for transfers between devices, shards(): pieces = lax.all_to_all(line_sum, 'seq', 0, 0, axis_index_groups=lines)  25.4 us
    all_to_all x1, waiting for transfers between devices, shards(): lax.all_to_all(jnp.broadcast_to(both, (8, 2 * T, 256)), 'head', 0, 0)  17.4 us
    unnamed x37, local copies, waits for them, and re-layouts  15.6 us
    all_to_all x1, blocking collectives, shards(): chip_carried = lax.all_to_all(carried, 'seq', 0, 0, axis_index_groups=chips)  14.5 us
    all_to_all x1, waiting for transfers between devices, shards(): lax.all_to_all(chip_states, 'seq', 0, 0, axis_index_groups=chips)  11.7 us
    all_to_all x1, starting transfers between devices, shards(): lax.all_to_all(chip_states, 'seq', 0, 0, axis_index_groups=chips)  8.83 us
  transfers between devices with their start and end apart: 9, of which 5 were waited for; matrix products, arithmetic and copies ran while one was open for 4% of the time, Pallas kernels for 7%

profile of v1, /device:TPU:8, one launch (start us, length us, event | category | flops | bytes accessed | tf_op | source)
XLA Modules:
  0.0 201.2 jit_solution(5646426971020538307)
XLA Ops:
  1.6 1.5 broadcast_in_dim.3
  3.1 7.5 %all-to-all-start = ((bf16[8,512,256]{2,1,0:T(8,128)(2,1)}), bf16[8,512,256]{2,1,0:T(8,128)(2,1)S(1)}, u32[]{:S(2)}, u32[]{:S(2)}) async-start(bf16[8,512,256]{2,1,0:T(8,128)(2,1)} %broadcast_in_dim.3), calls=%async_computation | async-start | bytes 4194304 | tf_op jit(solution)/shard_map/all_to_all | solution.py:254
  10.9 6.4 %shard_map.111 = (bf16[4,4,256,256]{3,2,1,0:T(8,128)(2,1)S(1)}, bf16[4,4,256,128]{3,2,1,0:T(8,128)(2,1)S(1)}, bf16[4,4,128,256]{3,2,1,0:T(8,128)(2,1)S(1)}, bf16[2048,512]{1,0:T(8,128)(2,1)}, bf16[2048,512]{1,0:T(8,128)(2,1)}) custom-call(bf16[2,256,128]{2,1,0:T(8,128)(2,1)S(1)} %copy-done.13, bf16[2,256,128]{2,1,0:T(8,128)(2,1)S(1)} %copy-done.14, ...), custom_call_target="tpu_custom_call" | custom-call | tf_op jit(solution)/shard_map/pallas_call | solution.py:27
  17.3 1.4 copy-done.8
  19.7 17.4 %all-to-all-done.gathered = bf16[8,512,256]{2,1,0:T(8,128)(2,1)S(1)} async-done(((bf16[8,512,256]{2,1,0:T(8,128)(2,1)}), bf16[8,512,256]{2,1,0:T(8,128)(2,1)S(1)}, u32[]{:S(2)}, u32[]{:S(2)}) %all-to-all-start) | async-done | bytes 2097184 | tf_op jit(solution)/shard_map/all_to_all | solution.py:254
  37.1 2.0 copy-done.12
  39.1 10.3 %shard_map.112 = (f32[4,256,512]{2,1,0:T(8,128)S(1)}, bf16[8,128,128]{2,1,0:T(8,128)(2,1)S(1)}, bf16[8,128,128]{2,1,0:T(8,128)(2,1)S(1)}) custom-call(s32[1]{0:T(128)} %bitcast.core, f32[4]{0:T(128)S(1)} %copy-done.15, bf16[8,512,256]{2,1,0:T(8,128)(2,1)S(1)} %all-to-all-done.gathered, bf16[2048,512]{1,0:T(8,128)(2,1)} %w_in.5, ...), custom_call_target="tpu_custom_call" | custom-call | tf_op jit(solution)/shard_map/pallas_call | solution.py:27
  49.4 1.4 copy-done.3
  53.2 8.8 %all-to-all-start.1 = ((bf16[16,80,128]{2,1,0:T(8,128)(2,1)}), bf16[16,80,128]{2,1,0:T(8,128)(2,1)S(1)}, u32[]{:S(2)}, u32[]{:S(2)}) async-start(bf16[16,80,128]{2,1,0:T(8,128)(2,1)} %shard_map.114), calls=%async_computation.1 | async-start | bytes 655360 | tf_op jit(solution)/shard_map/all_to_all | solution.py:291
  62.1 11.7 %all-to-all-done.1.states = bf16[16,80,128]{2,1,0:T(8,128)(2,1)S(1)} async-done(((bf16[16,80,128]{2,1,0:T(8,128)(2,1)}), bf16[16,80,128]{2,1,0:T(8,128)(2,1)S(1)}, u32[]{:S(2)}, u32[]{:S(2)}) %all-to-all-start.1) | async-done | bytes 327712 | tf_op jit(solution)/shard_map/all_to_all | solution.py:291
  74.1 14.5 %all_to_all.25.chip = bf16[16,64,128]{2,1,0:T(8,128)(2,1)S(1)} all-to-all(bf16[16,64,128]{2,1,0:T(8,128)(2,1)S(1)} %shard_map.115), channel_id=1, replica_groups={{0,16,32,48,64,80,96,112,128,144,160,176,192,208,224,240},{8,24,40,56,7..., dimensions={0} | all-to-all | bytes 524288 | tf_op jit(solution)/shard_map/all_to_all | solution.py:293
  89.1 2.9 %shard_map.117 = (bf16[2048,512]{1,0:T(8,128)(2,1)S(1)}, bf16[2048,512]{1,0:T(8,128)(2,1)S(1)}) custom-call(bf16[8,512,256]{2,1,0:T(8,128)(2,1)} %copy-done), custom_call_target="tpu_custom_call" | custom-call | tf_op jit(solution)/shard_map/pallas_call | solution.py:27
  93.3 1.4 copy-done.7
  94.7 7.1 %shard_map.118 = (bf16[1024,512]{1,0:T(8,128)(2,1)S(1)}, bf16[2,8,2,64,512]{4,3,2,1,0:T(8,128)(2,1)S(1)}, bf16[2,8,2,64,512]{4,3,2,1,0:T(8,128)(2,1)}) custom-call(s32[1]{0:T(128)} %bitcast.core, f32[4,256,512]{2,1,0:T(8,128)} %copy-done.3, bf16[4,4,256,128]{3,2,1,0:T(8,128)(2,1)S(1)} %get-tuple-element.24.readers, ...), custom_call_target="tpu_custom_call" | custom-call | tf_op jit(solution)/shard_map/pallas_call | solution.py:27
  101.8 1.4 copy-done.4
  105.9 5.2 %shard_map.119 = bf16[8,512,256]{2,1,0:T(8,128)(2,1)S(1)} custom-call(bf16[1024,512]{1,0:T(8,128)(2,1)S(1)} %copy-done.10, bf16[2048,512]{1,0:T(8,128)(2,1)S(1)} %copy-done.1, bf16[2048,512]{1,0:T(8,128)(2,1)} %get-tuple-element.19.in_rev, bf16[2048,512]{1,0:T(8,128)(2,1)} %w_out.5, bf16[2048,512]{1,0:T(8,128)(2,1)} %get-tuple-element.20.out_rev), custom_call_target="tpu_custom_call" | custom-call | tf_op jit(solution)/shard_map/pallas_call | solution.py:27
  112.4 6.1 %all-to-all-start.3 = ((bf16[8,512,256]{2,1,0:T(8,128)(2,1)}), bf16[8,512,256]{2,1,0:T(8,128)(2,1)}, u32[]{:S(2)}, u32[]{:S(2)}) async-start(bf16[8,512,256]{2,1,0:T(8,128)(2,1)} %copy-done.2), calls=%async_computation.3 | async-start | bytes 4194304 | tf_op jit(solution)/shard_map/all_to_all | solution.py:327
  118.6 2.4 %convert_add_fusion = f32[2,8,2,64,512]{4,3,2,1,0:T(8,128)S(1)} fusion(bf16[2,8,2,64,512]{4,3,2,1,0:T(8,128)(2,1)} %collective-permute-done.3, bf16[2,8,2,64,512]{4,3,2,1,0:T(8,128)(2,1)S(1)} %copy-done.5), kind=kLoop, calls=%fused_computation | loop fusion | flops 3145728 | bytes 8388608 | tf_op jit(solution)/shard_map/add | solution.py:323
  120.9 2.0 copy-done.16
  124.4 41.1 %collective-permute-done.4 = bf16[8,2,64,512]{3,2,1,0:T(8,128)(2,1)S(1)} collective-permute-done((bf16[8,2,64,512]{3,2,1,0:T(8,128)(2,1)S(1)}, bf16[8,2,64,512]{3,2,1,0:T(8,128)(2,1)S(1)}, u32[]{:S(2)}, u32[]{:S(2)}) %collective-permute-start.4) | collective-permute-done | bytes 1048608 | tf_op jit(solution)/shard_map/ppermute | solution.py:240
  165.5 3.0 %fusion = bf16[8,2,64,512]{3,2,1,0:T(8,128)(2,1)} fusion(bf16[8,2,64,512]{3,2,1,0:T(8,128)(2,1)S(1)} %collective-permute-done.4, f32[2,8,2,64,512]{4,3,2,1,0:T(8,128)} %copy-done.16, s32[]{:T(128)S(6)} %select_n.28), kind=kLoop, calls=%fused_computation.2 | loop fusion | flops 1572864 | bytes 4194308 | tf_op jit(solution)/shard_map/convert_element_type | solution.py:329
  168.5 3.8 %all-to-all-start.4 = ((bf16[8,2,64,512]{3,2,1,0:T(8,128)(2,1)}), bf16[8,2,64,512]{3,2,1,0:T(8,128)(2,1)S(1)}, u32[]{:S(2)}, u32[]{:S(2)}) async-start(bf16[8,2,64,512]{3,2,1,0:T(8,128)(2,1)} %fusion), calls=%async_computation.4 | async-start | bytes 2097152 | tf_op jit(solution)/shard_map/all_to_all | solution.py:330
  172.3 2.0 reduce_sum.21
  175.0 25.4 %all-to-all-done.4 = bf16[8,2,64,512]{3,2,1,0:T(8,128)(2,1)S(1)} async-done(((bf16[8,2,64,512]{3,2,1,0:T(8,128)(2,1)}), bf16[8,2,64,512]{3,2,1,0:T(8,128)(2,1)S(1)}, u32[]{:S(2)}, u32[]{:S(2)}) %all-to-all-start.4) | async-done | bytes 1048608 | tf_op jit(solution)/shard_map/all_to_all | solution.py:330
  (50 shorter events, 13.8 us)
Async XLA Ops:
  3.1 7.5 %copy-start.17 = (bf16[2,256,4]{1,2,0:T(4,128)(2,1)S(1)}, bf16[2,256,4]{1,2,0:T(4,128)(2,1)}, u32[]{:S(2)}) copy-start(bf16[2,256,4]{1,2,0:T(4,128)(2,1)} %param.13) | copy-start | bytes 12292
  3.1 7.7 %copy-start.13 = (bf16[2,256,128]{2,1,0:T(8,128)(2,1)S(1)}, bf16[2,256,128]{2,1,0:T(8,128)(2,1)}, u32[]{:S(2)}) copy-start(bf16[2,256,128]{2,1,0:T(8,128)(2,1)} %keys.1) | copy-start | bytes 393220
  3.1 7.7 %copy-start.14 = (bf16[2,256,128]{2,1,0:T(8,128)(2,1)S(1)}, bf16[2,256,128]{2,1,0:T(8,128)(2,1)}, u32[]{:S(2)}) copy-start(bf16[2,256,128]{2,1,0:T(8,128)(2,1)} %queries.1) | copy-start | bytes 393220
  3.1 34.0 %all-to-all-start = ((bf16[8,512,256]{2,1,0:T(8,128)(2,1)}), bf16[8,512,256]{2,1,0:T(8,128)(2,1)S(1)}, u32[]{:S(2)}, u32[]{:S(2)}) async-start(bf16[8,512,256]{2,1,0:T(8,128)(2,1)} %broadcast_in_dim.3), calls=%async_computation | async-start | bytes 4194304 | tf_op jit(solution)/shard_map/all_to_all | solution.py:254
  10.9 26.3 %copy-start.15 = (f32[4]{0:T(128)S(1)}, f32[4]{0:T(128)}, u32[]{:S(2)}) copy-start(f32[4]{0:T(128)} %skip.1) | copy-start | bytes 52
  17.3 1.4 copy-start.8
  37.1 12.3 %copy-start = (bf16[8,512,256]{2,1,0:T(8,128)(2,1)}, bf16[8,512,256]{2,1,0:T(8,128)(2,1)S(1)}, u32[]{:S(2)}) copy-start(bf16[8,512,256]{2,1,0:T(8,128)(2,1)S(1)} %all-to-all-done.gathered) | copy-start | bytes 6291460
  37.1 2.0 copy-start.12
  49.4 1.4 copy-start.3
  50.8 1.5 collective-permute-start
  51.0 1.4 collective-permute-start.1
  53.2 20.6 %all-to-all-start.1 = ((bf16[16,80,128]{2,1,0:T(8,128)(2,1)}), bf16[16,80,128]{2,1,0:T(8,128)(2,1)S(1)}, u32[]{:S(2)}, u32[]{:S(2)}) async-start(bf16[16,80,128]{2,1,0:T(8,128)(2,1)} %shard_map.114), calls=%async_computation.1 | async-start | bytes 655360 | tf_op jit(solution)/shard_map/all_to_all | solution.py:291
  88.8 5.9 %collective-permute-start.2 = (bf16[8,128,128]{2,1,0:T(8,128)(2,1)S(1)}, bf16[8,128,128]{2,1,0:T(8,128)(2,1)S(1)}, u32[]{:S(2)}, u32[]{:S(2)}) collective-permute-start(bf16[8,128,128]{2,1,0:T(8,128)(2,1)S(1)} %get-tuple-element.28), channel_id=1, source_target_pairs={{0,8},{8,0},{16,24},{24,16},{32,40},{40,32},{48,56},{56,48},{64,72... | collective-permute-start | bytes 786440 | tf_op jit(solution)/shard_map/ppermute | solution.py:240
  91.9 1.4 copy-start.6
  93.3 1.4 copy-start.7
  94.7 10.0 %copy-start.1 = (bf16[2048,512]{1,0:T(8,128)(2,1)S(1)}, bf16[2048,512]{1,0:T(8,128)(2,1)}, u32[]{:S(2)}) copy-start(bf16[2048,512]{1,0:T(8,128)(2,1)} %w_in.5) | copy-start | bytes 6291460
  101.8 1.4 copy-start.4
  104.1 14.4 %collective-permute-start.3 = (bf16[2,8,2,64,512]{4,3,2,1,0:T(8,128)(2,1)}, bf16[2,8,2,64,512]{4,3,2,1,0:T(8,128)(2,1)}, u32[]{:S(2)}, u32[]{:S(2)}) collective-permute-start(bf16[2,8,2,64,512]{4,3,2,1,0:T(8,128)(2,1)} %get-tuple-element.33), channel_id=1, source_target_pairs={{0,8},{8,0},{16,24},{24,16},{32,40},{40,32},{48,56},{56,48},{64,72... | collective-permute-start | bytes 6291464 | tf_op jit(solution)/shard_map/ppermute | solution.py:240
  111.1 1.3 copy-start.2
  112.4 6.1 %copy-start.5 = (bf16[2,8,2,64,512]{4,3,2,1,0:T(8,128)(2,1)S(1)}, bf16[2,8,2,64,512]{4,3,2,1,0:T(8,128)(2,1)}, u32[]{:S(2)}) copy-start(bf16[2,8,2,64,512]{4,3,2,1,0:T(8,128)(2,1)} %copy-done.4) | copy-start | bytes 6291460
  112.4 56.1 %all-to-all-start.3 = ((bf16[8,512,256]{2,1,0:T(8,128)(2,1)}), bf16[8,512,256]{2,1,0:T(8,128)(2,1)}, u32[]{:S(2)}, u32[]{:S(2)}) async-start(bf16[8,512,256]{2,1,0:T(8,128)(2,1)} %copy-done.2), calls=%async_computation.3 | async-start | bytes 4194304 | tf_op jit(solution)/shard_map/all_to_all | solution.py:327
  120.9 2.0 %copy-start.16 = (f32[2,8,2,64,512]{4,3,2,1,0:T(8,128)}, f32[2,8,2,64,512]{4,3,2,1,0:T(8,128)S(1)}, u32[]{:S(2)}) copy-start(f32[2,8,2,64,512]{4,3,2,1,0:T(8,128)S(1)} %convert_add_fusion) | copy-start | bytes 12582916
  123.1 42.4 %collective-permute-start.4 = (bf16[8,2,64,512]{3,2,1,0:T(8,128)(2,1)S(1)}, bf16[8,2,64,512]{3,2,1,0:T(8,128)(2,1)S(1)}, u32[]{:S(2)}, u32[]{:S(2)}) collective-permute-start(bf16[8,2,64,512]{3,2,1,0:T(8,128)(2,1)S(1)} %fusion.1), channel_id=1, source_target_pairs={{0,128},{8,136},{16,144},{24,152},{32,160},{40,168},{48,176},{56,1... | collective-permute-start | bytes 3145736 | tf_op jit(solution)/shard_map/ppermute | solution.py:240
  168.5 31.8 %all-to-all-start.4 = ((bf16[8,2,64,512]{3,2,1,0:T(8,128)(2,1)}), bf16[8,2,64,512]{3,2,1,0:T(8,128)(2,1)S(1)}, u32[]{:S(2)}, u32[]{:S(2)}) async-start(bf16[8,2,64,512]{3,2,1,0:T(8,128)(2,1)} %fusion), calls=%async_computation.4 | async-start | bytes 2097152 | tf_op jit(solution)/shard_map/all_to_all | solution.py:330
  (3 other events, 3.2 us)

commit v2 on v1

--- a/solution.py
+++ b/solution.py
@@ -7,7 +7,10 @@
 
 F32 = jnp.float32
 BF16 = jnp.bfloat16
-VMEM_BYTES = 48 * 1024 * 1024
+ORDER = 2
+SLACK = 2
+EARLY = False
+B_EXTRA = 42
 HEADS = 4
 N = 128
 T = 256
@@ -23,15 +26,35 @@
     return lax.dot_general(a, b, (((1,), (1,)), ((), ())), preferred_element_type=F32)
 
 
-def call(kernel, outs, *args, scalars=0):
+SMEM, VMEM, HBM = pltpu.SMEM, pltpu.VMEM, pltpu.HBM
+
+
+def call(kernel, outs, *args, scalars=0, far=(), far_outs=(), scratch=(), extra=0):
+    spaces = [SMEM if i < scalars else HBM if i in far else VMEM for i in range(len(args))]
+    out_spaces = [HBM if i in far_outs else VMEM for i in range(len(outs))]
+    arrays = list(args[scalars:]) + list(outs)
+    held = sum(a.size * a.dtype.itemsize for a in arrays)
     return pl.pallas_call(
         kernel,
         out_shape=outs,
-        in_specs=[pl.BlockSpec(memory_space=pltpu.SMEM)] * scalars
-        + [pl.BlockSpec(memory_space=pltpu.VMEM)] * (len(args) - scalars),
-        out_specs=[pl.BlockSpec(memory_space=pltpu.VMEM)] * len(outs),
-        compiler_params=pltpu.CompilerParams(vmem_limit_bytes=VMEM_BYTES),
+        in_specs=[pl.BlockSpec(memory_space=space) for space in spaces],
+        out_specs=[pl.BlockSpec(memory_space=space) for space in out_spaces],
+        scratch_shapes=list(scratch),
+        compiler_params=pltpu.CompilerParams(
+            vmem_limit_bytes=held + (extra + SLACK) * 1024 * 1024
+        ),
     )(*args)
+
+
+class Copies:
+    def __init__(self, semaphores):
+        self.semaphores, self.count = semaphores, 0
+
+    def start(self, source, target):
+        copy = pltpu.make_async_copy(source, target, self.semaphores.at[self.count])
+        self.count += 1
+        copy.start()
+        return copy
 
 
 def shaped(*dims, dtype=BF16):
@@ -59,7 +82,7 @@
         totals[d * HEADS : (d + 1) * HEADS, :] = sums
 
 
-def weights_kernel(keys, queries, decay, w_in, w_out, inner, readers, writers, in_rev, out_rev):
+def weights(keys, queries, decay, inner, readers, writers):
     row, column = iotas(T, T)
     lower = row >= column
     upper = row <= column
@@ -93,28 +116,42 @@
             readers[2 + d, h] = (jnp.exp(total_c - c) * k32).astype(BF16)
             writers[d, h] = (jnp.exp(total_r - r) * k_t).astype(BF16)
             writers[2 + d, h] = (jnp.exp(r) * q_t).astype(BF16)
+
+
+def sides_of(places, pieces):
+    here, across, left, left_x, right, right_x, far_t, far_c, far_tx, far_cx = pieces
+    found = []
+    for at, ref in enumerate((here, across, left, left_x, right, right_x)):
+        found.append((places[at], ref[:T, :], ref[T:, :]))
+    found.append((places[6], far_t[...], far_c[...]))
+    found.append((places[7], far_tx[...], far_cx[...]))
+    return found
+
+
+def inside_kernel(core, skip, places, *refs):
+    pieces, rest = refs[:10], refs[10:]
+    keys, queries, decay, w_in, w_out, local, readers, own, send = rest[:9]
+    sides, turned, here, inner, writers, semaphores = rest[9:]
+    c = core[0]
+    copies = Copies(semaphores)
+    waits = [copies.start(w_in, here.at[0]), copies.start(w_out, here.at[1])]
+    weights(keys, queries, decay, inner, readers, writers)
     flip = exchange(T)
-    for j in range(8):
-        rows = slice(T * j, T * (j + 1))
-        mirrored = slice(T * (7 - j), T * (8 - j))
-        in_rev[mirrored, :] = mm(flip, w_in[rows, :]).astype(BF16)
-        out_rev[mirrored, :] = mm(flip, w_out[rows, :]).astype(BF16)
-
-
-def inside_kernel(
-    core, skip, gathered, w_in, in_rev, w_out, out_rev, inner, writers, local, own, send
-):
-    c = core[0]
-    tokens = jnp.concatenate([gathered[j, :T, :] for j in range(8)], axis=1)
-    cotangent = jnp.concatenate([gathered[j, T:, :] for j in range(8)], axis=1)
-    sides = ((tokens, w_in), (tokens, in_rev), (cotangent, w_out), (cotangent, out_rev))
+    for place, *parts in sides_of(places, pieces):
+        columns = pl.ds(pl.multiple_of(place * T, T), T)
+        mirrored = pl.ds(pl.multiple_of((7 - place) * T, T), T)
+        for g, part in enumerate(parts):
+            sides[g, :, columns] = part
+            turned[g, :, mirrored] = mm(part, flip).astype(BF16)
     for k in range(4):
-        left, right = sides[k]
-        values = mm(left, right[...]).astype(BF16)
+        if k % 2 == 0:
+            waits[k // 2].wait()
+        side = (sides, turned)[k % 2]
+        values = mm(side[k // 2], here[k // 2]).astype(BF16)
         for h in range(HEADS):
             lanes = slice(N * h, N * (h + 1))
             v = values[:, lanes]
-            local[k, :, lanes] = mm(inner[k, h], v) + skip[h] * v.astype(F32)
+            local[k, :, lanes] = (mm(inner[k, h], v) + skip[h] * v.astype(F32)).astype(BF16)
             state = mm(writers[k, h], v).astype(BF16)
             at = 2 * k + h % 2
 
@@ -188,20 +225,32 @@
         send[at] = jnp.where(here, at_high, at_low).astype(BF16)
 
 
-def turned_kernel(gathered, tokens_t, cotangent_t):
+def turned_kernel(places, *refs):
+    pieces, (tokens_t, cotangent_t) = refs[:10], refs[10:]
     row, column = iotas(T, T)
     identity = (row == column).astype(F32).astype(BF16)
     flip = exchange(T)
+    for place, *parts in sides_of(places, pieces):
+        rows = pl.ds(pl.multiple_of(place * T, T), T)
+        mirrored = pl.ds(pl.multiple_of((7 - place) * T, T), T)
+        for part, out in zip(parts, (tokens_t, cotangent_t)):
+            out[rows, :T] = mm_nt(identity, part).astype(BF16)
+            out[mirrored, T:] = mm_nt(flip, part).astype(BF16)
+
+
+def gradient(here, left, right, keep, send):
     for j in range(8):
-        rows = slice(T * j, T * (j + 1))
-        for out, part in ((tokens_t, slice(0, T)), (cotangent_t, slice(T, 2 * T))):
-            out[rows, :T] = mm_nt(identity, gathered[j, part, :]).astype(BF16)
-            out[rows, T:] = mm_nt(flip, gathered[7 - j, part, :]).astype(BF16)
-
-
-def outputs_kernel(core, local, readers, mine, theirs, tokens_t, cotangent_t, results, keep, send):
-    c = core[0]
-    here = c == 0
+        part = mm(left[T * j : T * (j + 1), :], right)
+        for pair in range(2):
+            even = part[128 * pair : 128 * pair + 64, :]
+            odd = part[128 * pair + 64 : 128 * pair + 128, :]
+            at = 2 * j + pair
+            keep[at % 8, at // 8] = jnp.where(here, even, odd).astype(BF16)
+            send[at % 8, at // 8] = jnp.where(here, odd, even).astype(BF16)
+
+
+def outputs_kernel(core, local, readers, mine, theirs, results):
+    here = core[0] == 0
     for k in range(4):
         for h in range(HEADS):
             lanes = slice(N * h, N * (h + 1))
@@ -209,35 +258,121 @@
             a, b = mine[at].astype(F32), theirs[at].astype(F32)
             carried = jnp.where(here == (h // 2 == 0), a, b).astype(BF16)
             results[T * k : T * (k + 1), lanes] = (
-                local[k, :, lanes] + mm(readers[k, h], carried)
+                local[k, :, lanes].astype(F32) + mm(readers[k, h], carried)
             ).astype(BF16)
-    for g, (left, right) in enumerate(((tokens_t, 2), (cotangent_t, 0))):
-        stacked = results[T * right : T * (right + 2), :]
-        for j in range(8):
-            part = mm(left[T * j : T * (j + 1), :], stacked)
-            for pair in range(2):
-                even = part[128 * pair : 128 * pair + 64, :]
-                odd = part[128 * pair + 64 : 128 * pair + 128, :]
-                at = 2 * j + pair
-                keep[at // 8, at % 8, g] = jnp.where(here, even, odd).astype(BF16)
-                send[at // 8, at % 8, g] = jnp.where(here, odd, even).astype(BF16)
-
-
-def partials_kernel(results, w_in, in_rev, w_out, out_rev, out):
+
+
+def gradient_in_kernel(core, results, left, keep, send):
+    gradient(core[0] == 0, left, results[2 * T :, :], keep, send)
+
+
+def gradient_out_kernel(core, results, left, keep, send):
+    gradient(core[0] == 0, left, results[: 2 * T, :], keep, send)
+
+
+def partials_kernel(results, w_in, w_out, out, here, semaphores):
+    copies = Copies(semaphores)
+    flip = exchange(T)
+    stores = []
     for j in range(8):
-        rows = slice(T * j, T * (j + 1))
-        out[j, :T, :] = (
-            mm_nt(results[:T, :], w_out[rows, :]) + mm_nt(results[T : 2 * T, :], out_rev[rows, :])
-        ).astype(BF16)
-        out[j, T:, :] = (
-            mm_nt(results[2 * T : 3 * T, :], w_in[rows, :])
-            + mm_nt(results[3 * T :, :], in_rev[rows, :])
-        ).astype(BF16)
+        rows, mirrored = slice(T * j, T * (j + 1)), slice(T * (7 - j), T * (8 - j))
+        for g, weight in enumerate((w_out, w_in)):
+            first = results[2 * T * g : 2 * T * g + T, :]
+            second = results[2 * T * g + T : 2 * T * (g + 1), :]
+            turned = mm(flip, weight[mirrored, :]).astype(BF16)
+            here[j, T * g : T * (g + 1), :] = (
+                mm_nt(first, weight[rows, :]) + mm_nt(second, turned)
+            ).astype(BF16)
+        stores.append(copies.start(here.at[j], out.at[j]))
+    for copy in stores:
+        copy.wait()
+
+
+def shares_kernel(shares, mixed, tokens):
+    for g, out in enumerate((mixed, tokens)):
+        total = shares[0, T * g : T * (g + 1), :].astype(F32)
+        for j in range(1, 8):
+            total = total + shares[j, T * g : T * (g + 1), :].astype(F32)
+        out[...] = total.astype(BF16)
+
+
+def add(a, b):
+    return a.astype(F32) + b.astype(F32)
+
+
+def split_first_kernel(place, keep, recv, stay, left, right):
+    parity = lax.rem(place[0], 2)
+    for i in range(4):
+        mine, other = 2 * i + parity, 2 * i + 1 - parity
+        stay[i] = add(keep[mine], recv[mine]).astype(BF16)
+        left[i] = add(keep[other, 0], recv[other, 0]).astype(BF16)
+        right[i] = add(keep[other, 1], recv[other, 1]).astype(BF16)
+
+
+def quarter_first_kernel(place, stay, left, right, *outs):
+    for k in range(4):
+        at = lax.rem(lax.div(place[0], 2) + k, 4)
+        outs[k][0] = add(stay[at, 0], left[at]).astype(BF16)
+        outs[k][1] = add(stay[at, 1], right[at]).astype(BF16)
+
+
+def line_sum_kernel(x_lo, a, b, c, d, stay, away):
+    x = x_lo[0]
+    stay[...] = add(a[x], b[x]) + add(c[x], d[x])
+    away[...] = (add(a[1 - x], b[1 - x]) + add(c[1 - x], d[1 - x])).astype(BF16)
 
 
 def partner(block, bit):
     count = lax.axis_size("seq")
     return lax.ppermute(block, "seq", [(i, i ^ bit) for i in range(count)])
+
+
+def along_line(block, target):
+    route = []
+    for i in range(lax.axis_size("seq")):
+        x, z, c = i // 16, i // 2 % 8, i % 2
+        route.append((i, 16 * x + 2 * (target(z) % 8) + c))
+    return lax.ppermute(block, "seq", route)
+
+
+def around(block, step, turn):
+    route = []
+    for i in range(lax.axis_size("head")):
+        route.append((i, 2 * ((i // 2 + step) % 4) + (i + turn) % 2))
+    return lax.ppermute(block, "head", route)
+
+
+def beside(z):
+    return z ^ 1
+
+
+def otherwise(z):
+    return ((z - 1) ^ 1) + 1
+
+
+def z_first(line, keep, recv):
+    stay, left, right = call(
+        split_first_kernel,
+        [shaped(4, 2, 64, 512), shaped(4, 64, 512), shaped(4, 64, 512)],
+        line,
+        keep,
+        recv,
+        scalars=1,
+    )
+    return stay, along_line(left, beside), along_line(right, otherwise)
+
+
+def z_next(line, x_lo, stay, left, right):
+    parts = call(quarter_first_kernel, [shaped(2, 64, 512)] * 4, line, stay, left, right, scalars=1)
+    parts = [parts[0]] + [along_line(parts[k], lambda z, k=k: z + 2 * k) for k in (1, 2, 3)]
+    stay, away = call(
+        line_sum_kernel, [shaped(64, 512, dtype=F32), shaped(64, 512)], x_lo, *parts, scalars=1
+    )
+    return stay + partner(away, 16).astype(F32)
+
+
+def dma(count):
+    return pltpu.SemaphoreType.DMA((count,))
 
 
 def shards(tokens, weight_in, weight_out, state_keys, state_queries, log_decay, skip_gain, cotangent):
@@ -250,39 +385,45 @@
     chips = [[2 * i + c for i in range(16)] for c in range(2)]
     lines = [[16 * x + 2 * z + c for z in range(8)] for x in range(2) for c in range(2)]
 
+    head = lax.axis_index("head")
+    y, x_hi = head // 2, head % 2
+    places = jnp.stack([2 * ((y + d) % 4) + (x_hi + f) % 2 for d in (0, 3, 1, 2) for f in (0, 1)])
     both = jnp.concatenate([tokens, cotangent], axis=0)
-    gathered = lax.all_to_all(jnp.broadcast_to(both, (8, 2 * T, 256)), "head", 0, 0)
-
+    across = around(both, 0, 1)
+    left, right = around(both, 1, 0), around(both, -1, 0)
     (totals,) = call(totals_kernel, [shaped(8, N, dtype=F32)], log_decay)
     other_totals = partner(totals, 1)
-    inner, readers, writers, in_rev, out_rev = call(
-        weights_kernel,
-        [
-            shaped(4, HEADS, T, T),
-            shaped(4, HEADS, T, N),
-            shaped(4, HEADS, N, T),
-            shaped(2048, 512),
-            shaped(2048, 512),
-        ],
+    if EARLY:
+        left, right, totals, other_totals = lax.optimization_barrier(
+            (left, right, totals, other_totals)
+        )
+    left_x, right_x = around(across, 1, 0), around(across, -1, 0)
+    far_t, far_c = around(left[:T], 1, 0), around(right[T:], -1, 0)
+    far_tx, far_cx = around(left_x[:T], 1, 0), around(right_x[T:], -1, 0)
+    pieces = (both, across, left, left_x, right, right_x, far_t, far_c, far_tx, far_cx)
+    local, readers, own, send = call(
+        inside_kernel,
+        [shaped(4, T, 512), shaped(4, HEADS, T, N), shaped(8, N, N), shaped(8, N, N)],
+        core,
+        skip_gain,
+        places,
+        *pieces,
         state_keys,
         state_queries,
         log_decay,
         weight_in,
         weight_out,
-    )
-    local, own, send = call(
-        inside_kernel,
-        [shaped(4, T, 512, dtype=F32), shaped(8, N, N), shaped(8, N, N)],
-        core,
-        skip_gain,
-        gathered,
-        weight_in,
-        in_rev,
-        weight_out,
-        out_rev,
-        inner,
-        writers,
-        scalars=2,
+        scalars=3,
+        far=(16, 17),
+        scratch=[
+            VMEM((2, T, 2048), BF16),
+            VMEM((2, T, 2048), BF16),
+            VMEM((2, 2048, 512), BF16),
+            VMEM((4, HEADS, T, T), BF16),
+            VMEM((4, HEADS, N, T), BF16),
+            dma(2),
+        ],
+        extra=B_EXTRA,
     )
     recv = partner(send, 1)
     (chip_states,) = call(
@@ -290,6 +431,8 @@
     )
     spread_states = lax.all_to_all(chip_states, "seq", 0, 0, axis_index_groups=chips)
     (carried,) = call(carry_kernel, [shaped(16, 64, N)], upward, spread_states, scalars=1)
+    tokens_t, cotangent_t = call(turned_kernel, [shaped(2048, 512)] * 2, places, *pieces, scalars=1)
+    carried, tokens_t, cotangent_t = lax.optimization_barrier((carried, tokens_t, cotangent_t))
     chip_carried = lax.all_to_all(carried, "seq", 0, 0, axis_index_groups=chips)
     mine, send = call(
         spread_kernel,
@@ -303,33 +446,43 @@
         scalars=1,
     )
     theirs = partner(send, 1)
-    tokens_t, cotangent_t = call(turned_kernel, [shaped(2048, 512)] * 2, gathered)
-    results, keep, send = call(
+    halves = [shaped(8, 2, 64, 512)] * 2
+    (results,) = call(
         outputs_kernel,
-        [shaped(4 * T, 512), shaped(2, 8, 2, 64, 512), shaped(2, 8, 2, 64, 512)],
+        [shaped(4 * T, 512)],
         core,
         local,
         readers,
         mine,
         theirs,
-        tokens_t,
-        cotangent_t,
         scalars=1,
     )
-    recv = partner(send, 1)
+    keep_in, send_in = call(gradient_in_kernel, halves, core, results, tokens_t, scalars=1)
+    keep_out, send_out = call(gradient_out_kernel, halves, core, results, cotangent_t, scalars=1)
+    line, x_lo = (chip % 8).reshape(1), x_lo.reshape(1)
+    stay_in, left, right = z_first(line, keep_in, partner(send_in, 1))
+    stay_out, left_out, right_out = z_first(line, keep_out, partner(send_out, 1))
+    if ORDER == 0:
+        results, left, right = lax.optimization_barrier((results, left, right))
+    elif ORDER == 1:
+        results, left, right, left_out, right_out = lax.optimization_barrier(
+            (results, left, right, left_out, right_out)
+        )
     (partials,) = call(
-        partials_kernel, [shaped(8, 2 * T, 256)], results, weight_in, in_rev, weight_out, out_rev
-    )
-    chip_sum = keep.astype(F32) + recv.astype(F32)
-    away = lax.dynamic_index_in_dim(chip_sum, 1 - x_lo, 0, keepdims=False).astype(BF16)
-    stay = lax.dynamic_index_in_dim(chip_sum, x_lo, 0, keepdims=False)
-    arrived = partner(away, 16)
+        partials_kernel,
+        [shaped(8, 2 * T, 256)],
+        results,
+        weight_in,
+        weight_out,
+        far_outs=(0,),
+        scratch=[VMEM((8, 2 * T, 256), BF16), dma(8)],
+        extra=2,
+    )
     shares = lax.all_to_all(partials, "head", 0, 0)
-    sums = jnp.sum(shares.astype(F32), axis=0).astype(BF16)
-    line_sum = (stay + arrived.astype(F32)).astype(BF16)
-    pieces = lax.all_to_all(line_sum, "seq", 0, 0, axis_index_groups=lines)
-    gradients = jnp.sum(pieces.astype(F32), axis=0)
-    return sums[:T], sums[T:], gradients[0], gradients[1]
+    gradient_in = z_next(line, x_lo, stay_in, left, right)
+    gradient_out = z_next(line, x_lo, stay_out, left_out, right_out)
+    mixed, gradient_tokens = call(shares_kernel, [shaped(T, 256)] * 2, shares)
+    return mixed, gradient_tokens, gradient_in, gradient_out
 
 
 def solution(mesh):

time: 204 us -> 158 us (0.77); the launches traced: 201 us -> 157 us
  waiting for transfers between devices: 96.5 us -> 40.7 us
  starting transfers between devices: 28.8 us -> 48.9 us
  other arithmetic: 8.43 us -> 1.34 us
  blocking collectives: 14.5 us -> 17.9 us
  Pallas kernels: 33.4 us -> 30.1 us
    all_to_all x2 -> x0, waiting for transfers between devices: 42.8 us -> none  [the longest x1 25.4 us: shards(): pieces = lax.all_to_all(line_sum, 'seq', 0, 0, axis_index_groups=lines)]
    ppermute x5 -> x7, waiting for transfers between devices: 42 us -> 6.14 us  [partner(): return lax.ppermute(block, 'seq', [(i, i ^ bit) for i in range(count)])]
    ppermute x0 -> x19, waiting for transfers between devices: none -> 34.5 us  [the longest x10 21.4 us: along_line(): return lax.ppermute(block, 'seq', route)]
    ppermute x0 -> x19, starting transfers between devices: none -> 30.4 us  [the longest x10 18.9 us: along_line(): return lax.ppermute(block, 'seq', route)]
    all_to_all x1, waiting for transfers between devices: 11.7 us -> 0.01 us  [shards(): lax.all_to_all(chip_states, 'seq', 0, 0, axis_index_groups=chips)]
    all_to_all x2 -> x0, starting transfers between devices: 11.3 us -> none  [the longest x1 7.51 us: shards(): lax.all_to_all(jnp.broadcast_to(both, (8, 2 * T, 256)), 'head', 0, 0)]
    all_to_all x1, blocking collectives: 14.5 us -> 17.9 us  [shards(): chip_carried = lax.all_to_all(carried, 'seq', 0, 0, axis_index_groups=chips)]
    pallas_call x9 -> x17, Pallas kernels: 33.4 us -> 30.1 us  [call(): pl.pallas_call(kernel, out_shape=outs, in_specs=[pl.BlockSpec(memory_spac...]
  transfers between devices with their start and end apart: 9 -> 28, of which waited for: 5 -> 15; matrix products, arithmetic and copies ran while one was open for 4% -> 1% of each run, Pallas kernels for 7% -> 8%
where the time goes in v2:
time: 158 us; the launch traced here: 157 us
  starting transfers between devices  48.9 us (31%)
  waiting for transfers between devices  40.7 us (26%)
  Pallas kernels  30.1 us (19%)
  blocking collectives  17.9 us (11%)
  local copies, waits for them, and re-layouts  17.5 us (11%)
    pallas_call x17, Pallas kernels, call(): pl.pallas_call(kernel, out_shape=outs, in_specs=[pl.BlockSpec(memory_spac...  30.1 us
    ppermute x10, waiting for transfers between devices, along_line(): return lax.ppermute(block, 'seq', route)  21.4 us
    ppermute x10, starting transfers between devices, along_line(): return lax.ppermute(block, 'seq', route)  18.9 us
    all_to_all x1, blocking collectives, shards(): chip_carried = lax.all_to_all(carried, 'seq', 0, 0, axis_index_groups=chips)  17.9 us
    unnamed x64, local copies, waits for them, and re-layouts  16.5 us
    ppermute x9, waiting for transfers between devices, around(): return lax.ppermute(block, 'head', route)  13.1 us
    ppermute x9, starting transfers between devices, around(): return lax.ppermute(block, 'head', route)  11.5 us
    all_to_all x1, starting transfers between devices, shards(): lax.all_to_all(chip_states, 'seq', 0, 0, axis_index_groups=chips)  9.5 us
  transfers between devices with their start and end apart: 28, of which 15 were waited for; matrix products, arithmetic and copies ran while one was open for 1% of the time, Pallas kernels for 8%

profile of v2, /device:TPU:8, one launch (start us, length us, event | category | flops | bytes accessed | tf_op | source)
XLA Modules:
  0.0 157.4 jit_solution(17837430401378572246)
XLA Ops:
  2.5 3.1 %collective-permute-start = (bf16[512,256]{1,0:T(8,128)(2,1)S(1)}, bf16[512,256]{1,0:T(8,128)(2,1)S(1)}, u32[]{:S(2)}, u32[]{:S(2)}) collective-permute-start(bf16[512,256]{1,0:T(8,128)(2,1)S(1)} %constant_dynamic-update-slice_fusion.refs_0_), channel_id=1, source_target_pairs={{0,1},{1,0},{2,3},{3,2},{4,5},{5,4},{6,7},{7,6},{8,9},{9,8},{10,11... | collective-permute-start | bytes 786440 | tf_op jit(solution)/shard_map/ppermute | solution.py:342
  7.6 4.5 %collective-permute-done.refs_1_ = bf16[512,256]{1,0:T(8,128)(2,1)S(1)} collective-permute-done((bf16[512,256]{1,0:T(8,128)(2,1)S(1)}, bf16[512,256]{1,0:T(8,128)(2,1)S(1)}, u32[]{:S(2)}, u32[]{:S(2)}) %collective-permute-start) | collective-permute-done | bytes 262176 | tf_op jit(solution)/shard_map/ppermute | solution.py:342
  16.4 5.0 %collective-permute-done.2.refs_3_ = bf16[512,256]{1,0:T(8,128)(2,1)S(1)} collective-permute-done((bf16[512,256]{1,0:T(8,128)(2,1)S(1)}, bf16[512,256]{1,0:T(8,128)(2,1)S(1)}, u32[]{:S(2)}, u32[]{:S(2)}) %collective-permute-start.2) | collective-permute-done | bytes 262176 | tf_op jit(solution)/shard_map/ppermute | solution.py:342
  26.4 1.7 %collective-permute-done.8.refs_9_ = bf16[256,256]{1,0:T(8,128)(2,1)S(1)} collective-permute-done((bf16[256,256]{1,0:T(8,128)(2,1)S(1)}, bf16[256,256]{1,0:T(8,128)(2,1)S(1)}, u32[]{:S(2)}, u32[]{:S(2)}) %collective-permute-start.8) | collective-permute-done | bytes 131104 | tf_op jit(solution)/shard_map/ppermute | solution.py:342
  30.6 12.1 %shard_map.111 = (bf16[4,256,512]{2,1,0:T(8,128)(2,1)}, bf16[4,4,256,128]{3,2,1,0:T(8,128)(2,1)}, bf16[8,128,128]{2,1,0:T(8,128)(2,1)S(1)}, bf16[8,128,128]{2,1,0:T(8,128)(2,1)}) custom-call(s32[1]{0:T(128)} %bitcast.core, f32[4]{0:T(128)S(1)} %copy-done.30, s32[8]{0:T(128)S(1)} %stack.35.places, bf16[512,256]{1,0:T(8,128)(2,1)} %copy-done.12, ...), custom_call_target="tpu_custom_call" | custom-call | tf_op jit(solution)/shard_map/pallas_call | solution.py:37
  45.7 9.5 %all-to-all-start = ((bf16[16,80,128]{2,1,0:T(8,128)(2,1)}), bf16[16,80,128]{2,1,0:T(8,128)(2,1)S(1)}, u32[]{:S(2)}, u32[]{:S(2)}) async-start(bf16[16,80,128]{2,1,0:T(8,128)(2,1)} %shard_map.113), calls=%async_computation | async-start | bytes 655360 | tf_op jit(solution)/shard_map/all_to_all | solution.py:432
  63.7 1.8 %shard_map.115 = (bf16[2048,512]{1,0:T(8,128)(2,1)S(1)}, bf16[2048,512]{1,0:T(8,128)(2,1)S(1)}) custom-call(s32[8]{0:T(128)S(1)} %stack.35.places, bf16[512,256]{1,0:T(8,128)(2,1)S(1)} %copy-done.13, bf16[512,256]{1,0:T(8,128)(2,1)S(1)} %copy-done.15, bf16[512,256]{1,0:T(8,128)(2,1)S(1)} %copy-done.5, bf16[512,256]{1,0:T(8,128)(2,1)S(1)} %copy-done.9, ...), custom_call_target="tpu_custom_call" | custom-call | tf_op jit(solution)/shard_map/pallas_call | solution.py:37
  67.1 17.9 %all_to_all.15.chip = bf16[16,64,128]{2,1,0:T(8,128)(2,1)S(1)} all-to-all(bf16[16,64,128]{2,1,0:T(8,128)(2,1)S(1)} %shard_map.114), channel_id=1, replica_groups={{0,16,32,48,64,80,96,112,128,144,160,176,192,208,224,240},{8,24,40,56,7..., dimensions={0} | all-to-all | bytes 524288 | tf_op jit(solution)/shard_map/all_to_all | solution.py:436
  88.5 2.3 %shard_map.124 = (bf16[8,2,64,512]{3,2,1,0:T(8,128)(2,1)S(1)}, bf16[8,2,64,512]{3,2,1,0:T(8,128)(2,1)}) custom-call(s32[1]{0:T(128)} %bitcast.core, bf16[1024,512]{1,0:T(8,128)(2,1)S(1)} %shard_map.117.results, bf16[2048,512]{1,0:T(8,128)(2,1)S(1)} %copy-done.3), custom_call_target="tpu_custom_call" | custom-call | tf_op jit(solution)/shard_map/pallas_call | solution.py:37
  90.9 2.2 %shard_map.120 = (bf16[8,2,64,512]{3,2,1,0:T(8,128)(2,1)S(1)}, bf16[8,2,64,512]{3,2,1,0:T(8,128)(2,1)}) custom-call(s32[1]{0:T(128)} %bitcast.core, bf16[1024,512]{1,0:T(8,128)(2,1)S(1)} %shard_map.117.results, bf16[2048,512]{1,0:T(8,128)(2,1)S(1)} %get-tuple-element.50.left), custom_call_target="tpu_custom_call" | custom-call | tf_op jit(solution)/shard_map/pallas_call | solution.py:37
  93.6 4.8 %shard_map.118 = bf16[8,512,256]{2,1,0:T(8,128)(2,1)} custom-call(bf16[1024,512]{1,0:T(8,128)(2,1)S(1)} %shard_map.117.results, bf16[2048,512]{1,0:T(8,128)(2,1)S(1)} %copy-done, bf16[2048,512]{1,0:T(8,128)(2,1)S(1)} %copy-done.1), custom_call_target="tpu_custom_call" | custom-call | tf_op jit(solution)/shard_map/pallas_call | solution.py:37
  98.4 7.4 %all-to-all-start.2 = ((bf16[8,512,256]{2,1,0:T(8,128)(2,1)}), bf16[8,512,256]{2,1,0:T(8,128)(2,1)S(1)}, u32[]{:S(2)}, u32[]{:S(2)}) async-start(bf16[8,512,256]{2,1,0:T(8,128)(2,1)} %shard_map.118), calls=%async_computation.2 | async-start | bytes 4194304 | tf_op jit(solution)/shard_map/all_to_all | solution.py:481
  108.5 2.1 %collective-permute-start.20 = (bf16[4,64,512]{2,1,0:T(8,128)(2,1)S(1)}, bf16[4,64,512]{2,1,0:T(8,128)(2,1)S(1)}, u32[]{:S(2)}, u32[]{:S(2)}) collective-permute-start(bf16[4,64,512]{2,1,0:T(8,128)(2,1)S(1)} %get-tuple-element.66), channel_id=1, source_target_pairs={{0,16},{8,24},{16,0},{24,8},{32,48},{40,56},{48,32},{56,40},{64,80... | collective-permute-start | bytes 786440 | tf_op jit(solution)/shard_map/ppermute | solution.py:335
  113.9 1.8 %collective-permute-start.14 = (bf16[4,64,512]{2,1,0:T(8,128)(2,1)S(1)}, bf16[4,64,512]{2,1,0:T(8,128)(2,1)S(1)}, u32[]{:S(2)}, u32[]{:S(2)}) collective-permute-start(bf16[4,64,512]{2,1,0:T(8,128)(2,1)S(1)} %get-tuple-element.55), channel_id=1, source_target_pairs={{0,112},{8,120},{16,32},{24,40},{32,16},{40,24},{48,64},{56,72},{6... | collective-permute-start | bytes 786440 | tf_op jit(solution)/shard_map/ppermute | solution.py:335
  115.7 2.1 %collective-permute-done.20.left = bf16[4,64,512]{2,1,0:T(8,128)(2,1)S(1)} collective-permute-done((bf16[4,64,512]{2,1,0:T(8,128)(2,1)S(1)}, bf16[4,64,512]{2,1,0:T(8,128)(2,1)S(1)}, u32[]{:S(2)}, u32[]{:S(2)}) %collective-permute-start.20) | collective-permute-done | bytes 262176 | tf_op jit(solution)/shard_map/ppermute | solution.py:335
  117.7 3.3 %collective-permute-done.21.right = bf16[4,64,512]{2,1,0:T(8,128)(2,1)S(1)} collective-permute-done((bf16[4,64,512]{2,1,0:T(8,128)(2,1)S(1)}, bf16[4,64,512]{2,1,0:T(8,128)(2,1)S(1)}, u32[]{:S(2)}, u32[]{:S(2)}) %collective-permute-start.21) | collective-permute-done | bytes 262176 | tf_op jit(solution)/shard_map/ppermute | solution.py:335
  121.2 2.5 %collective-permute-start.23 = (bf16[2,64,512]{2,1,0:T(8,128)(2,1)S(1)}, bf16[2,64,512]{2,1,0:T(8,128)(2,1)S(1)}, u32[]{:S(2)}, u32[]{:S(2)}) collective-permute-start(bf16[2,64,512]{2,1,0:T(8,128)(2,1)S(1)} %get-tuple-element.70), channel_id=1, source_target_pairs={{0,64},{8,72},{16,80},{24,88},{32,96},{40,104},{48,112},{56,120},{... | collective-permute-start | bytes 393224 | tf_op jit(solution)/shard_map/ppermute | solution.py:335
  123.8 4.0 %collective-permute-start.24 = (bf16[2,64,512]{2,1,0:T(8,128)(2,1)S(1)}, bf16[2,64,512]{2,1,0:T(8,128)(2,1)S(1)}, u32[]{:S(2)}, u32[]{:S(2)}) collective-permute-start(bf16[2,64,512]{2,1,0:T(8,128)(2,1)S(1)} %get-tuple-element.71), channel_id=1, source_target_pairs={{0,96},{8,104},{16,112},{24,120},{32,0},{40,8},{48,16},{56,24},{64... | collective-permute-start | bytes 393224 | tf_op jit(solution)/shard_map/ppermute | solution.py:335
  127.8 11.5 %collective-permute-done.14.right = bf16[4,64,512]{2,1,0:T(8,128)(2,1)S(1)} collective-permute-done((bf16[4,64,512]{2,1,0:T(8,128)(2,1)S(1)}, bf16[4,64,512]{2,1,0:T(8,128)(2,1)S(1)}, u32[]{:S(2)}, u32[]{:S(2)}) %collective-permute-start.14) | collective-permute-done | bytes 262176 | tf_op jit(solution)/shard_map/ppermute | solution.py:335
  140.0 2.4 %collective-permute-start.16 = (bf16[2,64,512]{2,1,0:T(8,128)(2,1)}, bf16[2,64,512]{2,1,0:T(8,128)(2,1)S(1)}, u32[]{:S(2)}, u32[]{:S(2)}) collective-permute-start(bf16[2,64,512]{2,1,0:T(8,128)(2,1)} %get-tuple-element.58), channel_id=1, source_target_pairs={{0,64},{8,72},{16,80},{24,88},{32,96},{40,104},{48,112},{56,120},{... | collective-permute-start | bytes 393224 | tf_op jit(solution)/shard_map/ppermute | solution.py:335
  142.4 4.1 %collective-permute-start.17 = (bf16[2,64,512]{2,1,0:T(8,128)(2,1)S(1)}, bf16[2,64,512]{2,1,0:T(8,128)(2,1)S(1)}, u32[]{:S(2)}, u32[]{:S(2)}) collective-permute-start(bf16[2,64,512]{2,1,0:T(8,128)(2,1)S(1)} %get-tuple-element.59), channel_id=1, source_target_pairs={{0,96},{8,104},{16,112},{24,120},{32,0},{40,8},{48,16},{56,24},{64... | collective-permute-start | bytes 393224 | tf_op jit(solution)/shard_map/ppermute | solution.py:335
  147.3 1.9 %collective-permute-done.16.c = bf16[2,64,512]{2,1,0:T(8,128)(2,1)S(1)} collective-permute-done((bf16[2,64,512]{2,1,0:T(8,128)(2,1)}, bf16[2,64,512]{2,1,0:T(8,128)(2,1)S(1)}, u32[]{:S(2)}, u32[]{:S(2)}) %collective-permute-start.16) | collective-permute-done | bytes 131104 | tf_op jit(solution)/shard_map/ppermute | solution.py:335
  149.2 2.1 %collective-permute-done.17.d = bf16[2,64,512]{2,1,0:T(8,128)(2,1)S(1)} collective-permute-done((bf16[2,64,512]{2,1,0:T(8,128)(2,1)S(1)}, bf16[2,64,512]{2,1,0:T(8,128)(2,1)S(1)}, u32[]{:S(2)}, u32[]{:S(2)}) %collective-permute-start.17) | collective-permute-done | bytes 131104 | tf_op jit(solution)/shard_map/ppermute | solution.py:335
  152.2 3.6 %collective-permute-done.18 = bf16[64,512]{1,0:T(8,128)(2,1)S(1)} collective-permute-done((bf16[64,512]{1,0:T(8,128)(2,1)S(1)}, bf16[64,512]{1,0:T(8,128)(2,1)S(1)}, u32[]{:S(2)}, u32[]{:S(2)}) %collective-permute-start.18) | collective-permute-done | bytes 65568 | tf_op jit(solution)/shard_map/ppermute | solution.py:327
  (122 shorter events, 42.6 us)
Async XLA Ops:
  2.5 9.6 %collective-permute-start = (bf16[512,256]{1,0:T(8,128)(2,1)S(1)}, bf16[512,256]{1,0:T(8,128)(2,1)S(1)}, u32[]{:S(2)}, u32[]{:S(2)}) collective-permute-start(bf16[512,256]{1,0:T(8,128)(2,1)S(1)} %constant_dynamic-update-slice_fusion.refs_0_), channel_id=1, source_target_pairs={{0,1},{1,0},{2,3},{3,2},{4,5},{5,4},{6,7},{7,6},{8,9},{9,8},{10,11... | collective-permute-start | bytes 786440 | tf_op jit(solution)/shard_map/ppermute | solution.py:342
  5.6 8.6 %collective-permute-start.1 = (bf16[512,256]{1,0:T(8,128)(2,1)S(1)}, bf16[512,256]{1,0:T(8,128)(2,1)S(1)}, u32[]{:S(2)}, u32[]{:S(2)}) collective-permute-start(bf16[512,256]{1,0:T(8,128)(2,1)S(1)} %constant_dynamic-update-slice_fusion.refs_0_), channel_id=1, source_target_pairs={{0,2},{1,3},{2,4},{3,5},{4,6},{5,7},{6,0},{7,1},{8,10},{9,11},{10,... | collective-permute-start | bytes 786440 | tf_op jit(solution)/shard_map/ppermute | solution.py:342
  7.2 8.7 %collective-permute-start.3 = (bf16[512,256]{1,0:T(8,128)(2,1)S(1)}, bf16[512,256]{1,0:T(8,128)(2,1)S(1)}, u32[]{:S(2)}, u32[]{:S(2)}) collective-permute-start(bf16[512,256]{1,0:T(8,128)(2,1)S(1)} %constant_dynamic-update-slice_fusion.refs_0_), channel_id=1, source_target_pairs={{0,6},{1,7},{2,0},{3,1},{4,2},{5,3},{6,4},{7,5},{8,14},{9,15},{10,... | collective-permute-start | bytes 786440 | tf_op jit(solution)/shard_map/ppermute | solution.py:342
  12.1 9.2 %collective-permute-start.2 = (bf16[512,256]{1,0:T(8,128)(2,1)S(1)}, bf16[512,256]{1,0:T(8,128)(2,1)S(1)}, u32[]{:S(2)}, u32[]{:S(2)}) collective-permute-start(bf16[512,256]{1,0:T(8,128)(2,1)S(1)} %collective-permute-done.refs_1_), channel_id=1, source_target_pairs={{0,2},{1,3},{2,4},{3,5},{4,6},{5,7},{6,0},{7,1},{8,10},{9,11},{10,... | collective-permute-start | bytes 786440 | tf_op jit(solution)/shard_map/ppermute | solution.py:342
  13.7 9.3 %collective-permute-start.4 = (bf16[512,256]{1,0:T(8,128)(2,1)S(1)}, bf16[512,256]{1,0:T(8,128)(2,1)S(1)}, u32[]{:S(2)}, u32[]{:S(2)}) collective-permute-start(bf16[512,256]{1,0:T(8,128)(2,1)S(1)} %collective-permute-done.refs_1_), channel_id=1, source_target_pairs={{0,6},{1,7},{2,0},{3,1},{4,2},{5,3},{6,4},{7,5},{8,14},{9,15},{10,... | collective-permute-start | bytes 786440 | tf_op jit(solution)/shard_map/ppermute | solution.py:342
  14.2 10.4 %collective-permute-start.5 = (bf16[256,256]{1,0:T(8,128)(2,1)S(1)}, bf16[256,256]{1,0:T(8,128)(2,1)S(1)}, u32[]{:S(2)}, u32[]{:S(2)}) collective-permute-start(bf16[256,256]{1,0:T(8,128)(2,1)S(1)} %slice.16), channel_id=1, source_target_pairs={{0,2},{1,3},{2,4},{3,5},{4,6},{5,7},{6,0},{7,1},{8,10},{9,11},{10,... | collective-permute-start | bytes 393224 | tf_op jit(solution)/shard_map/ppermute | solution.py:342
  15.8 9.0 %collective-permute-start.6 = (bf16[256,256]{1,0:T(8,128)(2,1)S(1)}, bf16[256,256]{1,0:T(8,128)(2,1)S(1)}, u32[]{:S(2)}, u32[]{:S(2)}) collective-permute-start(bf16[256,256]{1,0:T(8,128)(2,1)S(1)} %slice.17), channel_id=1, source_target_pairs={{0,6},{1,7},{2,0},{3,1},{4,2},{5,3},{6,4},{7,5},{8,14},{9,15},{10,... | collective-permute-start | bytes 393224 | tf_op jit(solution)/shard_map/ppermute | solution.py:342
  21.4 5.0 %collective-permute-start.7 = (bf16[256,256]{1,0:T(8,128)(2,1)S(1)}, bf16[256,256]{1,0:T(8,128)(2,1)S(1)}, u32[]{:S(2)}, u32[]{:S(2)}) collective-permute-start(bf16[256,256]{1,0:T(8,128)(2,1)S(1)} %slice.18), channel_id=1, source_target_pairs={{0,2},{1,3},{2,4},{3,5},{4,6},{5,7},{6,0},{7,1},{8,10},{9,11},{10,... | collective-permute-start | bytes 393224 | tf_op jit(solution)/shard_map/ppermute | solution.py:342
  23.0 5.0 %collective-permute-start.8 = (bf16[256,256]{1,0:T(8,128)(2,1)S(1)}, bf16[256,256]{1,0:T(8,128)(2,1)S(1)}, u32[]{:S(2)}, u32[]{:S(2)}) collective-permute-start(bf16[256,256]{1,0:T(8,128)(2,1)S(1)} %slice.19), channel_id=1, source_target_pairs={{0,6},{1,7},{2,0},{3,1},{4,2},{5,3},{6,4},{7,5},{8,14},{9,15},{10,... | collective-permute-start | bytes 393224 | tf_op jit(solution)/shard_map/ppermute | solution.py:342
  45.7 21.2 %all-to-all-start = ((bf16[16,80,128]{2,1,0:T(8,128)(2,1)}), bf16[16,80,128]{2,1,0:T(8,128)(2,1)S(1)}, u32[]{:S(2)}, u32[]{:S(2)}) async-start(bf16[16,80,128]{2,1,0:T(8,128)(2,1)} %shard_map.113), calls=%async_computation | async-start | bytes 655360 | tf_op jit(solution)/shard_map/all_to_all | solution.py:432
  90.8 15.0 %collective-permute-start.19 = (bf16[8,2,64,512]{3,2,1,0:T(8,128)(2,1)}, bf16[8,2,64,512]{3,2,1,0:T(8,128)(2,1)}, u32[]{:S(2)}, u32[]{:S(2)}) collective-permute-start(bf16[8,2,64,512]{3,2,1,0:T(8,128)(2,1)} %get-tuple-element.64), channel_id=1, source_target_pairs={{0,8},{8,0},{16,24},{24,16},{32,40},{40,32},{48,56},{56,48},{64,72... | collective-permute-start | bytes 3145736 | tf_op jit(solution)/shard_map/ppermute | solution.py:327
  93.2 18.5 %collective-permute-start.12 = (bf16[8,2,64,512]{3,2,1,0:T(8,128)(2,1)}, bf16[8,2,64,512]{3,2,1,0:T(8,128)(2,1)}, u32[]{:S(2)}, u32[]{:S(2)}) collective-permute-start(bf16[8,2,64,512]{3,2,1,0:T(8,128)(2,1)} %get-tuple-element.52), channel_id=1, source_target_pairs={{0,8},{8,0},{16,24},{24,16},{32,40},{40,32},{48,56},{56,48},{64,72... | collective-permute-start | bytes 3145736 | tf_op jit(solution)/shard_map/ppermute | solution.py:327
  98.4 58.0 %all-to-all-start.2 = ((bf16[8,512,256]{2,1,0:T(8,128)(2,1)}), bf16[8,512,256]{2,1,0:T(8,128)(2,1)S(1)}, u32[]{:S(2)}, u32[]{:S(2)}) async-start(bf16[8,512,256]{2,1,0:T(8,128)(2,1)} %shard_map.118), calls=%async_computation.2 | async-start | bytes 4194304 | tf_op jit(solution)/shard_map/all_to_all | solution.py:481
  108.5 9.3 %collective-permute-start.20 = (bf16[4,64,512]{2,1,0:T(8,128)(2,1)S(1)}, bf16[4,64,512]{2,1,0:T(8,128)(2,1)S(1)}, u32[]{:S(2)}, u32[]{:S(2)}) collective-permute-start(bf16[4,64,512]{2,1,0:T(8,128)(2,1)S(1)} %get-tuple-element.66), channel_id=1, source_target_pairs={{0,16},{8,24},{16,0},{24,8},{32,48},{40,56},{48,32},{56,40},{64,80... | collective-permute-start | bytes 786440 | tf_op jit(solution)/shard_map/ppermute | solution.py:335
  110.6 10.5 %collective-permute-start.21 = (bf16[4,64,512]{2,1,0:T(8,128)(2,1)S(1)}, bf16[4,64,512]{2,1,0:T(8,128)(2,1)S(1)}, u32[]{:S(2)}, u32[]{:S(2)}) collective-permute-start(bf16[4,64,512]{2,1,0:T(8,128)(2,1)S(1)} %get-tuple-element.67), channel_id=1, source_target_pairs={{0,112},{8,120},{16,32},{24,40},{32,16},{40,24},{48,64},{56,72},{6... | collective-permute-start | bytes 786440 | tf_op jit(solution)/shard_map/ppermute | solution.py:335
  113.1 14.6 %collective-permute-start.13 = (bf16[4,64,512]{2,1,0:T(8,128)(2,1)S(1)}, bf16[4,64,512]{2,1,0:T(8,128)(2,1)S(1)}, u32[]{:S(2)}, u32[]{:S(2)}) collective-permute-start(bf16[4,64,512]{2,1,0:T(8,128)(2,1)S(1)} %get-tuple-element.54), channel_id=1, source_target_pairs={{0,16},{8,24},{16,0},{24,8},{32,48},{40,56},{48,32},{56,40},{64,80... | collective-permute-start | bytes 786440 | tf_op jit(solution)/shard_map/ppermute | solution.py:335
  113.9 25.4 %collective-permute-start.14 = (bf16[4,64,512]{2,1,0:T(8,128)(2,1)S(1)}, bf16[4,64,512]{2,1,0:T(8,128)(2,1)S(1)}, u32[]{:S(2)}, u32[]{:S(2)}) collective-permute-start(bf16[4,64,512]{2,1,0:T(8,128)(2,1)S(1)} %get-tuple-element.55), channel_id=1, source_target_pairs={{0,112},{8,120},{16,32},{24,40},{32,16},{40,24},{48,64},{56,72},{6... | collective-permute-start | bytes 786440 | tf_op jit(solution)/shard_map/ppermute | solution.py:335
  121.1 21.3 %collective-permute-start.22 = (bf16[2,64,512]{2,1,0:T(8,128)(2,1)S(1)}, bf16[2,64,512]{2,1,0:T(8,128)(2,1)S(1)}, u32[]{:S(2)}, u32[]{:S(2)}) collective-permute-start(bf16[2,64,512]{2,1,0:T(8,128)(2,1)S(1)} %get-tuple-element.69), channel_id=1, source_target_pairs={{0,32},{8,40},{16,48},{24,56},{32,64},{40,72},{48,80},{56,88},{64,... | collective-permute-start | bytes 393224 | tf_op jit(solution)/shard_map/ppermute | solution.py:335
  121.2 25.3 %collective-permute-start.23 = (bf16[2,64,512]{2,1,0:T(8,128)(2,1)S(1)}, bf16[2,64,512]{2,1,0:T(8,128)(2,1)S(1)}, u32[]{:S(2)}, u32[]{:S(2)}) collective-permute-start(bf16[2,64,512]{2,1,0:T(8,128)(2,1)S(1)} %get-tuple-element.70), channel_id=1, source_target_pairs={{0,64},{8,72},{16,80},{24,88},{32,96},{40,104},{48,112},{56,120},{... | collective-permute-start | bytes 393224 | tf_op jit(solution)/shard_map/ppermute | solution.py:335
  123.8 22.8 %collective-permute-start.24 = (bf16[2,64,512]{2,1,0:T(8,128)(2,1)S(1)}, bf16[2,64,512]{2,1,0:T(8,128)(2,1)S(1)}, u32[]{:S(2)}, u32[]{:S(2)}) collective-permute-start(bf16[2,64,512]{2,1,0:T(8,128)(2,1)S(1)} %get-tuple-element.71), channel_id=1, source_target_pairs={{0,96},{8,104},{16,112},{24,120},{32,0},{40,8},{48,16},{56,24},{64... | collective-permute-start | bytes 393224 | tf_op jit(solution)/shard_map/ppermute | solution.py:335
  140.0 7.3 %collective-permute-start.15 = (bf16[2,64,512]{2,1,0:T(8,128)(2,1)}, bf16[2,64,512]{2,1,0:T(8,128)(2,1)S(1)}, u32[]{:S(2)}, u32[]{:S(2)}) collective-permute-start(bf16[2,64,512]{2,1,0:T(8,128)(2,1)} %get-tuple-element.57), channel_id=1, source_target_pairs={{0,32},{8,40},{16,48},{24,56},{32,64},{40,72},{48,80},{56,88},{64,... | collective-permute-start | bytes 393224 | tf_op jit(solution)/shard_map/ppermute | solution.py:335
  140.0 9.2 %collective-permute-start.16 = (bf16[2,64,512]{2,1,0:T(8,128)(2,1)}, bf16[2,64,512]{2,1,0:T(8,128)(2,1)S(1)}, u32[]{:S(2)}, u32[]{:S(2)}) collective-permute-start(bf16[2,64,512]{2,1,0:T(8,128)(2,1)} %get-tuple-element.58), channel_id=1, source_target_pairs={{0,64},{8,72},{16,80},{24,88},{32,96},{40,104},{48,112},{56,120},{... | collective-permute-start | bytes 393224 | tf_op jit(solution)/shard_map/ppermute | solution.py:335
  142.4 8.9 %collective-permute-start.17 = (bf16[2,64,512]{2,1,0:T(8,128)(2,1)S(1)}, bf16[2,64,512]{2,1,0:T(8,128)(2,1)S(1)}, u32[]{:S(2)}, u32[]{:S(2)}) collective-permute-start(bf16[2,64,512]{2,1,0:T(8,128)(2,1)S(1)} %get-tuple-element.59), channel_id=1, source_target_pairs={{0,96},{8,104},{16,112},{24,120},{32,0},{40,8},{48,16},{56,24},{64... | collective-permute-start | bytes 393224 | tf_op jit(solution)/shard_map/ppermute | solution.py:335
  146.6 4.9 %collective-permute-start.25 = (bf16[64,512]{1,0:T(8,128)(2,1)S(1)}, bf16[64,512]{1,0:T(8,128)(2,1)S(1)}, u32[]{:S(2)}, u32[]{:S(2)}) collective-permute-start(bf16[64,512]{1,0:T(8,128)(2,1)S(1)} %get-tuple-element.73), channel_id=1, source_target_pairs={{0,128},{8,136},{16,144},{24,152},{32,160},{40,168},{48,176},{56,1... | collective-permute-start | bytes 196616 | tf_op jit(solution)/shard_map/ppermute | solution.py:327
  (35 other events, 220.1 us)

commit v3 on v2

--- a/solution.py
+++ b/solution.py
@@ -7,10 +7,13 @@
 
 F32 = jnp.float32
 BF16 = jnp.bfloat16
-ORDER = 2
+ORDER = 4
 SLACK = 2
-EARLY = False
+EARLY = True
 B_EXTRA = 42
+TURN_EXTRA = 42
+P_EXTRA = 42
+X_FIRST = True
 HEADS = 4
 N = 128
 T = 256
@@ -71,6 +74,11 @@
 def exchange(size):
     row, column = iotas(size, size)
     return (row + column == size - 1).astype(F32).astype(BF16)
+
+
+def both_kernel(tokens, cotangent, both):
+    both[:T, :] = tokens[...]
+    both[T:, :] = cotangent[...]
 
 
 def totals_kernel(decay, totals):
@@ -131,37 +139,54 @@
 def inside_kernel(core, skip, places, *refs):
     pieces, rest = refs[:10], refs[10:]
     keys, queries, decay, w_in, w_out, local, readers, own, send = rest[:9]
-    sides, turned, here, inner, writers, semaphores = rest[9:]
-    c = core[0]
+    sides, turned, weight, inner, readers_here, writers, local_here, semaphores = rest[9:]
+    here = core[0] == 0
     copies = Copies(semaphores)
-    waits = [copies.start(w_in, here.at[0]), copies.start(w_out, here.at[1])]
-    weights(keys, queries, decay, inner, readers, writers)
+    spots = []
+    for at in range(8):
+        spots.append(pl.ds(pl.multiple_of(places[at] * T, T), T))
+    loads = []
+    for at, ref in enumerate(pieces[:6]):
+        for g in range(2):
+            loads.append(copies.start(ref.at[pl.ds(T * g, T), :], sides.at[g, :, spots[at]]))
+    for at, ref in enumerate(pieces[6:]):
+        loads.append(copies.start(ref, sides.at[at % 2, :, spots[6 + at // 2]]))
+    waits = []
+    for g, source in enumerate((w_in, w_out)):
+        parts = [pl.ds(512 * part, 512) for part in range(4)]
+        waits.append([copies.start(source.at[at, :], weight.at[g, at, :]) for at in parts])
+    weights(keys, queries, decay, inner, readers_here, writers)
+    for copy in loads:
+        copy.wait()
+    stores = []
     flip = exchange(T)
-    for place, *parts in sides_of(places, pieces):
-        columns = pl.ds(pl.multiple_of(place * T, T), T)
-        mirrored = pl.ds(pl.multiple_of((7 - place) * T, T), T)
-        for g, part in enumerate(parts):
-            sides[g, :, columns] = part
-            turned[g, :, mirrored] = mm(part, flip).astype(BF16)
+    for g in range(2):
+        for j in range(8):
+            part = sides[g, :, T * j : T * (j + 1)]
+            turned[g, :, T * (7 - j) : T * (8 - j)] = mm(part, flip).astype(BF16)
     for k in range(4):
         if k % 2 == 0:
-            waits[k // 2].wait()
+            for copy in waits[k // 2]:
+                copy.wait()
+        if k == 2:
+            stores.append(copies.start(readers_here, readers))
         side = (sides, turned)[k % 2]
-        values = mm(side[k // 2], here[k // 2]).astype(BF16)
+        values = mm(side[k // 2], weight[k // 2]).astype(BF16)
+        states = []
         for h in range(HEADS):
             lanes = slice(N * h, N * (h + 1))
             v = values[:, lanes]
-            local[k, :, lanes] = (mm(inner[k, h], v) + skip[h] * v.astype(F32)).astype(BF16)
-            state = mm(writers[k, h], v).astype(BF16)
-            at = 2 * k + h % 2
-
-            @pl.when(c == h // 2)
-            def _():
-                own[at] = state
-
-            @pl.when(c != h // 2)
-            def _():
-                send[at] = state
+            local_here[k, :, lanes] = (
+                mm(inner[k, h], v) + skip[h] * v.astype(F32)
+            ).astype(BF16)
+            states.append(mm(writers[k, h], v))
+        for which in range(2):
+            low, high = states[which], states[2 + which]
+            own[2 * k + which] = jnp.where(here, low, high).astype(BF16)
+            send[2 * k + which] = jnp.where(here, high, low).astype(BF16)
+        stores.append(copies.start(local_here.at[k], local.at[k]))
+    for copy in stores:
+        copy.wait()
 
 
 def pair_of(c, own, recv, totals, other_totals, at):
@@ -270,34 +295,81 @@
     gradient(core[0] == 0, left, results[: 2 * T, :], keep, send)
 
 
-def partials_kernel(results, w_in, w_out, out, here, semaphores):
+def partials_kernel(results, w_in, w_out, out, weight, here, semaphores):
     copies = Copies(semaphores)
     flip = exchange(T)
+    pairs = [(j, 7 - j) for j in range(4)]
+    loads = []
+    for pair in pairs:
+        for j in pair:
+            for g, source in enumerate((w_out, w_in)):
+                loads.append(copies.start(source.at[pl.ds(T * j, T), :], weight.at[g, j]))
     stores = []
-    for j in range(8):
-        rows, mirrored = slice(T * j, T * (j + 1)), slice(T * (7 - j), T * (8 - j))
-        for g, weight in enumerate((w_out, w_in)):
-            first = results[2 * T * g : 2 * T * g + T, :]
-            second = results[2 * T * g + T : 2 * T * (g + 1), :]
-            turned = mm(flip, weight[mirrored, :]).astype(BF16)
-            here[j, T * g : T * (g + 1), :] = (
-                mm_nt(first, weight[rows, :]) + mm_nt(second, turned)
-            ).astype(BF16)
-        stores.append(copies.start(here.at[j], out.at[j]))
+    for at, pair in enumerate(pairs):
+        for copy in loads[4 * at : 4 * at + 4]:
+            copy.wait()
+        for j in pair:
+            for g in range(2):
+                first = results[2 * T * g : 2 * T * g + T, :]
+                second = results[2 * T * g + T : 2 * T * (g + 1), :]
+                turned = mm(flip, weight[g, 7 - j]).astype(BF16)
+                here[j, T * g : T * (g + 1), :] = (
+                    mm_nt(first, weight[g, j]) + mm_nt(second, turned)
+                ).astype(BF16)
+            stores.append(copies.start(here.at[j], out.at[j]))
     for copy in stores:
         copy.wait()
 
 
-def shares_kernel(shares, mixed, tokens):
+def half_sum_kernel(x_hi, shares, stay, away):
+    x = x_hi[0]
+    stay[...] = add(shares[0, x], shares[1, x]) + add(shares[2, x], shares[3, x])
+    away[...] = (
+        add(shares[0, 1 - x], shares[1, 1 - x]) + add(shares[2, 1 - x], shares[3, 1 - x])
+    ).astype(BF16)
+
+
+def whole_sum_kernel(stay, arrived, mixed, tokens):
     for g, out in enumerate((mixed, tokens)):
-        total = shares[0, T * g : T * (g + 1), :].astype(F32)
-        for j in range(1, 8):
-            total = total + shares[j, T * g : T * (g + 1), :].astype(F32)
-        out[...] = total.astype(BF16)
+        rows = slice(T * g, T * (g + 1))
+        out[...] = (stay[rows, :] + arrived[rows, :].astype(F32)).astype(BF16)
 
 
 def add(a, b):
     return a.astype(F32) + b.astype(F32)
+
+
+def split_x_kernel(x_lo, keep, recv, stay, away):
+    x = x_lo[0]
+    for z in range(8):
+        stay[z] = add(keep[z, x], recv[z, x]).astype(BF16)
+        away[z] = add(keep[z, 1 - x], recv[z, 1 - x]).astype(BF16)
+
+
+def split_second_kernel(place, keep, recv, stay, left, right):
+    parity = lax.rem(place[0], 2)
+    for i in range(4):
+        mine, other = 2 * i + parity, 2 * i + 1 - parity
+        stay[i] = add(keep[mine], recv[mine]).astype(BF16)
+        away = add(keep[other], recv[other]).astype(BF16)
+        left[i] = away[:32]
+        right[i] = away[32:]
+
+
+def quarter_second_kernel(place, stay, left, right, *outs):
+    for k in range(4):
+        at = lax.rem(lax.div(place[0], 2) + k, 4)
+        outs[k][:32] = add(stay[at, :32], left[at]).astype(BF16)
+        outs[k][32:] = add(stay[at, 32:], right[at]).astype(BF16)
+
+
+def last_sum_kernel(a, b, c, d, out):
+    out[...] = add(a[...], b[...]) + add(c[...], d[...])
+
+
+def partner(block, bit):
+    count = lax.axis_size("seq")
+    return lax.ppermute(block, "seq", [(i, i ^ bit) for i in range(count)])
 
 
 def split_first_kernel(place, keep, recv, stay, left, right):
@@ -350,8 +422,29 @@
     return ((z - 1) ^ 1) + 1
 
 
+def x_first(line, x_lo, keep, recv, parts):
+    stay, away = call(split_x_kernel, [shaped(8, 64, 512)] * 2, x_lo, keep, recv, scalars=1)
+    across = partner(away, 16)
+    if ORDER & 8:
+        across, *parts = lax.optimization_barrier((across, *parts))
+    first_parts = parts
+    stay, left, right = call(
+        split_second_kernel,
+        [shaped(4, 64, 512), shaped(4, 32, 512), shaped(4, 32, 512)],
+        line,
+        stay,
+        across,
+        scalars=1,
+    )
+    left, right = along_line(left, beside), along_line(right, otherwise)
+    parts = call(quarter_second_kernel, [shaped(64, 512)] * 4, line, stay, left, right, scalars=1)
+    parts = [parts[0]] + [along_line(parts[k], lambda z, k=k: z + 2 * k) for k in (1, 2, 3)]
+    (total,) = call(last_sum_kernel, [shaped(64, 512, dtype=F32)], *parts)
+    return total, first_parts
+
+
 def z_first(line, keep, recv):
-    stay, left, right = call(
+    return call(
         split_first_kernel,
         [shaped(4, 2, 64, 512), shaped(4, 64, 512), shaped(4, 64, 512)],
         line,
@@ -359,12 +452,14 @@
         recv,
         scalars=1,
     )
-    return stay, along_line(left, beside), along_line(right, otherwise)
-
-
-def z_next(line, x_lo, stay, left, right):
+
+
+def quarters(line, stay, left, right):
     parts = call(quarter_first_kernel, [shaped(2, 64, 512)] * 4, line, stay, left, right, scalars=1)
-    parts = [parts[0]] + [along_line(parts[k], lambda z, k=k: z + 2 * k) for k in (1, 2, 3)]
+    return [parts[0]] + [along_line(parts[k], lambda z, k=k: z + 2 * k) for k in (1, 2, 3)]
+
+
+def z_next(x_lo, parts):
     stay, away = call(
         line_sum_kernel, [shaped(64, 512, dtype=F32), shaped(64, 512)], x_lo, *parts, scalars=1
     )
@@ -388,7 +483,7 @@
     head = lax.axis_index("head")
     y, x_hi = head // 2, head % 2
     places = jnp.stack([2 * ((y + d) % 4) + (x_hi + f) % 2 for d in (0, 3, 1, 2) for f in (0, 1)])
-    both = jnp.concatenate([tokens, cotangent], axis=0)
+    (both,) = call(both_kernel, [shaped(2 * T, 256)], tokens, cotangent)
     across = around(both, 0, 1)
     left, right = around(both, 1, 0), around(both, -1, 0)
     (totals,) = call(totals_kernel, [shaped(8, N, dtype=F32)], log_decay)
@@ -414,14 +509,17 @@
         weight_in,
         weight_out,
         scalars=3,
-        far=(16, 17),
+        far=[*range(3, 13), 16, 17],
+        far_outs=(0, 1),
         scratch=[
             VMEM((2, T, 2048), BF16),
             VMEM((2, T, 2048), BF16),
             VMEM((2, 2048, 512), BF16),
             VMEM((4, HEADS, T, T), BF16),
+            VMEM((4, HEADS, T, N), BF16),
             VMEM((4, HEADS, N, T), BF16),
-            dma(2),
+            VMEM((4, T, 512), BF16),
+            dma(29),
         ],
         extra=B_EXTRA,
     )
@@ -431,7 +529,7 @@
     )
     spread_states = lax.all_to_all(chip_states, "seq", 0, 0, axis_index_groups=chips)
     (carried,) = call(carry_kernel, [shaped(16, 64, N)], upward, spread_states, scalars=1)
-    tokens_t, cotangent_t = call(turned_kernel, [shaped(2048, 512)] * 2, places, *pieces, scalars=1)
+    tokens_t, cotangent_t = call(turned_kernel, [shaped(2048, 512)] * 2, places, *pieces, scalars=1, extra=TURN_EXTRA)
     carried, tokens_t, cotangent_t = lax.optimization_barrier((carried, tokens_t, cotangent_t))
     chip_carried = lax.all_to_all(carried, "seq", 0, 0, axis_index_groups=chips)
     mine, send = call(
@@ -460,28 +558,42 @@
     keep_in, send_in = call(gradient_in_kernel, halves, core, results, tokens_t, scalars=1)
     keep_out, send_out = call(gradient_out_kernel, halves, core, results, cotangent_t, scalars=1)
     line, x_lo = (chip % 8).reshape(1), x_lo.reshape(1)
-    stay_in, left, right = z_first(line, keep_in, partner(send_in, 1))
-    stay_out, left_out, right_out = z_first(line, keep_out, partner(send_out, 1))
-    if ORDER == 0:
+    recv_in = partner(send_in, 1)
+    if ORDER & 1:
+        recv_in, keep_out = lax.optimization_barrier((recv_in, keep_out))
+    stay_in, left, right = z_first(line, keep_in, recv_in)
+    if ORDER & 2:
         results, left, right = lax.optimization_barrier((results, left, right))
-    elif ORDER == 1:
-        results, left, right, left_out, right_out = lax.optimization_barrier(
-            (results, left, right, left_out, right_out)
-        )
+    left, right = along_line(left, beside), along_line(right, otherwise)
+    if ORDER & 4:
+        keep_out, left, right = lax.optimization_barrier((keep_out, left, right))
     (partials,) = call(
         partials_kernel,
         [shaped(8, 2 * T, 256)],
         results,
         weight_in,
         weight_out,
+        far=(1, 2),
         far_outs=(0,),
-        scratch=[VMEM((8, 2 * T, 256), BF16), dma(8)],
-        extra=2,
-    )
-    shares = lax.all_to_all(partials, "head", 0, 0)
-    gradient_in = z_next(line, x_lo, stay_in, left, right)
-    gradient_out = z_next(line, x_lo, stay_out, left_out, right_out)
-    mixed, gradient_tokens = call(shares_kernel, [shaped(T, 256)] * 2, shares)
+        scratch=[VMEM((2, 8, T, 512), BF16), VMEM((8, 2 * T, 256), BF16), dma(24)],
+        extra=P_EXTRA,
+    )
+    columns = [[2 * i + x for i in range(4)] for x in range(2)]
+    partials = partials.reshape(4, 2, 2 * T, 256)
+    shares = lax.all_to_all(partials, "head", 0, 0, axis_index_groups=columns)
+    stay, away = call(
+        half_sum_kernel,
+        [shaped(2 * T, 256, dtype=F32), shaped(2 * T, 256)],
+        x_hi.reshape(1),
+        shares,
+        scalars=1,
+    )
+    mixed, gradient_tokens = call(
+        whole_sum_kernel, [shaped(T, 256)] * 2, stay, around(away, 0, 1)
+    )
+    parts = quarters(line, stay_in, left, right)
+    gradient_out, parts = x_first(line, x_lo, keep_out, partner(send_out, 1), parts)
+    gradient_in = z_next(x_lo, parts)
     return mixed, gradient_tokens, gradient_in, gradient_out
 
 

time: 158 us -> 148 us (0.937)
  local copies, waits for them, and re-layouts: 17.5 us -> 10.6 us
  waiting for transfers between devices: 40.7 us -> 35.8 us
  Pallas kernels: 30.1 us -> 32.3 us
  blocking collectives: 17.9 us -> 15.8 us
  starting transfers between devices: 48.9 us -> 50.9 us
    unnamed x64 -> x51, local copies, waits for them, and re-layouts: 16.5 us -> 10.5 us
    ppermute x10, waiting for transfers between devices: 21.4 us -> 15.8 us  [along_line(): return lax.ppermute(block, 'seq', route)]
    ppermute x9 -> x10, waiting for transfers between devices: 13.1 us -> 9.41 us  [around(): return lax.ppermute(block, 'head', route)]
    ppermute x9 -> x10, starting transfers between devices: 11.5 us -> 14.8 us  [around(): return lax.ppermute(block, 'head', route)]
    ppermute x7, waiting for transfers between devices: 6.14 us -> 8.58 us  [partner(): return lax.ppermute(block, 'seq', [(i, i ^ bit) for i in range(count)])]
    pallas_call x17 -> x20, Pallas kernels: 30.1 us -> 32.3 us  [call(): pl.pallas_call(kernel, out_shape=outs, in_specs=[pl.BlockSpec(memory_spac...]
    all_to_all x1, blocking collectives: 17.9 us -> 15.8 us  [shards(): chip_carried = lax.all_to_all(carried, 'seq', 0, 0, axis_index_groups=chips)]
    all_to_all x1, waiting for transfers between devices: 0.01 us -> 2.06 us  [shards(): lax.all_to_all(chip_states, 'seq', 0, 0, axis_index_groups=chips)]
  transfers between devices with their start and end apart: 28 -> 29, of which waited for: 15 -> 16; matrix products, arithmetic and copies ran while one was open for 1% -> 1% of each run, Pallas kernels for 8% -> 13%
where the time goes in v3:
time: 148 us; the launch traced here: 147 us
  starting transfers between devices  50.9 us (34%)
  waiting for transfers between devices  35.8 us (24%)
  Pallas kernels  32.3 us (22%)
  blocking collectives  15.8 us (11%)
  local copies, waits for them, and re-layouts  10.6 us (7%)
    pallas_call x20, Pallas kernels, call(): pl.pallas_call(kernel, out_shape=outs, in_specs=[pl.BlockSpec(memory_spac...  32.3 us
    ppermute x10, starting transfers between devices, along_line(): return lax.ppermute(block, 'seq', route)  17.4 us
    all_to_all x1, blocking collectives, shards(): chip_carried = lax.all_to_all(carried, 'seq', 0, 0, axis_index_groups=chips)  15.8 us
    ppermute x10, waiting for transfers between devices, along_line(): return lax.ppermute(block, 'seq', route)  15.8 us
    ppermute x10, starting transfers between devices, around(): return lax.ppermute(block, 'head', route)  14.8 us
    unnamed x51, local copies, waits for them, and re-layouts  10.5 us
    all_to_all x1, starting transfers between devices, shards(): lax.all_to_all(chip_states, 'seq', 0, 0, axis_index_groups=chips)  9.5 us
    ppermute x10, waiting for transfers between devices, around(): return lax.ppermute(block, 'head', route)  9.41 us
  transfers between devices with their start and end apart: 29, of which 16 were waited for; matrix products, arithmetic and copies ran while one was open for 1% of the time, Pallas kernels for 13%

profile of v3, /device:TPU:8, one launch (start us, length us, event | category | flops | bytes accessed | tf_op | source)
XLA Modules:
  0.0 147.0 jit_solution(1625644030617102229)
XLA Ops:
  2.5 3.1 %collective-permute-start = (bf16[512,256]{1,0:T(8,128)(2,1)S(1)}, bf16[512,256]{1,0:T(8,128)(2,1)S(1)}, u32[]{:S(2)}, u32[]{:S(2)}) collective-permute-start(bf16[512,256]{1,0:T(8,128)(2,1)S(1)} %shard_map.111.refs_0_), channel_id=1, source_target_pairs={{0,1},{1,0},{2,3},{3,2},{4,5},{5,4},{6,7},{7,6},{8,9},{9,8},{10,11... | collective-permute-start | bytes 786440 | tf_op jit(solution)/shard_map/ppermute | solution.py:414
  7.7 4.5 %collective-permute-done.refs_1_ = bf16[512,256]{1,0:T(8,128)(2,1)S(1)} collective-permute-done((bf16[512,256]{1,0:T(8,128)(2,1)S(1)}, bf16[512,256]{1,0:T(8,128)(2,1)S(1)}, u32[]{:S(2)}, u32[]{:S(2)}) %collective-permute-start) | collective-permute-done | bytes 262176 | tf_op jit(solution)/shard_map/ppermute | solution.py:414
  22.2 2.3 %collective-permute-done.7.refs_7_ = bf16[256,256]{1,0:T(8,128)(2,1)S(1)} collective-permute-done((bf16[256,256]{1,0:T(8,128)(2,1)S(1)}, bf16[256,256]{1,0:T(8,128)(2,1)S(1)}, u32[]{:S(2)}, u32[]{:S(2)}) %collective-permute-start.7) | collective-permute-done | bytes 131104 | tf_op jit(solution)/shard_map/ppermute | solution.py:414
  26.4 8.7 %shard_map.113 = (bf16[4,256,512]{2,1,0:T(8,128)(2,1)}, bf16[4,4,256,128]{3,2,1,0:T(8,128)(2,1)}, bf16[8,128,128]{2,1,0:T(8,128)(2,1)S(1)}, bf16[8,128,128]{2,1,0:T(8,128)(2,1)}) custom-call(s32[1]{0:T(128)} %bitcast.1.core, f32[4]{0:T(128)S(1)} %copy-done.24, s32[8]{0:T(128)S(1)} %stack.35.places, bf16[512,256]{1,0:T(8,128)(2,1)} %copy-done, ...), custom_call_target="tpu_custom_call" | custom-call | tf_op jit(solution)/shard_map/pallas_call | solution.py:40
  37.8 9.5 %all-to-all-start = ((bf16[16,80,128]{2,1,0:T(8,128)(2,1)}), bf16[16,80,128]{2,1,0:T(8,128)(2,1)S(1)}, u32[]{:S(2)}, u32[]{:S(2)}) async-start(bf16[16,80,128]{2,1,0:T(8,128)(2,1)} %shard_map.114), calls=%async_computation | async-start | bytes 655360 | tf_op jit(solution)/shard_map/all_to_all | solution.py:530
  53.1 3.8 %shard_map.116 = (bf16[2048,512]{1,0:T(8,128)(2,1)}, bf16[2048,512]{1,0:T(8,128)(2,1)}) custom-call(s32[8]{0:T(128)S(1)} %stack.35.places, bf16[512,256]{1,0:T(8,128)(2,1)S(1)} %copy-done.1, bf16[512,256]{1,0:T(8,128)(2,1)S(1)} %copy-done.13, bf16[512,256]{1,0:T(8,128)(2,1)S(1)} %copy-done.5, bf16[512,256]{1,0:T(8,128)(2,1)S(1)} %copy-done.9, ...), custom_call_target="tpu_custom_call" | custom-call | tf_op jit(solution)/shard_map/pallas_call | solution.py:40
  56.9 2.1 %all-to-all-done.states = bf16[16,80,128]{2,1,0:T(8,128)(2,1)S(1)} async-done(((bf16[16,80,128]{2,1,0:T(8,128)(2,1)}), bf16[16,80,128]{2,1,0:T(8,128)(2,1)S(1)}, u32[]{:S(2)}, u32[]{:S(2)}) %all-to-all-start) | async-done | bytes 327712 | tf_op jit(solution)/shard_map/all_to_all | solution.py:530
  59.2 15.8 %all_to_all.15.chip = bf16[16,64,128]{2,1,0:T(8,128)(2,1)S(1)} all-to-all(bf16[16,64,128]{2,1,0:T(8,128)(2,1)S(1)} %shard_map.115), channel_id=1, replica_groups={{0,16,32,48,64,80,96,112,128,144,160,176,192,208,224,240},{8,24,40,56,7..., dimensions={0} | all-to-all | bytes 524288 | tf_op jit(solution)/shard_map/all_to_all | solution.py:534
  77.3 2.3 %shard_map.122 = (bf16[8,2,64,512]{3,2,1,0:T(8,128)(2,1)S(1)}, bf16[8,2,64,512]{3,2,1,0:T(8,128)(2,1)}) custom-call(s32[1]{0:T(128)} %bitcast.1.core, bf16[1024,512]{1,0:T(8,128)(2,1)S(1)} %shard_map.118.results, bf16[2048,512]{1,0:T(8,128)(2,1)S(1)} %copy-done.3), custom_call_target="tpu_custom_call" | custom-call | tf_op jit(solution)/shard_map/pallas_call | solution.py:40
  79.7 2.2 %shard_map.124 = (bf16[8,2,64,512]{3,2,1,0:T(8,128)(2,1)S(1)}, bf16[8,2,64,512]{3,2,1,0:T(8,128)(2,1)}) custom-call(s32[1]{0:T(128)} %bitcast.1.core, bf16[1024,512]{1,0:T(8,128)(2,1)S(1)} %shard_map.118.results, bf16[2048,512]{1,0:T(8,128)(2,1)S(1)} %copy-done.2), custom_call_target="tpu_custom_call" | custom-call | tf_op jit(solution)/shard_map/pallas_call | solution.py:40
  82.4 6.6 %shard_map.119 = bf16[8,512,256]{2,1,0:T(8,128)(2,1)} custom-call(bf16[1024,512]{1,0:T(8,128)(2,1)S(1)} %shard_map.118.results, bf16[2048,512]{1,0:T(8,128)(2,1)} %w_in.1, bf16[2048,512]{1,0:T(8,128)(2,1)} %w_out.1), custom_call_target="tpu_custom_call" | custom-call | tf_op jit(solution)/shard_map/pallas_call | solution.py:40
  89.0 6.3 %all-to-all-start.2 = ((bf16[4,2,512,256]{3,2,1,0:T(8,128)(2,1)}), bf16[4,2,512,256]{3,2,1,0:T(8,128)(2,1)S(1)}, u32[]{:S(2)}, u32[]{:S(2)}) async-start(bf16[4,2,512,256]{3,2,1,0:T(8,128)(2,1)} %bitcast.14), calls=%async_computation.2 | async-start | bytes 4194304 | tf_op jit(solution)/shard_map/all_to_all | solution.py:583
  96.5 2.2 %shard_map.123 = (bf16[4,2,64,512]{3,2,1,0:T(8,128)(2,1)S(1)}, bf16[4,64,512]{2,1,0:T(8,128)(2,1)}, bf16[4,64,512]{2,1,0:T(8,128)(2,1)}) custom-call(s32[1]{0:T(128)} %bitcast.13.place, bf16[8,2,64,512]{3,2,1,0:T(8,128)(2,1)S(1)} %copy-done.15, bf16[8,2,64,512]{3,2,1,0:T(8,128)(2,1)} %collective-permute-done.13.recv), custom_call_target="tpu_custom_call" | custom-call | tf_op jit(solution)/shard_map/pallas_call | solution.py:40
  99.5 2.0 %collective-permute-start.14 = (bf16[4,64,512]{2,1,0:T(8,128)(2,1)}, bf16[4,64,512]{2,1,0:T(8,128)(2,1)S(1)}, u32[]{:S(2)}, u32[]{:S(2)}) collective-permute-start(bf16[4,64,512]{2,1,0:T(8,128)(2,1)} %get-tuple-element.71), channel_id=1, source_target_pairs={{0,16},{8,24},{16,0},{24,8},{32,48},{40,56},{48,32},{56,40},{64,80... | collective-permute-start | bytes 786440 | tf_op jit(solution)/shard_map/ppermute | solution.py:407
  102.6 5.2 %collective-permute-done.14.left = bf16[4,64,512]{2,1,0:T(8,128)(2,1)S(1)} collective-permute-done((bf16[4,64,512]{2,1,0:T(8,128)(2,1)}, bf16[4,64,512]{2,1,0:T(8,128)(2,1)S(1)}, u32[]{:S(2)}, u32[]{:S(2)}) %collective-permute-start.14) | collective-permute-done | bytes 262176 | tf_op jit(solution)/shard_map/ppermute | solution.py:407
  107.8 2.8 %collective-permute-done.15.right = bf16[4,64,512]{2,1,0:T(8,128)(2,1)} collective-permute-done((bf16[4,64,512]{2,1,0:T(8,128)(2,1)}, bf16[4,64,512]{2,1,0:T(8,128)(2,1)}, u32[]{:S(2)}, u32[]{:S(2)}) %collective-permute-start.15) | collective-permute-done | bytes 262176 | tf_op jit(solution)/shard_map/ppermute | solution.py:407
  114.5 2.9 %collective-permute-start.17 = (bf16[2,64,512]{2,1,0:T(8,128)(2,1)S(1)}, bf16[2,64,512]{2,1,0:T(8,128)(2,1)S(1)}, u32[]{:S(2)}, u32[]{:S(2)}) collective-permute-start(bf16[2,64,512]{2,1,0:T(8,128)(2,1)S(1)} %get-tuple-element.77), channel_id=1, source_target_pairs={{0,64},{8,72},{16,80},{24,88},{32,96},{40,104},{48,112},{56,120},{... | collective-permute-start | bytes 393224 | tf_op jit(solution)/shard_map/ppermute | solution.py:407
  117.4 2.8 %collective-permute-start.18 = (bf16[2,64,512]{2,1,0:T(8,128)(2,1)S(1)}, bf16[2,64,512]{2,1,0:T(8,128)(2,1)S(1)}, u32[]{:S(2)}, u32[]{:S(2)}) collective-permute-start(bf16[2,64,512]{2,1,0:T(8,128)(2,1)S(1)} %get-tuple-element.78), channel_id=1, source_target_pairs={{0,96},{8,104},{16,112},{24,120},{32,0},{40,8},{48,16},{56,24},{64... | collective-permute-start | bytes 393224 | tf_op jit(solution)/shard_map/ppermute | solution.py:407
  120.2 4.1 %collective-permute-done.21.recv = bf16[8,64,512]{2,1,0:T(8,128)(2,1)S(1)} collective-permute-done((bf16[8,64,512]{2,1,0:T(8,128)(2,1)S(1)}, bf16[8,64,512]{2,1,0:T(8,128)(2,1)S(1)}, u32[]{:S(2)}, u32[]{:S(2)}) %collective-permute-start.21) | collective-permute-done | bytes 524320 | tf_op jit(solution)/shard_map/ppermute | solution.py:399
  126.7 3.0 %collective-permute-done.18.d = bf16[2,64,512]{2,1,0:T(8,128)(2,1)S(1)} collective-permute-done((bf16[2,64,512]{2,1,0:T(8,128)(2,1)S(1)}, bf16[2,64,512]{2,1,0:T(8,128)(2,1)S(1)}, u32[]{:S(2)}, u32[]{:S(2)}) %collective-permute-start.18) | collective-permute-done | bytes 131104 | tf_op jit(solution)/shard_map/ppermute | solution.py:407
  131.0 2.8 %collective-permute-start.12 = (bf16[512,256]{1,0:T(8,128)(2,1)S(1)}, bf16[512,256]{1,0:T(8,128)(2,1)S(1)}, u32[]{:S(2)}, u32[]{:S(2)}) collective-permute-start(bf16[512,256]{1,0:T(8,128)(2,1)S(1)} %get-tuple-element.62), channel_id=1, source_target_pairs={{0,1},{1,0},{2,3},{3,2},{4,5},{5,4},{6,7},{7,6},{8,9},{9,8},{10,11... | collective-permute-start | bytes 786440 | tf_op jit(solution)/shard_map/ppermute | solution.py:414
  133.9 3.5 %collective-permute-start.24 = (bf16[64,512]{1,0:T(8,128)(2,1)S(1)}, bf16[64,512]{1,0:T(8,128)(2,1)S(1)}, u32[]{:S(2)}, u32[]{:S(2)}) collective-permute-start(bf16[64,512]{1,0:T(8,128)(2,1)S(1)} %get-tuple-element.89), channel_id=1, source_target_pairs={{0,32},{8,40},{16,48},{24,56},{32,64},{40,72},{48,80},{56,88},{64,... | collective-permute-start | bytes 196616 | tf_op jit(solution)/shard_map/ppermute | solution.py:407
  139.1 2.0 %collective-permute-start.26 = (bf16[64,512]{1,0:T(8,128)(2,1)S(1)}, bf16[64,512]{1,0:T(8,128)(2,1)S(1)}, u32[]{:S(2)}, u32[]{:S(2)}) collective-permute-start(bf16[64,512]{1,0:T(8,128)(2,1)S(1)} %get-tuple-element.91), channel_id=1, source_target_pairs={{0,96},{8,104},{16,112},{24,120},{32,0},{40,8},{48,16},{56,24},{64... | collective-permute-start | bytes 196616 | tf_op jit(solution)/shard_map/ppermute | solution.py:407
  142.5 3.8 %collective-permute-done.25.c = bf16[64,512]{1,0:T(8,128)(2,1)S(1)} collective-permute-done((bf16[64,512]{1,0:T(8,128)(2,1)S(1)}, bf16[64,512]{1,0:T(8,128)(2,1)S(1)}, u32[]{:S(2)}, u32[]{:S(2)}) %collective-permute-start.25) | collective-permute-done | bytes 65568 | tf_op jit(solution)/shard_map/ppermute | solution.py:407
  (112 shorter events, 41.5 us)
Async XLA Ops:
  2.5 9.6 %collective-permute-start = (bf16[512,256]{1,0:T(8,128)(2,1)S(1)}, bf16[512,256]{1,0:T(8,128)(2,1)S(1)}, u32[]{:S(2)}, u32[]{:S(2)}) collective-permute-start(bf16[512,256]{1,0:T(8,128)(2,1)S(1)} %shard_map.111.refs_0_), channel_id=1, source_target_pairs={{0,1},{1,0},{2,3},{3,2},{4,5},{5,4},{6,7},{7,6},{8,9},{9,8},{10,11... | collective-permute-start | bytes 786440 | tf_op jit(solution)/shard_map/ppermute | solution.py:414
  5.6 10.8 %collective-permute-start.1 = (bf16[512,256]{1,0:T(8,128)(2,1)S(1)}, bf16[512,256]{1,0:T(8,128)(2,1)S(1)}, u32[]{:S(2)}, u32[]{:S(2)}) collective-permute-start(bf16[512,256]{1,0:T(8,128)(2,1)S(1)} %shard_map.111.refs_0_), channel_id=1, source_target_pairs={{0,2},{1,3},{2,4},{3,5},{4,6},{5,7},{6,0},{7,1},{8,10},{9,11},{10,... | collective-permute-start | bytes 786440 | tf_op jit(solution)/shard_map/ppermute | solution.py:414
  7.2 9.2 %collective-permute-start.2 = (bf16[512,256]{1,0:T(8,128)(2,1)S(1)}, bf16[512,256]{1,0:T(8,128)(2,1)S(1)}, u32[]{:S(2)}, u32[]{:S(2)}) collective-permute-start(bf16[512,256]{1,0:T(8,128)(2,1)S(1)} %shard_map.111.refs_0_), channel_id=1, source_target_pairs={{0,6},{1,7},{2,0},{3,1},{4,2},{5,3},{6,4},{7,5},{8,14},{9,15},{10,... | collective-permute-start | bytes 786440 | tf_op jit(solution)/shard_map/ppermute | solution.py:414
  12.2 7.2 %collective-permute-start.4 = (bf16[512,256]{1,0:T(8,128)(2,1)S(1)}, bf16[512,256]{1,0:T(8,128)(2,1)S(1)}, u32[]{:S(2)}, u32[]{:S(2)}) collective-permute-start(bf16[512,256]{1,0:T(8,128)(2,1)S(1)} %collective-permute-done.refs_1_), channel_id=1, source_target_pairs={{0,2},{1,3},{2,4},{3,5},{4,6},{5,7},{6,0},{7,1},{8,10},{9,11},{10,... | collective-permute-start | bytes 786440 | tf_op jit(solution)/shard_map/ppermute | solution.py:414
  13.8 7.3 %collective-permute-start.5 = (bf16[512,256]{1,0:T(8,128)(2,1)S(1)}, bf16[512,256]{1,0:T(8,128)(2,1)S(1)}, u32[]{:S(2)}, u32[]{:S(2)}) collective-permute-start(bf16[512,256]{1,0:T(8,128)(2,1)S(1)} %collective-permute-done.refs_1_), channel_id=1, source_target_pairs={{0,6},{1,7},{2,0},{3,1},{4,2},{5,3},{6,4},{7,5},{8,14},{9,15},{10,... | collective-permute-start | bytes 786440 | tf_op jit(solution)/shard_map/ppermute | solution.py:414
  16.5 5.7 %collective-permute-start.6 = (bf16[256,256]{1,0:T(8,128)(2,1)S(1)}, bf16[256,256]{1,0:T(8,128)(2,1)S(1)}, u32[]{:S(2)}, u32[]{:S(2)}) collective-permute-start(bf16[256,256]{1,0:T(8,128)(2,1)S(1)} %slice.12), channel_id=1, source_target_pairs={{0,2},{1,3},{2,4},{3,5},{4,6},{5,7},{6,0},{7,1},{8,10},{9,11},{10,... | collective-permute-start | bytes 393224 | tf_op jit(solution)/shard_map/ppermute | solution.py:414
  18.1 6.4 %collective-permute-start.7 = (bf16[256,256]{1,0:T(8,128)(2,1)S(1)}, bf16[256,256]{1,0:T(8,128)(2,1)S(1)}, u32[]{:S(2)}, u32[]{:S(2)}) collective-permute-start(bf16[256,256]{1,0:T(8,128)(2,1)S(1)} %slice.13), channel_id=1, source_target_pairs={{0,6},{1,7},{2,0},{3,1},{4,2},{5,3},{6,4},{7,5},{8,14},{9,15},{10,... | collective-permute-start | bytes 393224 | tf_op jit(solution)/shard_map/ppermute | solution.py:414
  37.8 21.2 %all-to-all-start = ((bf16[16,80,128]{2,1,0:T(8,128)(2,1)}), bf16[16,80,128]{2,1,0:T(8,128)(2,1)S(1)}, u32[]{:S(2)}, u32[]{:S(2)}) async-start(bf16[16,80,128]{2,1,0:T(8,128)(2,1)} %shard_map.114), calls=%async_computation | async-start | bytes 655360 | tf_op jit(solution)/shard_map/all_to_all | solution.py:530
  79.6 15.7 %collective-permute-start.13 = (bf16[8,2,64,512]{3,2,1,0:T(8,128)(2,1)}, bf16[8,2,64,512]{3,2,1,0:T(8,128)(2,1)}, u32[]{:S(2)}, u32[]{:S(2)}) collective-permute-start(bf16[8,2,64,512]{3,2,1,0:T(8,128)(2,1)} %get-tuple-element.67), channel_id=1, source_target_pairs={{0,8},{8,0},{16,24},{24,16},{32,40},{40,32},{48,56},{56,48},{64,72... | collective-permute-start | bytes 3145736 | tf_op jit(solution)/shard_map/ppermute | solution.py:399
  82.0 28.6 %collective-permute-start.20 = (bf16[8,2,64,512]{3,2,1,0:T(8,128)(2,1)}, bf16[8,2,64,512]{3,2,1,0:T(8,128)(2,1)}, u32[]{:S(2)}, u32[]{:S(2)}) collective-permute-start(bf16[8,2,64,512]{3,2,1,0:T(8,128)(2,1)} %get-tuple-element.82), channel_id=1, source_target_pairs={{0,8},{8,0},{16,24},{24,16},{32,40},{40,32},{48,56},{56,48},{64,72... | collective-permute-start | bytes 3145736 | tf_op jit(solution)/shard_map/ppermute | solution.py:399
  89.0 41.7 %all-to-all-start.2 = ((bf16[4,2,512,256]{3,2,1,0:T(8,128)(2,1)}), bf16[4,2,512,256]{3,2,1,0:T(8,128)(2,1)S(1)}, u32[]{:S(2)}, u32[]{:S(2)}) async-start(bf16[4,2,512,256]{3,2,1,0:T(8,128)(2,1)} %bitcast.14), calls=%async_computation.2 | async-start | bytes 4194304 | tf_op jit(solution)/shard_map/all_to_all | solution.py:583
  99.5 8.3 %collective-permute-start.14 = (bf16[4,64,512]{2,1,0:T(8,128)(2,1)}, bf16[4,64,512]{2,1,0:T(8,128)(2,1)S(1)}, u32[]{:S(2)}, u32[]{:S(2)}) collective-permute-start(bf16[4,64,512]{2,1,0:T(8,128)(2,1)} %get-tuple-element.71), channel_id=1, source_target_pairs={{0,16},{8,24},{16,0},{24,8},{32,48},{40,56},{48,32},{56,40},{64,80... | collective-permute-start | bytes 786440 | tf_op jit(solution)/shard_map/ppermute | solution.py:407
  101.5 9.0 %collective-permute-start.15 = (bf16[4,64,512]{2,1,0:T(8,128)(2,1)}, bf16[4,64,512]{2,1,0:T(8,128)(2,1)}, u32[]{:S(2)}, u32[]{:S(2)}) collective-permute-start(bf16[4,64,512]{2,1,0:T(8,128)(2,1)} %get-tuple-element.72), channel_id=1, source_target_pairs={{0,112},{8,120},{16,32},{24,40},{32,16},{40,24},{48,64},{56,72},{6... | collective-permute-start | bytes 786440 | tf_op jit(solution)/shard_map/ppermute | solution.py:407
  112.1 12.3 %collective-permute-start.21 = (bf16[8,64,512]{2,1,0:T(8,128)(2,1)S(1)}, bf16[8,64,512]{2,1,0:T(8,128)(2,1)S(1)}, u32[]{:S(2)}, u32[]{:S(2)}) collective-permute-start(bf16[8,64,512]{2,1,0:T(8,128)(2,1)S(1)} %get-tuple-element.84), channel_id=1, source_target_pairs={{0,128},{8,136},{16,144},{24,152},{32,160},{40,168},{48,176},{56,1... | collective-permute-start | bytes 1572872 | tf_op jit(solution)/shard_map/ppermute | solution.py:399
  114.4 12.3 %collective-permute-start.16 = (bf16[2,64,512]{2,1,0:T(8,128)(2,1)S(1)}, bf16[2,64,512]{2,1,0:T(8,128)(2,1)S(1)}, u32[]{:S(2)}, u32[]{:S(2)}) collective-permute-start(bf16[2,64,512]{2,1,0:T(8,128)(2,1)S(1)} %get-tuple-element.76), channel_id=1, source_target_pairs={{0,32},{8,40},{16,48},{24,56},{32,64},{40,72},{48,80},{56,88},{64,... | collective-permute-start | bytes 393224 | tf_op jit(solution)/shard_map/ppermute | solution.py:407
  114.5 12.2 %collective-permute-start.17 = (bf16[2,64,512]{2,1,0:T(8,128)(2,1)S(1)}, bf16[2,64,512]{2,1,0:T(8,128)(2,1)S(1)}, u32[]{:S(2)}, u32[]{:S(2)}) collective-permute-start(bf16[2,64,512]{2,1,0:T(8,128)(2,1)S(1)} %get-tuple-element.77), channel_id=1, source_target_pairs={{0,64},{8,72},{16,80},{24,88},{32,96},{40,104},{48,112},{56,120},{... | collective-permute-start | bytes 393224 | tf_op jit(solution)/shard_map/ppermute | solution.py:407
  117.4 12.3 %collective-permute-start.18 = (bf16[2,64,512]{2,1,0:T(8,128)(2,1)S(1)}, bf16[2,64,512]{2,1,0:T(8,128)(2,1)S(1)}, u32[]{:S(2)}, u32[]{:S(2)}) collective-permute-start(bf16[2,64,512]{2,1,0:T(8,128)(2,1)S(1)} %get-tuple-element.78), channel_id=1, source_target_pairs={{0,96},{8,104},{16,112},{24,120},{32,0},{40,8},{48,16},{56,24},{64... | collective-permute-start | bytes 393224 | tf_op jit(solution)/shard_map/ppermute | solution.py:407
  124.5 9.3 %collective-permute-start.22 = (bf16[4,32,512]{2,1,0:T(8,128)(2,1)S(1)}, bf16[4,32,512]{2,1,0:T(8,128)(2,1)S(1)}, u32[]{:S(2)}, u32[]{:S(2)}) collective-permute-start(bf16[4,32,512]{2,1,0:T(8,128)(2,1)S(1)} %get-tuple-element.86), channel_id=1, source_target_pairs={{0,16},{8,24},{16,0},{24,8},{32,48},{40,56},{48,32},{56,40},{64,80... | collective-permute-start | bytes 393224 | tf_op jit(solution)/shard_map/ppermute | solution.py:407
  124.6 9.2 %collective-permute-start.23 = (bf16[4,32,512]{2,1,0:T(8,128)(2,1)S(1)}, bf16[4,32,512]{2,1,0:T(8,128)(2,1)S(1)}, u32[]{:S(2)}, u32[]{:S(2)}) collective-permute-start(bf16[4,32,512]{2,1,0:T(8,128)(2,1)S(1)} %get-tuple-element.87), channel_id=1, source_target_pairs={{0,112},{8,120},{16,32},{24,40},{32,16},{40,24},{48,64},{56,72},{6... | collective-permute-start | bytes 393224 | tf_op jit(solution)/shard_map/ppermute | solution.py:407
  129.8 11.3 %collective-permute-start.19 = (bf16[64,512]{1,0:T(8,128)(2,1)S(1)}, bf16[64,512]{1,0:T(8,128)(2,1)S(1)}, u32[]{:S(2)}, u32[]{:S(2)}) collective-permute-start(bf16[64,512]{1,0:T(8,128)(2,1)S(1)} %get-tuple-element.80), channel_id=1, source_target_pairs={{0,128},{8,136},{16,144},{24,152},{32,160},{40,168},{48,176},{56,1... | collective-permute-start | bytes 196616 | tf_op jit(solution)/shard_map/ppermute | solution.py:399
  131.0 10.8 %collective-permute-start.12 = (bf16[512,256]{1,0:T(8,128)(2,1)S(1)}, bf16[512,256]{1,0:T(8,128)(2,1)S(1)}, u32[]{:S(2)}, u32[]{:S(2)}) collective-permute-start(bf16[512,256]{1,0:T(8,128)(2,1)S(1)} %get-tuple-element.62), channel_id=1, source_target_pairs={{0,1},{1,0},{2,3},{3,2},{4,5},{5,4},{6,7},{7,6},{8,9},{9,8},{10,11... | collective-permute-start | bytes 786440 | tf_op jit(solution)/shard_map/ppermute | solution.py:414
  133.9 8.6 %collective-permute-start.24 = (bf16[64,512]{1,0:T(8,128)(2,1)S(1)}, bf16[64,512]{1,0:T(8,128)(2,1)S(1)}, u32[]{:S(2)}, u32[]{:S(2)}) collective-permute-start(bf16[64,512]{1,0:T(8,128)(2,1)S(1)} %get-tuple-element.89), channel_id=1, source_target_pairs={{0,32},{8,40},{16,48},{24,56},{32,64},{40,72},{48,80},{56,88},{64,... | collective-permute-start | bytes 196616 | tf_op jit(solution)/shard_map/ppermute | solution.py:407
  137.4 8.9 %collective-permute-start.25 = (bf16[64,512]{1,0:T(8,128)(2,1)S(1)}, bf16[64,512]{1,0:T(8,128)(2,1)S(1)}, u32[]{:S(2)}, u32[]{:S(2)}) collective-permute-start(bf16[64,512]{1,0:T(8,128)(2,1)S(1)} %get-tuple-element.90), channel_id=1, source_target_pairs={{0,64},{8,72},{16,80},{24,88},{32,96},{40,104},{48,112},{56,120},{... | collective-permute-start | bytes 196616 | tf_op jit(solution)/shard_map/ppermute | solution.py:407
  139.1 7.3 %collective-permute-start.26 = (bf16[64,512]{1,0:T(8,128)(2,1)S(1)}, bf16[64,512]{1,0:T(8,128)(2,1)S(1)}, u32[]{:S(2)}, u32[]{:S(2)}) collective-permute-start(bf16[64,512]{1,0:T(8,128)(2,1)S(1)} %get-tuple-element.91), channel_id=1, source_target_pairs={{0,96},{8,104},{16,112},{24,120},{32,0},{40,8},{48,16},{56,24},{64... | collective-permute-start | bytes 196616 | tf_op jit(solution)/shard_map/ppermute | solution.py:407
  (30 other events, 245.9 us)

commit v4 on v3

--- a/solution.py
+++ b/solution.py
@@ -7,7 +7,7 @@
 
 F32 = jnp.float32
 BF16 = jnp.bfloat16
-ORDER = 4
+ORDER = 0
 SLACK = 2
 EARLY = True
 B_EXTRA = 42
@@ -556,6 +556,7 @@
         scalars=1,
     )
     keep_in, send_in = call(gradient_in_kernel, halves, core, results, tokens_t, scalars=1)
+    results, keep_in = lax.optimization_barrier((results, keep_in))
     keep_out, send_out = call(gradient_out_kernel, halves, core, results, cotangent_t, scalars=1)
     line, x_lo = (chip % 8).reshape(1), x_lo.reshape(1)
     recv_in = partner(send_in, 1)
@@ -564,6 +565,7 @@
     stay_in, left, right = z_first(line, keep_in, recv_in)
     if ORDER & 2:
         results, left, right = lax.optimization_barrier((results, left, right))
+    keep_out, left, right = lax.optimization_barrier((keep_out, left, right))
     left, right = along_line(left, beside), along_line(right, otherwise)
     if ORDER & 4:
         keep_out, left, right = lax.optimization_barrier((keep_out, left, right))

time: 148 us -> 145 us (0.980)
  Pallas kernels: 32.3 us -> 30.6 us
    ppermute x10, waiting for transfers between devices: 15.8 us -> 20.3 us  [along_line(): return lax.ppermute(block, 'seq', route)]
    ppermute x7, waiting for transfers between devices: 8.58 us -> 4.44 us  [partner(): return lax.ppermute(block, 'seq', [(i, i ^ bit) for i in range(count)])]
    pallas_call x20, Pallas kernels: 32.3 us -> 30.6 us  [call(): pl.pallas_call(kernel, out_shape=outs, in_specs=[pl.BlockSpec(memory_spac...]
    unnamed x51 -> x47, local copies, waits for them, and re-layouts: 10.5 us -> 9.67 us
  transfers between devices with their start and end apart: 29 -> 29, of which waited for: 16 -> 16; matrix products, arithmetic and copies ran while one was open for 1% -> 1% of each run, Pallas kernels for 13% -> 12%
where the time goes in v4:
time: 145 us
  starting transfers between devices  50.7 us (35%)
  waiting for transfers between devices  36.2 us (25%)
  Pallas kernels  30.6 us (21%)
  blocking collectives  15.8 us (11%)
  local copies, waits for them, and re-layouts  9.79 us (7%)
    pallas_call x20, Pallas kernels, call(): pl.pallas_call(kernel, out_shape=outs, in_specs=[pl.BlockSpec(memory_spac...  30.6 us
    ppermute x10, waiting for transfers between devices, along_line(): return lax.ppermute(block, 'seq', route)  20.3 us
    ppermute x10, starting transfers between devices, along_line(): return lax.ppermute(block, 'seq', route)  17.1 us
    all_to_all x1, blocking collectives, shards(): chip_carried = lax.all_to_all(carried, 'seq', 0, 0, axis_index_groups=chips)  15.8 us
    ppermute x10, starting transfers between devices, around(): return lax.ppermute(block, 'head', route)  14.8 us
    unnamed x47, local copies, waits for them, and re-layouts  9.67 us
    all_to_all x1, starting transfers between devices, shards(): lax.all_to_all(chip_states, 'seq', 0, 0, axis_index_groups=chips)  9.5 us
    ppermute x10, waiting for transfers between devices, around(): return lax.ppermute(block, 'head', route)  9.41 us
  transfers between devices with their start and end apart: 29, of which 16 were waited for; matrix products, arithmetic and copies ran while one was open for 1% of the time, Pallas kernels for 12%

profile of v4, /device:TPU:8, one launch (start us, length us, event | category | flops | bytes accessed | tf_op | source)
XLA Modules:
  0.0 144.8 jit_solution(13613861405946945700)
XLA Ops:
  2.5 3.1 %collective-permute-start = (bf16[512,256]{1,0:T(8,128)(2,1)S(1)}, bf16[512,256]{1,0:T(8,128)(2,1)S(1)}, u32[]{:S(2)}, u32[]{:S(2)}) collective-permute-start(bf16[512,256]{1,0:T(8,128)(2,1)S(1)} %shard_map.111.refs_0_), channel_id=1, source_target_pairs={{0,1},{1,0},{2,3},{3,2},{4,5},{5,4},{6,7},{7,6},{8,9},{9,8},{10,11... | collective-permute-start | bytes 786440 | tf_op jit(solution)/shard_map/ppermute | solution.py:414
  7.7 4.5 %collective-permute-done.refs_1_ = bf16[512,256]{1,0:T(8,128)(2,1)S(1)} collective-permute-done((bf16[512,256]{1,0:T(8,128)(2,1)S(1)}, bf16[512,256]{1,0:T(8,128)(2,1)S(1)}, u32[]{:S(2)}, u32[]{:S(2)}) %collective-permute-start) | collective-permute-done | bytes 262176 | tf_op jit(solution)/shard_map/ppermute | solution.py:414
  22.2 2.3 %collective-permute-done.7.refs_7_ = bf16[256,256]{1,0:T(8,128)(2,1)S(1)} collective-permute-done((bf16[256,256]{1,0:T(8,128)(2,1)S(1)}, bf16[256,256]{1,0:T(8,128)(2,1)S(1)}, u32[]{:S(2)}, u32[]{:S(2)}) %collective-permute-start.7) | collective-permute-done | bytes 131104 | tf_op jit(solution)/shard_map/ppermute | solution.py:414
  26.4 8.7 %shard_map.113 = (bf16[4,256,512]{2,1,0:T(8,128)(2,1)}, bf16[4,4,256,128]{3,2,1,0:T(8,128)(2,1)}, bf16[8,128,128]{2,1,0:T(8,128)(2,1)S(1)}, bf16[8,128,128]{2,1,0:T(8,128)(2,1)}) custom-call(s32[1]{0:T(128)} %bitcast.1.core, f32[4]{0:T(128)S(1)} %copy-done.22, s32[8]{0:T(128)S(1)} %stack.35.places, bf16[512,256]{1,0:T(8,128)(2,1)} %copy-done, ...), custom_call_target="tpu_custom_call" | custom-call | tf_op jit(solution)/shard_map/pallas_call | solution.py:40
  35.2 1.7 %collective-permute-done.10.recv = bf16[8,128,128]{2,1,0:T(8,128)(2,1)S(1)} collective-permute-done((bf16[8,128,128]{2,1,0:T(8,128)(2,1)}, bf16[8,128,128]{2,1,0:T(8,128)(2,1)S(1)}, u32[]{:S(2)}, u32[]{:S(2)}) %collective-permute-start.10) | collective-permute-done | bytes 262176 | tf_op jit(solution)/shard_map/ppermute | solution.py:399
  37.8 9.5 %all-to-all-start = ((bf16[16,80,128]{2,1,0:T(8,128)(2,1)}), bf16[16,80,128]{2,1,0:T(8,128)(2,1)S(1)}, u32[]{:S(2)}, u32[]{:S(2)}) async-start(bf16[16,80,128]{2,1,0:T(8,128)(2,1)} %shard_map.114), calls=%async_computation | async-start | bytes 655360 | tf_op jit(solution)/shard_map/all_to_all | solution.py:530
  53.1 3.8 %shard_map.116 = (bf16[2048,512]{1,0:T(8,128)(2,1)}, bf16[2048,512]{1,0:T(8,128)(2,1)}) custom-call(s32[8]{0:T(128)S(1)} %stack.35.places, bf16[512,256]{1,0:T(8,128)(2,1)S(1)} %copy-done.1, bf16[512,256]{1,0:T(8,128)(2,1)S(1)} %copy-done.13, bf16[512,256]{1,0:T(8,128)(2,1)S(1)} %copy-done.5, bf16[512,256]{1,0:T(8,128)(2,1)S(1)} %copy-done.9, ...), custom_call_target="tpu_custom_call" | custom-call | tf_op jit(solution)/shard_map/pallas_call | solution.py:40
  56.9 2.1 %all-to-all-done.states = bf16[16,80,128]{2,1,0:T(8,128)(2,1)S(1)} async-done(((bf16[16,80,128]{2,1,0:T(8,128)(2,1)}), bf16[16,80,128]{2,1,0:T(8,128)(2,1)S(1)}, u32[]{:S(2)}, u32[]{:S(2)}) %all-to-all-start) | async-done | bytes 327712 | tf_op jit(solution)/shard_map/all_to_all | solution.py:530
  59.3 15.8 %all_to_all.15.chip = bf16[16,64,128]{2,1,0:T(8,128)(2,1)S(1)} all-to-all(bf16[16,64,128]{2,1,0:T(8,128)(2,1)S(1)} %shard_map.115), channel_id=1, replica_groups={{0,16,32,48,64,80,96,112,128,144,160,176,192,208,224,240},{8,24,40,56,7..., dimensions={0} | all-to-all | bytes 524288 | tf_op jit(solution)/shard_map/all_to_all | solution.py:534
  77.3 2.2 %shard_map.119 = (bf16[8,2,64,512]{3,2,1,0:T(8,128)(2,1)S(1)}, bf16[8,2,64,512]{3,2,1,0:T(8,128)(2,1)}) custom-call(s32[1]{0:T(128)} %bitcast.1.core, bf16[1024,512]{1,0:T(8,128)(2,1)S(1)} %shard_map.118.results, bf16[2048,512]{1,0:T(8,128)(2,1)S(1)} %copy-done.3), custom_call_target="tpu_custom_call" | custom-call | tf_op jit(solution)/shard_map/pallas_call | solution.py:40
  79.7 2.3 %shard_map.124 = (bf16[8,2,64,512]{3,2,1,0:T(8,128)(2,1)S(1)}, bf16[8,2,64,512]{3,2,1,0:T(8,128)(2,1)}) custom-call(s32[1]{0:T(128)} %bitcast.1.core, bf16[1024,512]{1,0:T(8,128)(2,1)S(1)} %shard_map.118.results, bf16[2048,512]{1,0:T(8,128)(2,1)S(1)} %copy-done.2), custom_call_target="tpu_custom_call" | custom-call | tf_op jit(solution)/shard_map/pallas_call | solution.py:40
  82.4 6.6 %shard_map.120 = bf16[8,512,256]{2,1,0:T(8,128)(2,1)} custom-call(bf16[1024,512]{1,0:T(8,128)(2,1)S(1)} %shard_map.118.results, bf16[2048,512]{1,0:T(8,128)(2,1)} %w_in.1, bf16[2048,512]{1,0:T(8,128)(2,1)} %w_out.1), custom_call_target="tpu_custom_call" | custom-call | tf_op jit(solution)/shard_map/pallas_call | solution.py:40
  89.0 6.3 %all-to-all-start.2 = ((bf16[4,2,512,256]{3,2,1,0:T(8,128)(2,1)}), bf16[4,2,512,256]{3,2,1,0:T(8,128)(2,1)S(1)}, u32[]{:S(2)}, u32[]{:S(2)}) async-start(bf16[4,2,512,256]{3,2,1,0:T(8,128)(2,1)} %bitcast.14), calls=%async_computation.2 | async-start | bytes 4194304 | tf_op jit(solution)/shard_map/all_to_all | solution.py:585
  100.9 1.9 %collective-permute-start.14 = (bf16[4,64,512]{2,1,0:T(8,128)(2,1)S(1)}, bf16[4,64,512]{2,1,0:T(8,128)(2,1)S(1)}, u32[]{:S(2)}, u32[]{:S(2)}) collective-permute-start(bf16[4,64,512]{2,1,0:T(8,128)(2,1)S(1)} %get-tuple-element.77), channel_id=1, source_target_pairs={{0,16},{8,24},{16,0},{24,8},{32,48},{40,56},{48,32},{56,40},{64,80... | collective-permute-start | bytes 786440 | tf_op jit(solution)/shard_map/ppermute | solution.py:407
  103.8 4.7 %collective-permute-done.14.left = bf16[4,64,512]{2,1,0:T(8,128)(2,1)S(1)} collective-permute-done((bf16[4,64,512]{2,1,0:T(8,128)(2,1)S(1)}, bf16[4,64,512]{2,1,0:T(8,128)(2,1)S(1)}, u32[]{:S(2)}, u32[]{:S(2)}) %collective-permute-start.14) | collective-permute-done | bytes 262176 | tf_op jit(solution)/shard_map/ppermute | solution.py:407
  108.6 2.7 %collective-permute-done.15.right = bf16[4,64,512]{2,1,0:T(8,128)(2,1)S(1)} collective-permute-done((bf16[4,64,512]{2,1,0:T(8,128)(2,1)S(1)}, bf16[4,64,512]{2,1,0:T(8,128)(2,1)S(1)}, u32[]{:S(2)}, u32[]{:S(2)}) %collective-permute-start.15) | collective-permute-done | bytes 262176 | tf_op jit(solution)/shard_map/ppermute | solution.py:407
  111.4 2.9 %collective-permute-start.17 = (bf16[2,64,512]{2,1,0:T(8,128)(2,1)S(1)}, bf16[2,64,512]{2,1,0:T(8,128)(2,1)S(1)}, u32[]{:S(2)}, u32[]{:S(2)}) collective-permute-start(bf16[2,64,512]{2,1,0:T(8,128)(2,1)S(1)} %get-tuple-element.81), channel_id=1, source_target_pairs={{0,64},{8,72},{16,80},{24,88},{32,96},{40,104},{48,112},{56,120},{... | collective-permute-start | bytes 393224 | tf_op jit(solution)/shard_map/ppermute | solution.py:407
  114.3 2.8 %collective-permute-start.18 = (bf16[2,64,512]{2,1,0:T(8,128)(2,1)S(1)}, bf16[2,64,512]{2,1,0:T(8,128)(2,1)S(1)}, u32[]{:S(2)}, u32[]{:S(2)}) collective-permute-start(bf16[2,64,512]{2,1,0:T(8,128)(2,1)S(1)} %get-tuple-element.82), channel_id=1, source_target_pairs={{0,96},{8,104},{16,112},{24,120},{32,0},{40,8},{48,16},{56,24},{64... | collective-permute-start | bytes 393224 | tf_op jit(solution)/shard_map/ppermute | solution.py:407
  118.9 4.7 %collective-permute-done.16.b = bf16[2,64,512]{2,1,0:T(8,128)(2,1)S(1)} collective-permute-done((bf16[2,64,512]{2,1,0:T(8,128)(2,1)S(1)}, bf16[2,64,512]{2,1,0:T(8,128)(2,1)S(1)}, u32[]{:S(2)}, u32[]{:S(2)}) %collective-permute-start.16) | collective-permute-done | bytes 131104 | tf_op jit(solution)/shard_map/ppermute | solution.py:407
  123.7 3.5 %collective-permute-done.18.d = bf16[2,64,512]{2,1,0:T(8,128)(2,1)S(1)} collective-permute-done((bf16[2,64,512]{2,1,0:T(8,128)(2,1)S(1)}, bf16[2,64,512]{2,1,0:T(8,128)(2,1)S(1)}, u32[]{:S(2)}, u32[]{:S(2)}) %collective-permute-start.18) | collective-permute-done | bytes 131104 | tf_op jit(solution)/shard_map/ppermute | solution.py:407
  128.4 2.8 %collective-permute-start.12 = (bf16[512,256]{1,0:T(8,128)(2,1)S(1)}, bf16[512,256]{1,0:T(8,128)(2,1)S(1)}, u32[]{:S(2)}, u32[]{:S(2)}) collective-permute-start(bf16[512,256]{1,0:T(8,128)(2,1)S(1)} %get-tuple-element.67), channel_id=1, source_target_pairs={{0,1},{1,0},{2,3},{3,2},{4,5},{5,4},{6,7},{7,6},{8,9},{9,8},{10,11... | collective-permute-start | bytes 786440 | tf_op jit(solution)/shard_map/ppermute | solution.py:414
  131.3 3.0 %collective-permute-start.24 = (bf16[64,512]{1,0:T(8,128)(2,1)S(1)}, bf16[64,512]{1,0:T(8,128)(2,1)S(1)}, u32[]{:S(2)}, u32[]{:S(2)}) collective-permute-start(bf16[64,512]{1,0:T(8,128)(2,1)S(1)} %get-tuple-element.93), channel_id=1, source_target_pairs={{0,32},{8,40},{16,48},{24,56},{32,64},{40,72},{48,80},{56,88},{64,... | collective-permute-start | bytes 196616 | tf_op jit(solution)/shard_map/ppermute | solution.py:407
  134.3 2.5 %collective-permute-start.25 = (bf16[64,512]{1,0:T(8,128)(2,1)S(1)}, bf16[64,512]{1,0:T(8,128)(2,1)S(1)}, u32[]{:S(2)}, u32[]{:S(2)}) collective-permute-start(bf16[64,512]{1,0:T(8,128)(2,1)S(1)} %get-tuple-element.94), channel_id=1, source_target_pairs={{0,64},{8,72},{16,80},{24,88},{32,96},{40,104},{48,112},{56,120},{... | collective-permute-start | bytes 196616 | tf_op jit(solution)/shard_map/ppermute | solution.py:407
  138.7 3.8 %collective-permute-done.25.c = bf16[64,512]{1,0:T(8,128)(2,1)S(1)} collective-permute-done((bf16[64,512]{1,0:T(8,128)(2,1)S(1)}, bf16[64,512]{1,0:T(8,128)(2,1)S(1)}, u32[]{:S(2)}, u32[]{:S(2)}) %collective-permute-start.25) | collective-permute-done | bytes 65568 | tf_op jit(solution)/shard_map/ppermute | solution.py:407
  (108 shorter events, 39.4 us)
Async XLA Ops:
  2.5 9.6 %collective-permute-start = (bf16[512,256]{1,0:T(8,128)(2,1)S(1)}, bf16[512,256]{1,0:T(8,128)(2,1)S(1)}, u32[]{:S(2)}, u32[]{:S(2)}) collective-permute-start(bf16[512,256]{1,0:T(8,128)(2,1)S(1)} %shard_map.111.refs_0_), channel_id=1, source_target_pairs={{0,1},{1,0},{2,3},{3,2},{4,5},{5,4},{6,7},{7,6},{8,9},{9,8},{10,11... | collective-permute-start | bytes 786440 | tf_op jit(solution)/shard_map/ppermute | solution.py:414
  5.6 10.8 %collective-permute-start.1 = (bf16[512,256]{1,0:T(8,128)(2,1)S(1)}, bf16[512,256]{1,0:T(8,128)(2,1)S(1)}, u32[]{:S(2)}, u32[]{:S(2)}) collective-permute-start(bf16[512,256]{1,0:T(8,128)(2,1)S(1)} %shard_map.111.refs_0_), channel_id=1, source_target_pairs={{0,2},{1,3},{2,4},{3,5},{4,6},{5,7},{6,0},{7,1},{8,10},{9,11},{10,... | collective-permute-start | bytes 786440 | tf_op jit(solution)/shard_map/ppermute | solution.py:414
  7.2 9.2 %collective-permute-start.2 = (bf16[512,256]{1,0:T(8,128)(2,1)S(1)}, bf16[512,256]{1,0:T(8,128)(2,1)S(1)}, u32[]{:S(2)}, u32[]{:S(2)}) collective-permute-start(bf16[512,256]{1,0:T(8,128)(2,1)S(1)} %shard_map.111.refs_0_), channel_id=1, source_target_pairs={{0,6},{1,7},{2,0},{3,1},{4,2},{5,3},{6,4},{7,5},{8,14},{9,15},{10,... | collective-permute-start | bytes 786440 | tf_op jit(solution)/shard_map/ppermute | solution.py:414
  12.2 7.2 %collective-permute-start.4 = (bf16[512,256]{1,0:T(8,128)(2,1)S(1)}, bf16[512,256]{1,0:T(8,128)(2,1)S(1)}, u32[]{:S(2)}, u32[]{:S(2)}) collective-permute-start(bf16[512,256]{1,0:T(8,128)(2,1)S(1)} %collective-permute-done.refs_1_), channel_id=1, source_target_pairs={{0,2},{1,3},{2,4},{3,5},{4,6},{5,7},{6,0},{7,1},{8,10},{9,11},{10,... | collective-permute-start | bytes 786440 | tf_op jit(solution)/shard_map/ppermute | solution.py:414
  13.8 7.3 %collective-permute-start.5 = (bf16[512,256]{1,0:T(8,128)(2,1)S(1)}, bf16[512,256]{1,0:T(8,128)(2,1)S(1)}, u32[]{:S(2)}, u32[]{:S(2)}) collective-permute-start(bf16[512,256]{1,0:T(8,128)(2,1)S(1)} %collective-permute-done.refs_1_), channel_id=1, source_target_pairs={{0,6},{1,7},{2,0},{3,1},{4,2},{5,3},{6,4},{7,5},{8,14},{9,15},{10,... | collective-permute-start | bytes 786440 | tf_op jit(solution)/shard_map/ppermute | solution.py:414
  16.5 5.7 %collective-permute-start.6 = (bf16[256,256]{1,0:T(8,128)(2,1)S(1)}, bf16[256,256]{1,0:T(8,128)(2,1)S(1)}, u32[]{:S(2)}, u32[]{:S(2)}) collective-permute-start(bf16[256,256]{1,0:T(8,128)(2,1)S(1)} %slice.12), channel_id=1, source_target_pairs={{0,2},{1,3},{2,4},{3,5},{4,6},{5,7},{6,0},{7,1},{8,10},{9,11},{10,... | collective-permute-start | bytes 393224 | tf_op jit(solution)/shard_map/ppermute | solution.py:414
  18.1 6.4 %collective-permute-start.7 = (bf16[256,256]{1,0:T(8,128)(2,1)S(1)}, bf16[256,256]{1,0:T(8,128)(2,1)S(1)}, u32[]{:S(2)}, u32[]{:S(2)}) collective-permute-start(bf16[256,256]{1,0:T(8,128)(2,1)S(1)} %slice.13), channel_id=1, source_target_pairs={{0,6},{1,7},{2,0},{3,1},{4,2},{5,3},{6,4},{7,5},{8,14},{9,15},{10,... | collective-permute-start | bytes 393224 | tf_op jit(solution)/shard_map/ppermute | solution.py:414
  37.8 21.2 %all-to-all-start = ((bf16[16,80,128]{2,1,0:T(8,128)(2,1)}), bf16[16,80,128]{2,1,0:T(8,128)(2,1)S(1)}, u32[]{:S(2)}, u32[]{:S(2)}) async-start(bf16[16,80,128]{2,1,0:T(8,128)(2,1)} %shard_map.114), calls=%async_computation | async-start | bytes 655360 | tf_op jit(solution)/shard_map/all_to_all | solution.py:530
  79.6 15.7 %collective-permute-start.13 = (bf16[8,2,64,512]{3,2,1,0:T(8,128)(2,1)}, bf16[8,2,64,512]{3,2,1,0:T(8,128)(2,1)}, u32[]{:S(2)}, u32[]{:S(2)}) collective-permute-start(bf16[8,2,64,512]{3,2,1,0:T(8,128)(2,1)} %get-tuple-element.71), channel_id=1, source_target_pairs={{0,8},{8,0},{16,24},{24,16},{32,40},{40,32},{48,56},{56,48},{64,72... | collective-permute-start | bytes 3145736 | tf_op jit(solution)/shard_map/ppermute | solution.py:399
  82.0 16.0 %collective-permute-start.20 = (bf16[8,2,64,512]{3,2,1,0:T(8,128)(2,1)}, bf16[8,2,64,512]{3,2,1,0:T(8,128)(2,1)}, u32[]{:S(2)}, u32[]{:S(2)}) collective-permute-start(bf16[8,2,64,512]{3,2,1,0:T(8,128)(2,1)} %get-tuple-element.86), channel_id=1, source_target_pairs={{0,8},{8,0},{16,24},{24,16},{32,40},{40,32},{48,56},{56,48},{64,72... | collective-permute-start | bytes 3145736 | tf_op jit(solution)/shard_map/ppermute | solution.py:399
  89.0 39.2 %all-to-all-start.2 = ((bf16[4,2,512,256]{3,2,1,0:T(8,128)(2,1)}), bf16[4,2,512,256]{3,2,1,0:T(8,128)(2,1)S(1)}, u32[]{:S(2)}, u32[]{:S(2)}) async-start(bf16[4,2,512,256]{3,2,1,0:T(8,128)(2,1)} %bitcast.14), calls=%async_computation.2 | async-start | bytes 4194304 | tf_op jit(solution)/shard_map/all_to_all | solution.py:585
  99.5 17.7 %collective-permute-start.21 = (bf16[8,64,512]{2,1,0:T(8,128)(2,1)S(1)}, bf16[8,64,512]{2,1,0:T(8,128)(2,1)S(1)}, u32[]{:S(2)}, u32[]{:S(2)}) collective-permute-start(bf16[8,64,512]{2,1,0:T(8,128)(2,1)S(1)} %get-tuple-element.88), channel_id=1, source_target_pairs={{0,128},{8,136},{16,144},{24,152},{32,160},{40,168},{48,176},{56,1... | collective-permute-start | bytes 1572872 | tf_op jit(solution)/shard_map/ppermute | solution.py:399
  100.9 7.6 %collective-permute-start.14 = (bf16[4,64,512]{2,1,0:T(8,128)(2,1)S(1)}, bf16[4,64,512]{2,1,0:T(8,128)(2,1)S(1)}, u32[]{:S(2)}, u32[]{:S(2)}) collective-permute-start(bf16[4,64,512]{2,1,0:T(8,128)(2,1)S(1)} %get-tuple-element.77), channel_id=1, source_target_pairs={{0,16},{8,24},{16,0},{24,8},{32,48},{40,56},{48,32},{56,40},{64,80... | collective-permute-start | bytes 786440 | tf_op jit(solution)/shard_map/ppermute | solution.py:407
  102.8 8.4 %collective-permute-start.15 = (bf16[4,64,512]{2,1,0:T(8,128)(2,1)S(1)}, bf16[4,64,512]{2,1,0:T(8,128)(2,1)S(1)}, u32[]{:S(2)}, u32[]{:S(2)}) collective-permute-start(bf16[4,64,512]{2,1,0:T(8,128)(2,1)S(1)} %get-tuple-element.78), channel_id=1, source_target_pairs={{0,112},{8,120},{16,32},{24,40},{32,16},{40,24},{48,64},{56,72},{6... | collective-permute-start | bytes 786440 | tf_op jit(solution)/shard_map/ppermute | solution.py:407
  111.4 12.3 %collective-permute-start.16 = (bf16[2,64,512]{2,1,0:T(8,128)(2,1)S(1)}, bf16[2,64,512]{2,1,0:T(8,128)(2,1)S(1)}, u32[]{:S(2)}, u32[]{:S(2)}) collective-permute-start(bf16[2,64,512]{2,1,0:T(8,128)(2,1)S(1)} %get-tuple-element.80), channel_id=1, source_target_pairs={{0,32},{8,40},{16,48},{24,56},{32,64},{40,72},{48,80},{56,88},{64,... | collective-permute-start | bytes 393224 | tf_op jit(solution)/shard_map/ppermute | solution.py:407
  111.4 12.2 %collective-permute-start.17 = (bf16[2,64,512]{2,1,0:T(8,128)(2,1)S(1)}, bf16[2,64,512]{2,1,0:T(8,128)(2,1)S(1)}, u32[]{:S(2)}, u32[]{:S(2)}) collective-permute-start(bf16[2,64,512]{2,1,0:T(8,128)(2,1)S(1)} %get-tuple-element.81), channel_id=1, source_target_pairs={{0,64},{8,72},{16,80},{24,88},{32,96},{40,104},{48,112},{56,120},{... | collective-permute-start | bytes 393224 | tf_op jit(solution)/shard_map/ppermute | solution.py:407
  114.3 12.8 %collective-permute-start.18 = (bf16[2,64,512]{2,1,0:T(8,128)(2,1)S(1)}, bf16[2,64,512]{2,1,0:T(8,128)(2,1)S(1)}, u32[]{:S(2)}, u32[]{:S(2)}) collective-permute-start(bf16[2,64,512]{2,1,0:T(8,128)(2,1)S(1)} %get-tuple-element.82), channel_id=1, source_target_pairs={{0,96},{8,104},{16,112},{24,120},{32,0},{40,8},{48,16},{56,24},{64... | collective-permute-start | bytes 393224 | tf_op jit(solution)/shard_map/ppermute | solution.py:407
  117.3 14.0 %collective-permute-start.22 = (bf16[4,32,512]{2,1,0:T(8,128)(2,1)S(1)}, bf16[4,32,512]{2,1,0:T(8,128)(2,1)S(1)}, u32[]{:S(2)}, u32[]{:S(2)}) collective-permute-start(bf16[4,32,512]{2,1,0:T(8,128)(2,1)S(1)} %get-tuple-element.90), channel_id=1, source_target_pairs={{0,16},{8,24},{16,0},{24,8},{32,48},{40,56},{48,32},{56,40},{64,80... | collective-permute-start | bytes 393224 | tf_op jit(solution)/shard_map/ppermute | solution.py:407
  117.5 13.8 %collective-permute-start.23 = (bf16[4,32,512]{2,1,0:T(8,128)(2,1)S(1)}, bf16[4,32,512]{2,1,0:T(8,128)(2,1)S(1)}, u32[]{:S(2)}, u32[]{:S(2)}) collective-permute-start(bf16[4,32,512]{2,1,0:T(8,128)(2,1)S(1)} %get-tuple-element.91), channel_id=1, source_target_pairs={{0,112},{8,120},{16,32},{24,40},{32,16},{40,24},{48,64},{56,72},{6... | collective-permute-start | bytes 393224 | tf_op jit(solution)/shard_map/ppermute | solution.py:407
  127.2 10.8 %collective-permute-start.19 = (bf16[64,512]{1,0:T(8,128)(2,1)S(1)}, bf16[64,512]{1,0:T(8,128)(2,1)S(1)}, u32[]{:S(2)}, u32[]{:S(2)}) collective-permute-start(bf16[64,512]{1,0:T(8,128)(2,1)S(1)} %get-tuple-element.84), channel_id=1, source_target_pairs={{0,128},{8,136},{16,144},{24,152},{32,160},{40,168},{48,176},{56,1... | collective-permute-start | bytes 196616 | tf_op jit(solution)/shard_map/ppermute | solution.py:399
  128.4 15.6 %collective-permute-start.12 = (bf16[512,256]{1,0:T(8,128)(2,1)S(1)}, bf16[512,256]{1,0:T(8,128)(2,1)S(1)}, u32[]{:S(2)}, u32[]{:S(2)}) collective-permute-start(bf16[512,256]{1,0:T(8,128)(2,1)S(1)} %get-tuple-element.67), channel_id=1, source_target_pairs={{0,1},{1,0},{2,3},{3,2},{4,5},{5,4},{6,7},{7,6},{8,9},{9,8},{10,11... | collective-permute-start | bytes 786440 | tf_op jit(solution)/shard_map/ppermute | solution.py:414
  131.3 7.4 %collective-permute-start.24 = (bf16[64,512]{1,0:T(8,128)(2,1)S(1)}, bf16[64,512]{1,0:T(8,128)(2,1)S(1)}, u32[]{:S(2)}, u32[]{:S(2)}) collective-permute-start(bf16[64,512]{1,0:T(8,128)(2,1)S(1)} %get-tuple-element.93), channel_id=1, source_target_pairs={{0,32},{8,40},{16,48},{24,56},{32,64},{40,72},{48,80},{56,88},{64,... | collective-permute-start | bytes 196616 | tf_op jit(solution)/shard_map/ppermute | solution.py:407
  134.3 8.2 %collective-permute-start.25 = (bf16[64,512]{1,0:T(8,128)(2,1)S(1)}, bf16[64,512]{1,0:T(8,128)(2,1)S(1)}, u32[]{:S(2)}, u32[]{:S(2)}) collective-permute-start(bf16[64,512]{1,0:T(8,128)(2,1)S(1)} %get-tuple-element.94), channel_id=1, source_target_pairs={{0,64},{8,72},{16,80},{24,88},{32,96},{40,104},{48,112},{56,120},{... | collective-permute-start | bytes 196616 | tf_op jit(solution)/shard_map/ppermute | solution.py:407
  136.8 6.6 %collective-permute-start.26 = (bf16[64,512]{1,0:T(8,128)(2,1)S(1)}, bf16[64,512]{1,0:T(8,128)(2,1)S(1)}, u32[]{:S(2)}, u32[]{:S(2)}) collective-permute-start(bf16[64,512]{1,0:T(8,128)(2,1)S(1)} %get-tuple-element.95), channel_id=1, source_target_pairs={{0,96},{8,104},{16,112},{24,120},{32,0},{40,8},{48,16},{56,24},{64... | collective-permute-start | bytes 196616 | tf_op jit(solution)/shard_map/ppermute | solution.py:407
  (28 other events, 234.4 us)

commit v5 on v4

--- a/solution.py
+++ b/solution.py
@@ -321,7 +321,7 @@
         copy.wait()
 
 
-def half_sum_kernel(x_hi, shares, stay, away):
+def half_sum_kernel(x_hi, shares, _, stay, away):
     x = x_hi[0]
     stay[...] = add(shares[0, x], shares[1, x]) + add(shares[2, x], shares[3, x])
     away[...] = (
@@ -440,7 +440,7 @@
     parts = call(quarter_second_kernel, [shaped(64, 512)] * 4, line, stay, left, right, scalars=1)
     parts = [parts[0]] + [along_line(parts[k], lambda z, k=k: z + 2 * k) for k in (1, 2, 3)]
     (total,) = call(last_sum_kernel, [shaped(64, 512, dtype=F32)], *parts)
-    return total, first_parts
+    return total, first_parts, parts[0]
 
 
 def z_first(line, keep, recv):
@@ -583,19 +583,20 @@
     columns = [[2 * i + x for i in range(4)] for x in range(2)]
     partials = partials.reshape(4, 2, 2 * T, 256)
     shares = lax.all_to_all(partials, "head", 0, 0, axis_index_groups=columns)
+    parts = quarters(line, stay_in, left, right)
+    gradient_out, parts, after = x_first(line, x_lo, keep_out, partner(send_out, 1), parts)
+    gradient_in = z_next(x_lo, parts)
     stay, away = call(
         half_sum_kernel,
         [shaped(2 * T, 256, dtype=F32), shaped(2 * T, 256)],
         x_hi.reshape(1),
         shares,
+        after,
         scalars=1,
     )
     mixed, gradient_tokens = call(
         whole_sum_kernel, [shaped(T, 256)] * 2, stay, around(away, 0, 1)
     )
-    parts = quarters(line, stay_in, left, right)
-    gradient_out, parts = x_first(line, x_lo, keep_out, partner(send_out, 1), parts)
-    gradient_in = z_next(x_lo, parts)
     return mixed, gradient_tokens, gradient_in, gradient_out
 
 

time: 145 us -> 147 us (1.014); the launches traced: 145 us -> 144 us
  no operation moved by 1% of the time
where the time goes in v5:
time: 147 us; the launch traced here: 144 us
  starting transfers between devices  51.2 us (35%)
  waiting for transfers between devices  35.4 us (24%)
  Pallas kernels  30.6 us (21%)
  blocking collectives  15.8 us (11%)
  local copies, waits for them, and re-layouts  9.79 us (7%)
    pallas_call x20, Pallas kernels, call(): pl.pallas_call(kernel, out_shape=outs, in_specs=[pl.BlockSpec(memory_spac...  30.6 us
    ppermute x10, waiting for transfers between devices, along_line(): return lax.ppermute(block, 'seq', route)  19.4 us
    ppermute x10, starting transfers between devices, along_line(): return lax.ppermute(block, 'seq', route)  17.6 us
    all_to_all x1, blocking collectives, shards(): chip_carried = lax.all_to_all(carried, 'seq', 0, 0, axis_index_groups=chips)  15.8 us
    ppermute x10, starting transfers between devices, around(): return lax.ppermute(block, 'head', route)  14.8 us
    unnamed x47, local copies, waits for them, and re-layouts  9.67 us
    all_to_all x1, starting transfers between devices, shards(): lax.all_to_all(chip_states, 'seq', 0, 0, axis_index_groups=chips)  9.5 us
    ppermute x10, waiting for transfers between devices, around(): return lax.ppermute(block, 'head', route)  9.41 us
  transfers between devices with their start and end apart: 29, of which 16 were waited for; matrix products, arithmetic and copies ran while one was open for 1% of the time, Pallas kernels for 12%

profile of v5, /device:TPU:8, one launch (start us, length us, event | category | flops | bytes accessed | tf_op | source)
XLA Modules:
  0.0 144.5 jit_solution(9377627740934840651)
XLA Ops:
  2.5 3.1 %collective-permute-start = (bf16[512,256]{1,0:T(8,128)(2,1)S(1)}, bf16[512,256]{1,0:T(8,128)(2,1)S(1)}, u32[]{:S(2)}, u32[]{:S(2)}) collective-permute-start(bf16[512,256]{1,0:T(8,128)(2,1)S(1)} %shard_map.111.refs_0_), channel_id=1, source_target_pairs={{0,1},{1,0},{2,3},{3,2},{4,5},{5,4},{6,7},{7,6},{8,9},{9,8},{10,11... | collective-permute-start | bytes 786440 | tf_op jit(solution)/shard_map/ppermute | solution.py:414
  7.7 4.5 %collective-permute-done.refs_1_ = bf16[512,256]{1,0:T(8,128)(2,1)S(1)} collective-permute-done((bf16[512,256]{1,0:T(8,128)(2,1)S(1)}, bf16[512,256]{1,0:T(8,128)(2,1)S(1)}, u32[]{:S(2)}, u32[]{:S(2)}) %collective-permute-start) | collective-permute-done | bytes 262176 | tf_op jit(solution)/shard_map/ppermute | solution.py:414
  22.2 2.3 %collective-permute-done.7.refs_7_ = bf16[256,256]{1,0:T(8,128)(2,1)S(1)} collective-permute-done((bf16[256,256]{1,0:T(8,128)(2,1)S(1)}, bf16[256,256]{1,0:T(8,128)(2,1)S(1)}, u32[]{:S(2)}, u32[]{:S(2)}) %collective-permute-start.7) | collective-permute-done | bytes 131104 | tf_op jit(solution)/shard_map/ppermute | solution.py:414
  26.4 8.7 %shard_map.113 = (bf16[4,256,512]{2,1,0:T(8,128)(2,1)}, bf16[4,4,256,128]{3,2,1,0:T(8,128)(2,1)}, bf16[8,128,128]{2,1,0:T(8,128)(2,1)S(1)}, bf16[8,128,128]{2,1,0:T(8,128)(2,1)}) custom-call(s32[1]{0:T(128)} %bitcast.1.core, f32[4]{0:T(128)S(1)} %copy-done.22, s32[8]{0:T(128)S(1)} %stack.35.places, bf16[512,256]{1,0:T(8,128)(2,1)} %copy-done, ...), custom_call_target="tpu_custom_call" | custom-call | tf_op jit(solution)/shard_map/pallas_call | solution.py:40
  37.8 9.5 %all-to-all-start = ((bf16[16,80,128]{2,1,0:T(8,128)(2,1)}), bf16[16,80,128]{2,1,0:T(8,128)(2,1)S(1)}, u32[]{:S(2)}, u32[]{:S(2)}) async-start(bf16[16,80,128]{2,1,0:T(8,128)(2,1)} %shard_map.114), calls=%async_computation | async-start | bytes 655360 | tf_op jit(solution)/shard_map/all_to_all | solution.py:530
  53.1 3.8 %shard_map.116 = (bf16[2048,512]{1,0:T(8,128)(2,1)}, bf16[2048,512]{1,0:T(8,128)(2,1)}) custom-call(s32[8]{0:T(128)S(1)} %stack.35.places, bf16[512,256]{1,0:T(8,128)(2,1)S(1)} %copy-done.1, bf16[512,256]{1,0:T(8,128)(2,1)S(1)} %copy-done.13, bf16[512,256]{1,0:T(8,128)(2,1)S(1)} %copy-done.5, bf16[512,256]{1,0:T(8,128)(2,1)S(1)} %copy-done.9, ...), custom_call_target="tpu_custom_call" | custom-call | tf_op jit(solution)/shard_map/pallas_call | solution.py:40
  56.9 2.1 %all-to-all-done.states = bf16[16,80,128]{2,1,0:T(8,128)(2,1)S(1)} async-done(((bf16[16,80,128]{2,1,0:T(8,128)(2,1)}), bf16[16,80,128]{2,1,0:T(8,128)(2,1)S(1)}, u32[]{:S(2)}, u32[]{:S(2)}) %all-to-all-start) | async-done | bytes 327712 | tf_op jit(solution)/shard_map/all_to_all | solution.py:530
  59.3 15.8 %all_to_all.15.chip = bf16[16,64,128]{2,1,0:T(8,128)(2,1)S(1)} all-to-all(bf16[16,64,128]{2,1,0:T(8,128)(2,1)S(1)} %shard_map.115), channel_id=1, replica_groups={{0,16,32,48,64,80,96,112,128,144,160,176,192,208,224,240},{8,24,40,56,7..., dimensions={0} | all-to-all | bytes 524288 | tf_op jit(solution)/shard_map/all_to_all | solution.py:534
  77.3 2.2 %shard_map.119 = (bf16[8,2,64,512]{3,2,1,0:T(8,128)(2,1)S(1)}, bf16[8,2,64,512]{3,2,1,0:T(8,128)(2,1)}) custom-call(s32[1]{0:T(128)} %bitcast.1.core, bf16[1024,512]{1,0:T(8,128)(2,1)S(1)} %shard_map.118.results, bf16[2048,512]{1,0:T(8,128)(2,1)S(1)} %copy-done.3), custom_call_target="tpu_custom_call" | custom-call | tf_op jit(solution)/shard_map/pallas_call | solution.py:40
  79.7 2.3 %shard_map.121 = (bf16[8,2,64,512]{3,2,1,0:T(8,128)(2,1)S(1)}, bf16[8,2,64,512]{3,2,1,0:T(8,128)(2,1)}) custom-call(s32[1]{0:T(128)} %bitcast.1.core, bf16[1024,512]{1,0:T(8,128)(2,1)S(1)} %shard_map.118.results, bf16[2048,512]{1,0:T(8,128)(2,1)S(1)} %copy-done.2), custom_call_target="tpu_custom_call" | custom-call | tf_op jit(solution)/shard_map/pallas_call | solution.py:40
  82.4 6.6 %shard_map.120 = bf16[8,512,256]{2,1,0:T(8,128)(2,1)} custom-call(bf16[1024,512]{1,0:T(8,128)(2,1)S(1)} %shard_map.118.results, bf16[2048,512]{1,0:T(8,128)(2,1)} %w_in.1, bf16[2048,512]{1,0:T(8,128)(2,1)} %w_out.1), custom_call_target="tpu_custom_call" | custom-call | tf_op jit(solution)/shard_map/pallas_call | solution.py:40
  89.0 6.3 %all-to-all-start.2 = ((bf16[4,2,512,256]{3,2,1,0:T(8,128)(2,1)}), bf16[4,2,512,256]{3,2,1,0:T(8,128)(2,1)S(1)}, u32[]{:S(2)}, u32[]{:S(2)}) async-start(bf16[4,2,512,256]{3,2,1,0:T(8,128)(2,1)} %bitcast.14), calls=%async_computation.2 | async-start | bytes 4194304 | tf_op jit(solution)/shard_map/all_to_all | solution.py:585
  100.9 1.9 %collective-permute-start.18 = (bf16[4,64,512]{2,1,0:T(8,128)(2,1)S(1)}, bf16[4,64,512]{2,1,0:T(8,128)(2,1)S(1)}, u32[]{:S(2)}, u32[]{:S(2)}) collective-permute-start(bf16[4,64,512]{2,1,0:T(8,128)(2,1)S(1)} %get-tuple-element.85), channel_id=1, source_target_pairs={{0,16},{8,24},{16,0},{24,8},{32,48},{40,56},{48,32},{56,40},{64,80... | collective-permute-start | bytes 786440 | tf_op jit(solution)/shard_map/ppermute | solution.py:407
  103.8 4.7 %collective-permute-done.18.left = bf16[4,64,512]{2,1,0:T(8,128)(2,1)S(1)} collective-permute-done((bf16[4,64,512]{2,1,0:T(8,128)(2,1)S(1)}, bf16[4,64,512]{2,1,0:T(8,128)(2,1)S(1)}, u32[]{:S(2)}, u32[]{:S(2)}) %collective-permute-start.18) | collective-permute-done | bytes 262176 | tf_op jit(solution)/shard_map/ppermute | solution.py:407
  108.6 2.7 %collective-permute-done.19.right = bf16[4,64,512]{2,1,0:T(8,128)(2,1)S(1)} collective-permute-done((bf16[4,64,512]{2,1,0:T(8,128)(2,1)S(1)}, bf16[4,64,512]{2,1,0:T(8,128)(2,1)S(1)}, u32[]{:S(2)}, u32[]{:S(2)}) %collective-permute-start.19) | collective-permute-done | bytes 262176 | tf_op jit(solution)/shard_map/ppermute | solution.py:407
  111.4 2.9 %collective-permute-start.21 = (bf16[2,64,512]{2,1,0:T(8,128)(2,1)S(1)}, bf16[2,64,512]{2,1,0:T(8,128)(2,1)S(1)}, u32[]{:S(2)}, u32[]{:S(2)}) collective-permute-start(bf16[2,64,512]{2,1,0:T(8,128)(2,1)S(1)} %get-tuple-element.89), channel_id=1, source_target_pairs={{0,64},{8,72},{16,80},{24,88},{32,96},{40,104},{48,112},{56,120},{... | collective-permute-start | bytes 393224 | tf_op jit(solution)/shard_map/ppermute | solution.py:407
  114.3 2.8 %collective-permute-start.22 = (bf16[2,64,512]{2,1,0:T(8,128)(2,1)S(1)}, bf16[2,64,512]{2,1,0:T(8,128)(2,1)S(1)}, u32[]{:S(2)}, u32[]{:S(2)}) collective-permute-start(bf16[2,64,512]{2,1,0:T(8,128)(2,1)S(1)} %get-tuple-element.90), channel_id=1, source_target_pairs={{0,96},{8,104},{16,112},{24,120},{32,0},{40,8},{48,16},{56,24},{64... | collective-permute-start | bytes 393224 | tf_op jit(solution)/shard_map/ppermute | solution.py:407
  118.9 4.7 %collective-permute-done.20.b = bf16[2,64,512]{2,1,0:T(8,128)(2,1)S(1)} collective-permute-done((bf16[2,64,512]{2,1,0:T(8,128)(2,1)S(1)}, bf16[2,64,512]{2,1,0:T(8,128)(2,1)S(1)}, u32[]{:S(2)}, u32[]{:S(2)}) %collective-permute-start.20) | collective-permute-done | bytes 131104 | tf_op jit(solution)/shard_map/ppermute | solution.py:407
  123.7 3.5 %collective-permute-done.22.d = bf16[2,64,512]{2,1,0:T(8,128)(2,1)S(1)} collective-permute-done((bf16[2,64,512]{2,1,0:T(8,128)(2,1)S(1)}, bf16[2,64,512]{2,1,0:T(8,128)(2,1)S(1)}, u32[]{:S(2)}, u32[]{:S(2)}) %collective-permute-start.22) | collective-permute-done | bytes 131104 | tf_op jit(solution)/shard_map/ppermute | solution.py:407
  129.0 2.8 %collective-permute-start.17 = (bf16[512,256]{1,0:T(8,128)(2,1)S(1)}, bf16[512,256]{1,0:T(8,128)(2,1)S(1)}, u32[]{:S(2)}, u32[]{:S(2)}) collective-permute-start(bf16[512,256]{1,0:T(8,128)(2,1)S(1)} %get-tuple-element.81), channel_id=1, source_target_pairs={{0,1},{1,0},{2,3},{3,2},{4,5},{5,4},{6,7},{7,6},{8,9},{9,8},{10,11... | collective-permute-start | bytes 786440 | tf_op jit(solution)/shard_map/ppermute | solution.py:414
  131.9 2.4 %collective-permute-start.24 = (bf16[64,512]{1,0:T(8,128)(2,1)S(1)}, bf16[64,512]{1,0:T(8,128)(2,1)S(1)}, u32[]{:S(2)}, u32[]{:S(2)}) collective-permute-start(bf16[64,512]{1,0:T(8,128)(2,1)S(1)} %get-tuple-element.93), channel_id=1, source_target_pairs={{0,32},{8,40},{16,48},{24,56},{32,64},{40,72},{48,80},{56,88},{64,... | collective-permute-start | bytes 196616 | tf_op jit(solution)/shard_map/ppermute | solution.py:407
  134.3 2.5 %collective-permute-start.25 = (bf16[64,512]{1,0:T(8,128)(2,1)S(1)}, bf16[64,512]{1,0:T(8,128)(2,1)S(1)}, u32[]{:S(2)}, u32[]{:S(2)}) collective-permute-start(bf16[64,512]{1,0:T(8,128)(2,1)S(1)} %get-tuple-element.94), channel_id=1, source_target_pairs={{0,64},{8,72},{16,80},{24,88},{32,96},{40,104},{48,112},{56,120},{... | collective-permute-start | bytes 196616 | tf_op jit(solution)/shard_map/ppermute | solution.py:407
  136.7 2.3 %collective-permute-start.26 = (bf16[64,512]{1,0:T(8,128)(2,1)S(1)}, bf16[64,512]{1,0:T(8,128)(2,1)S(1)}, u32[]{:S(2)}, u32[]{:S(2)}) collective-permute-start(bf16[64,512]{1,0:T(8,128)(2,1)S(1)} %get-tuple-element.95), channel_id=1, source_target_pairs={{0,96},{8,104},{16,112},{24,120},{32,0},{40,8},{48,16},{56,24},{64... | collective-permute-start | bytes 196616 | tf_op jit(solution)/shard_map/ppermute | solution.py:407
  139.8 3.3 %collective-permute-done.25.c = bf16[64,512]{1,0:T(8,128)(2,1)S(1)} collective-permute-done((bf16[64,512]{1,0:T(8,128)(2,1)S(1)}, bf16[64,512]{1,0:T(8,128)(2,1)S(1)}, u32[]{:S(2)}, u32[]{:S(2)}) %collective-permute-start.25) | collective-permute-done | bytes 65568 | tf_op jit(solution)/shard_map/ppermute | solution.py:407
  (108 shorter events, 39.7 us)
Async XLA Ops:
  2.5 9.6 %collective-permute-start = (bf16[512,256]{1,0:T(8,128)(2,1)S(1)}, bf16[512,256]{1,0:T(8,128)(2,1)S(1)}, u32[]{:S(2)}, u32[]{:S(2)}) collective-permute-start(bf16[512,256]{1,0:T(8,128)(2,1)S(1)} %shard_map.111.refs_0_), channel_id=1, source_target_pairs={{0,1},{1,0},{2,3},{3,2},{4,5},{5,4},{6,7},{7,6},{8,9},{9,8},{10,11... | collective-permute-start | bytes 786440 | tf_op jit(solution)/shard_map/ppermute | solution.py:414
  5.6 10.8 %collective-permute-start.1 = (bf16[512,256]{1,0:T(8,128)(2,1)S(1)}, bf16[512,256]{1,0:T(8,128)(2,1)S(1)}, u32[]{:S(2)}, u32[]{:S(2)}) collective-permute-start(bf16[512,256]{1,0:T(8,128)(2,1)S(1)} %shard_map.111.refs_0_), channel_id=1, source_target_pairs={{0,2},{1,3},{2,4},{3,5},{4,6},{5,7},{6,0},{7,1},{8,10},{9,11},{10,... | collective-permute-start | bytes 786440 | tf_op jit(solution)/shard_map/ppermute | solution.py:414
  7.2 9.2 %collective-permute-start.2 = (bf16[512,256]{1,0:T(8,128)(2,1)S(1)}, bf16[512,256]{1,0:T(8,128)(2,1)S(1)}, u32[]{:S(2)}, u32[]{:S(2)}) collective-permute-start(bf16[512,256]{1,0:T(8,128)(2,1)S(1)} %shard_map.111.refs_0_), channel_id=1, source_target_pairs={{0,6},{1,7},{2,0},{3,1},{4,2},{5,3},{6,4},{7,5},{8,14},{9,15},{10,... | collective-permute-start | bytes 786440 | tf_op jit(solution)/shard_map/ppermute | solution.py:414
  12.2 7.2 %collective-permute-start.4 = (bf16[512,256]{1,0:T(8,128)(2,1)S(1)}, bf16[512,256]{1,0:T(8,128)(2,1)S(1)}, u32[]{:S(2)}, u32[]{:S(2)}) collective-permute-start(bf16[512,256]{1,0:T(8,128)(2,1)S(1)} %collective-permute-done.refs_1_), channel_id=1, source_target_pairs={{0,2},{1,3},{2,4},{3,5},{4,6},{5,7},{6,0},{7,1},{8,10},{9,11},{10,... | collective-permute-start | bytes 786440 | tf_op jit(solution)/shard_map/ppermute | solution.py:414
  13.8 7.3 %collective-permute-start.5 = (bf16[512,256]{1,0:T(8,128)(2,1)S(1)}, bf16[512,256]{1,0:T(8,128)(2,1)S(1)}, u32[]{:S(2)}, u32[]{:S(2)}) collective-permute-start(bf16[512,256]{1,0:T(8,128)(2,1)S(1)} %collective-permute-done.refs_1_), channel_id=1, source_target_pairs={{0,6},{1,7},{2,0},{3,1},{4,2},{5,3},{6,4},{7,5},{8,14},{9,15},{10,... | collective-permute-start | bytes 786440 | tf_op jit(solution)/shard_map/ppermute | solution.py:414
  16.5 5.7 %collective-permute-start.6 = (bf16[256,256]{1,0:T(8,128)(2,1)S(1)}, bf16[256,256]{1,0:T(8,128)(2,1)S(1)}, u32[]{:S(2)}, u32[]{:S(2)}) collective-permute-start(bf16[256,256]{1,0:T(8,128)(2,1)S(1)} %slice.12), channel_id=1, source_target_pairs={{0,2},{1,3},{2,4},{3,5},{4,6},{5,7},{6,0},{7,1},{8,10},{9,11},{10,... | collective-permute-start | bytes 393224 | tf_op jit(solution)/shard_map/ppermute | solution.py:414
  18.1 6.4 %collective-permute-start.7 = (bf16[256,256]{1,0:T(8,128)(2,1)S(1)}, bf16[256,256]{1,0:T(8,128)(2,1)S(1)}, u32[]{:S(2)}, u32[]{:S(2)}) collective-permute-start(bf16[256,256]{1,0:T(8,128)(2,1)S(1)} %slice.13), channel_id=1, source_target_pairs={{0,6},{1,7},{2,0},{3,1},{4,2},{5,3},{6,4},{7,5},{8,14},{9,15},{10,... | collective-permute-start | bytes 393224 | tf_op jit(solution)/shard_map/ppermute | solution.py:414
  37.8 21.2 %all-to-all-start = ((bf16[16,80,128]{2,1,0:T(8,128)(2,1)}), bf16[16,80,128]{2,1,0:T(8,128)(2,1)S(1)}, u32[]{:S(2)}, u32[]{:S(2)}) async-start(bf16[16,80,128]{2,1,0:T(8,128)(2,1)} %shard_map.114), calls=%async_computation | async-start | bytes 655360 | tf_op jit(solution)/shard_map/all_to_all | solution.py:530
  79.6 15.7 %collective-permute-start.12 = (bf16[8,2,64,512]{3,2,1,0:T(8,128)(2,1)}, bf16[8,2,64,512]{3,2,1,0:T(8,128)(2,1)}, u32[]{:S(2)}, u32[]{:S(2)}) collective-permute-start(bf16[8,2,64,512]{3,2,1,0:T(8,128)(2,1)} %get-tuple-element.69), channel_id=1, source_target_pairs={{0,8},{8,0},{16,24},{24,16},{32,40},{40,32},{48,56},{56,48},{64,72... | collective-permute-start | bytes 3145736 | tf_op jit(solution)/shard_map/ppermute | solution.py:399
  82.0 16.0 %collective-permute-start.13 = (bf16[8,2,64,512]{3,2,1,0:T(8,128)(2,1)}, bf16[8,2,64,512]{3,2,1,0:T(8,128)(2,1)}, u32[]{:S(2)}, u32[]{:S(2)}) collective-permute-start(bf16[8,2,64,512]{3,2,1,0:T(8,128)(2,1)} %get-tuple-element.73), channel_id=1, source_target_pairs={{0,8},{8,0},{16,24},{24,16},{32,40},{40,32},{48,56},{56,48},{64,72... | collective-permute-start | bytes 3145736 | tf_op jit(solution)/shard_map/ppermute | solution.py:399
  89.0 39.8 %all-to-all-start.2 = ((bf16[4,2,512,256]{3,2,1,0:T(8,128)(2,1)}), bf16[4,2,512,256]{3,2,1,0:T(8,128)(2,1)S(1)}, u32[]{:S(2)}, u32[]{:S(2)}) async-start(bf16[4,2,512,256]{3,2,1,0:T(8,128)(2,1)} %bitcast.14), calls=%async_computation.2 | async-start | bytes 4194304 | tf_op jit(solution)/shard_map/all_to_all | solution.py:585
  99.5 17.7 %collective-permute-start.14 = (bf16[8,64,512]{2,1,0:T(8,128)(2,1)S(1)}, bf16[8,64,512]{2,1,0:T(8,128)(2,1)S(1)}, u32[]{:S(2)}, u32[]{:S(2)}) collective-permute-start(bf16[8,64,512]{2,1,0:T(8,128)(2,1)S(1)} %get-tuple-element.75), channel_id=1, source_target_pairs={{0,128},{8,136},{16,144},{24,152},{32,160},{40,168},{48,176},{56,1... | collective-permute-start | bytes 1572872 | tf_op jit(solution)/shard_map/ppermute | solution.py:399
  100.9 7.6 %collective-permute-start.18 = (bf16[4,64,512]{2,1,0:T(8,128)(2,1)S(1)}, bf16[4,64,512]{2,1,0:T(8,128)(2,1)S(1)}, u32[]{:S(2)}, u32[]{:S(2)}) collective-permute-start(bf16[4,64,512]{2,1,0:T(8,128)(2,1)S(1)} %get-tuple-element.85), channel_id=1, source_target_pairs={{0,16},{8,24},{16,0},{24,8},{32,48},{40,56},{48,32},{56,40},{64,80... | collective-permute-start | bytes 786440 | tf_op jit(solution)/shard_map/ppermute | solution.py:407
  102.8 8.4 %collective-permute-start.19 = (bf16[4,64,512]{2,1,0:T(8,128)(2,1)S(1)}, bf16[4,64,512]{2,1,0:T(8,128)(2,1)S(1)}, u32[]{:S(2)}, u32[]{:S(2)}) collective-permute-start(bf16[4,64,512]{2,1,0:T(8,128)(2,1)S(1)} %get-tuple-element.86), channel_id=1, source_target_pairs={{0,112},{8,120},{16,32},{24,40},{32,16},{40,24},{48,64},{56,72},{6... | collective-permute-start | bytes 786440 | tf_op jit(solution)/shard_map/ppermute | solution.py:407
  111.4 12.3 %collective-permute-start.20 = (bf16[2,64,512]{2,1,0:T(8,128)(2,1)S(1)}, bf16[2,64,512]{2,1,0:T(8,128)(2,1)S(1)}, u32[]{:S(2)}, u32[]{:S(2)}) collective-permute-start(bf16[2,64,512]{2,1,0:T(8,128)(2,1)S(1)} %get-tuple-element.88), channel_id=1, source_target_pairs={{0,32},{8,40},{16,48},{24,56},{32,64},{40,72},{48,80},{56,88},{64,... | collective-permute-start | bytes 393224 | tf_op jit(solution)/shard_map/ppermute | solution.py:407
  111.4 12.2 %collective-permute-start.21 = (bf16[2,64,512]{2,1,0:T(8,128)(2,1)S(1)}, bf16[2,64,512]{2,1,0:T(8,128)(2,1)S(1)}, u32[]{:S(2)}, u32[]{:S(2)}) collective-permute-start(bf16[2,64,512]{2,1,0:T(8,128)(2,1)S(1)} %get-tuple-element.89), channel_id=1, source_target_pairs={{0,64},{8,72},{16,80},{24,88},{32,96},{40,104},{48,112},{56,120},{... | collective-permute-start | bytes 393224 | tf_op jit(solution)/shard_map/ppermute | solution.py:407
  114.3 12.8 %collective-permute-start.22 = (bf16[2,64,512]{2,1,0:T(8,128)(2,1)S(1)}, bf16[2,64,512]{2,1,0:T(8,128)(2,1)S(1)}, u32[]{:S(2)}, u32[]{:S(2)}) collective-permute-start(bf16[2,64,512]{2,1,0:T(8,128)(2,1)S(1)} %get-tuple-element.90), channel_id=1, source_target_pairs={{0,96},{8,104},{16,112},{24,120},{32,0},{40,8},{48,16},{56,24},{64... | collective-permute-start | bytes 393224 | tf_op jit(solution)/shard_map/ppermute | solution.py:407
  117.3 11.4 %collective-permute-start.15 = (bf16[4,32,512]{2,1,0:T(8,128)(2,1)S(1)}, bf16[4,32,512]{2,1,0:T(8,128)(2,1)S(1)}, u32[]{:S(2)}, u32[]{:S(2)}) collective-permute-start(bf16[4,32,512]{2,1,0:T(8,128)(2,1)S(1)} %get-tuple-element.77), channel_id=1, source_target_pairs={{0,16},{8,24},{16,0},{24,8},{32,48},{40,56},{48,32},{56,40},{64,80... | collective-permute-start | bytes 393224 | tf_op jit(solution)/shard_map/ppermute | solution.py:407
  117.5 11.2 %collective-permute-start.16 = (bf16[4,32,512]{2,1,0:T(8,128)(2,1)S(1)}, bf16[4,32,512]{2,1,0:T(8,128)(2,1)S(1)}, u32[]{:S(2)}, u32[]{:S(2)}) collective-permute-start(bf16[4,32,512]{2,1,0:T(8,128)(2,1)S(1)} %get-tuple-element.78), channel_id=1, source_target_pairs={{0,112},{8,120},{16,32},{24,40},{32,16},{40,24},{48,64},{56,72},{6... | collective-permute-start | bytes 393224 | tf_op jit(solution)/shard_map/ppermute | solution.py:407
  127.2 11.9 %collective-permute-start.23 = (bf16[64,512]{1,0:T(8,128)(2,1)S(1)}, bf16[64,512]{1,0:T(8,128)(2,1)S(1)}, u32[]{:S(2)}, u32[]{:S(2)}) collective-permute-start(bf16[64,512]{1,0:T(8,128)(2,1)S(1)} %get-tuple-element.92), channel_id=1, source_target_pairs={{0,128},{8,136},{16,144},{24,152},{32,160},{40,168},{48,176},{56,1... | collective-permute-start | bytes 196616 | tf_op jit(solution)/shard_map/ppermute | solution.py:399
  129.0 14.7 %collective-permute-start.17 = (bf16[512,256]{1,0:T(8,128)(2,1)S(1)}, bf16[512,256]{1,0:T(8,128)(2,1)S(1)}, u32[]{:S(2)}, u32[]{:S(2)}) collective-permute-start(bf16[512,256]{1,0:T(8,128)(2,1)S(1)} %get-tuple-element.81), channel_id=1, source_target_pairs={{0,1},{1,0},{2,3},{3,2},{4,5},{5,4},{6,7},{7,6},{8,9},{9,8},{10,11... | collective-permute-start | bytes 786440 | tf_op jit(solution)/shard_map/ppermute | solution.py:414
  131.9 7.9 %collective-permute-start.24 = (bf16[64,512]{1,0:T(8,128)(2,1)S(1)}, bf16[64,512]{1,0:T(8,128)(2,1)S(1)}, u32[]{:S(2)}, u32[]{:S(2)}) collective-permute-start(bf16[64,512]{1,0:T(8,128)(2,1)S(1)} %get-tuple-element.93), channel_id=1, source_target_pairs={{0,32},{8,40},{16,48},{24,56},{32,64},{40,72},{48,80},{56,88},{64,... | collective-permute-start | bytes 196616 | tf_op jit(solution)/shard_map/ppermute | solution.py:407
  134.3 8.8 %collective-permute-start.25 = (bf16[64,512]{1,0:T(8,128)(2,1)S(1)}, bf16[64,512]{1,0:T(8,128)(2,1)S(1)}, u32[]{:S(2)}, u32[]{:S(2)}) collective-permute-start(bf16[64,512]{1,0:T(8,128)(2,1)S(1)} %get-tuple-element.94), channel_id=1, source_target_pairs={{0,64},{8,72},{16,80},{24,88},{32,96},{40,104},{48,112},{56,120},{... | collective-permute-start | bytes 196616 | tf_op jit(solution)/shard_map/ppermute | solution.py:407
  136.7 6.3 %collective-permute-start.26 = (bf16[64,512]{1,0:T(8,128)(2,1)S(1)}, bf16[64,512]{1,0:T(8,128)(2,1)S(1)}, u32[]{:S(2)}, u32[]{:S(2)}) collective-permute-start(bf16[64,512]{1,0:T(8,128)(2,1)S(1)} %get-tuple-element.95), channel_id=1, source_target_pairs={{0,96},{8,104},{16,112},{24,120},{32,0},{40,8},{48,16},{56,24},{64... | collective-permute-start | bytes 196616 | tf_op jit(solution)/shard_map/ppermute | solution.py:407
  (28 other events, 234.4 us)
